TPU v7x, 128 devices: a whole 4x4x4 slice. The times are simulated.
128 devices in a mesh: pipe: 16 (over z_hi, x, core), fsdp: 8 (over y, z_lo).
Axes of the slice: x: 4, y: 4, z: 4 (z_hi: 2, z_lo: 2; z = z_hi * 2 + z_lo), core: 2. Of those that a mesh axis runs over, the one named last changes fastest.
Arguments:
- hidden: bfloat16 [16384, 6144], P(('pipe', 'fsdp')), may hold values from -24 to 24
- gain: float32 [16, 6144], P('pipe'), may hold values from 0.5 to 1.5
- head: bfloat16 [16, 4096, 6144], P('pipe', 'fsdp'), may hold values from -0.50618622 to 0.50618622
- teacher_index: int32 [16384, 64], P('pipe'), may hold values from 0 to 4095, all different within a row
- teacher_logits: float32 [16384, 64], P('pipe'), may hold values from -12 to 410
- cotangent: float32 [16384], P('pipe'), may hold values from 64 to 512
Outputs:
- loss: float32 [16384], P(('pipe', 'fsdp'))
- grad_hidden: bfloat16 [16384, 6144], P(('pipe', 'fsdp'))
- grad_head: bfloat16 [16, 4096, 6144], P('pipe', 'fsdp')
- grad_gain: bfloat16 [16, 6144], P('pipe')
Inputs may be any that keep to these rules, and one draw needn't show every extreme that they name: `teacher_index`: each row names 64 different entries.
All inputs are finite; a program needn't handle non-finite values.
Results may differ from a plain program's by a relative error of at most 0.019.
Values may be sent and summed in bfloat16 or wider, within the bound.
No kernel may reach another device: no remote copies, remote signals or barrier semaphores. Data moves between devices by JAX's collectives and lax.ppermute only.
A program may use at most 128 MiB of HBM per device.

v0:
```python
import math

import jax
import jax.numpy as jnp
from jax import lax
from jax.sharding import PartitionSpec as P

smoothing = 0.1
epsilon = 1e-05


def pick_entries(local_index, logits, block_rows):
    rows, width = logits.shape
    num_top = local_index.shape[1]
    blocks = rows // block_rows

    def pick_one_block(pair):
        index_block, logit_block = pair
        column = lax.broadcasted_iota(jnp.int32, (1, 1, width), 2)
        hits = index_block[:, :, None] == column
        return jnp.sum(jnp.where(hits, logit_block[:, None, :], 0.0), axis=2)

    found = lax.map(
        pick_one_block,
        (
            local_index.reshape(blocks, block_rows, num_top),
            logits.reshape(blocks, block_rows, width),
        ),
    )
    return found.reshape(rows, num_top)


def spread_entries(local_index, values, width, block_rows):
    rows, num_top = local_index.shape
    blocks = rows // block_rows

    def spread_one_block(pair):
        index_block, value_block = pair
        column = lax.broadcasted_iota(jnp.int32, (1, 1, width), 2)
        hits = index_block[:, :, None] == column
        return jnp.sum(jnp.where(hits, value_block[:, :, None], 0.0), axis=1)

    dense = lax.map(
        spread_one_block,
        (
            local_index.reshape(blocks, block_rows, num_top),
            values.reshape(blocks, block_rows, num_top),
        ),
    )
    return dense.reshape(rows, width)


def body(hidden, gain, head, teacher_index, teacher_logits, cotangent):
    floats = hidden.astype(jnp.float32)
    scale = lax.rsqrt(jnp.mean(floats * floats, axis=1) + epsilon)
    unit = floats * scale[:, None]
    gain_row = gain[0]
    normed = (unit * gain_row[None, :]).astype(jnp.bfloat16)
    gathered = lax.all_gather(normed, "fsdp", axis=0, tiled=True)
    table = head[0]
    width = table.shape[0]
    num_top = teacher_index.shape[1]
    vocab_all = width * lax.axis_size("fsdp")
    rest = math.log(smoothing / (vocab_all - num_top))
    logits = lax.dot_general(
        gathered, table, (((1,), (1,)), ((), ())), preferred_element_type=jnp.float32
    )
    section_rows = logits.shape[0]
    block_rows = math.gcd(section_rows, 256)
    local_index = teacher_index - lax.axis_index("fsdp") * width
    own_picks = pick_entries(local_index, logits, block_rows)
    local_top = jnp.max(logits, axis=1)
    top = lax.pmax(local_top, "fsdp")
    shifted = logits - top[:, None]
    expo = jnp.exp(shifted)
    total, moment, picks = lax.psum(
        (jnp.sum(expo, axis=1), jnp.sum(expo * shifted, axis=1), own_picks), "fsdp"
    )
    logz = top + jnp.log(total)
    entropy = moment / total - jnp.log(total)
    chosen = jnp.exp(picks - logz[:, None])
    teacher_log = math.log(1.0 - smoothing) + jax.nn.log_softmax(teacher_logits, axis=1)
    loss = entropy - jnp.sum(chosen * teacher_log, axis=1) - (1.0 - jnp.sum(chosen, axis=1)) * rest
    probs = jnp.exp(logits - logz[:, None])
    extra = cotangent[:, None] * chosen * (rest - teacher_log)
    dlogits = cotangent[:, None] * probs * (
        logits - logz[:, None] - rest - loss[:, None]
    ) + spread_entries(local_index, extra, width, block_rows)
    dlow = dlogits.astype(jnp.bfloat16)
    grad_table = lax.dot_general(
        dlow, gathered, (((0,), (0,)), ((), ())), preferred_element_type=jnp.float32
    ).astype(jnp.bfloat16)
    own_rows = floats.shape[0]
    dnormed = lax.psum_scatter(
        jnp.dot(dlow, table, preferred_element_type=jnp.float32).astype(jnp.bfloat16),
        "fsdp",
        scatter_dimension=0,
        tiled=True,
    ).astype(jnp.float32)
    grad_gain = lax.psum(jnp.sum(unit * dnormed, axis=0), "fsdp").astype(jnp.bfloat16)
    scaled = gain_row[None, :] * dnormed
    grad_states = scale[:, None] * scaled - scale[:, None] * unit * jnp.mean(
        unit * scaled, axis=1, keepdims=True
    )
    own_loss = lax.dynamic_slice_in_dim(loss, lax.axis_index("fsdp") * own_rows, own_rows, 0)
    section_grad = grad_table[None]
    section_gain = grad_gain[None]
    block_table, block_gain = (
        lax.all_to_all(section_grad, "pipe", split_axis=1, concat_axis=0, tiled=True),
        lax.all_to_all(section_gain, "pipe", split_axis=1, concat_axis=0, tiled=True),
    )
    summed_table = (
        block_table.astype(jnp.float32) + jnp.flip(block_table, 0).astype(jnp.float32)
    ).astype(jnp.bfloat16)
    summed_gain = (
        block_gain.astype(jnp.float32) + jnp.flip(block_gain, 0).astype(jnp.float32)
    ).astype(jnp.bfloat16)
    merged_table, merged_gain = (
        lax.all_to_all(summed_table, "pipe", split_axis=0, concat_axis=1, tiled=True),
        lax.all_to_all(summed_gain, "pipe", split_axis=0, concat_axis=1, tiled=True),
    )
    return (own_loss, grad_states.astype(jnp.bfloat16), merged_table, merged_gain)


def solution(mesh):
    in_specs = (
        P(("pipe", "fsdp"), None),
        P("pipe", None),
        P("pipe", "fsdp", None),
        P("pipe", None),
        P("pipe", None),
        P("pipe"),
    )
    out_specs = (
        P(("pipe", "fsdp")),
        P(("pipe", "fsdp"), None),
        P("pipe", "fsdp", None),
        P("pipe", None),
    )
    return jax.shard_map(body, mesh=mesh, in_specs=in_specs, out_specs=out_specs, check_vma=False)
```

profile of v0, /device:TPU:1, one launch (start us, length us, event | category | flops | bytes accessed | tf_op | source)
XLA Modules:
  0.0 903.1 jit_solution(8677912274870854864)
XLA Ops:
  12.6 250.0 %all-gather.2.cloned.1.call-done = bf16[1024,6144]{1,0:T(8,128)(2,1)} async-done(((bf16[128,6144]{1,0:T(8,128)(2,1)}), bf16[1024,6144]{1,0:T(8,128)(2,1)}) %all-gather.2.cloned.1.call-update) | async-done | bytes 12582928 | tf_op jit(solution)/shard_map/all_gather | solution.py:59
  262.6 11.7 %fusion.19 = (f32[1024]{0:T(1024)S(1)}, f32[1024,512]{1,0:T(8,128)S(1)}) fusion(bf16[1024,6144]{1,0:T(8,128)(2,1)} %all-gather.2.cloned.1.call-done, bf16[1,512,6144]{2,1,0:T(8,128)(2,1)} %param.12), kind=kOutput, calls=%fused_computation.51 | convolution fusion | flops 6442974208 | bytes 20975616 | tf_op jit(solution)/shard_map/dot_general | solution.py:65
  274.2 14.8 %pmax.7 = f32[1024]{0:T(1024)S(1)} all-reduce(f32[1024]{0:T(1024)S(1)} %get-tuple-element.75), channel_id=1, replica_groups=mesh['pipe'=16,'fsdp'=8] {'fsdp'}, use_global_device_ids=true, to_apply=%region_2.3 | all-reduce | flops 1024 | bytes 8192 | tf_op jit(solution)/shard_map/pmax | solution.py:73
  289.1 26.4 %while.20 = (s32[]{:T(128)}, f32[4,256,64]{2,1,0:T(8,128)S(1)}, s32[4,256,64]{2,1,0:T(8,128)S(1)}, f32[4,256,512]{2,1,0:T(8,128)S(1)}, s32[]{:T(128)}) while((s32[]{:T(128)}, f32[4,256,64]{2,1,0:T(8,128)S(1)}, s32[4,256,64]{2,1,0:T(8,128)S(1)}, f32[4,256,512]{2,1,0:T(8,128)S(1)}, s32[]{:T(128)}) %tuple.55), condition=%wide.region_9.10_spmd, body=%wide.region_7.9_spmd.sunk | while | flops 25149440 | bytes 2097225 | solution.py:23
  317.3 12.9 %all-reduce = (f32[1024]{0:T(1024)S(1)}, f32[1024]{0:T(1024)S(1)}) all-reduce(f32[1024]{0:T(1024)S(1)} %get-tuple-element.53, f32[1024]{0:T(1024)S(1)} %get-tuple-element.52), channel_id=1, replica_groups=mesh['pipe'=16,'fsdp'=8] {'fsdp'}, use_global_device_ids=true, to_apply=%region_6.7 | all-reduce | flops 2048 | bytes 16384 | tf_op jit(solution)/shard_map/psum | solution.py:76
  330.3 57.5 %all-reduce.3.cloned.1.call-done = f32[1024,64]{0,1:T(8,128)} async-done(((f32[1024,64]{0,1:T(8,128)}), f32[1024,64]{0,1:T(8,128)}) %all-reduce.3.cloned.1.call-update) | async-done | bytes 262160 | tf_op jit(solution)/shard_map/psum | solution.py:76
  389.0 33.6 %while.21 = (s32[]{:T(128)}, f32[4,256,512]{2,1,0:T(8,128)}, s32[4,256,64]{2,1,0:T(8,128)S(1)}, f32[4,256,64]{2,1,0:T(8,128)S(1)}, s32[]{:T(128)}) while((s32[]{:T(128)}, f32[4,256,512]{2,1,0:T(8,128)}, s32[4,256,64]{2,1,0:T(8,128)S(1)}, f32[4,256,64]{2,1,0:T(8,128)S(1)}, s32[]{:T(128)}) %tuple.57), condition=%wide.region_17.18_spmd, body=%wide.region_15.17_spmd.sunk | while | flops 25034752 | bytes 1966661 | solution.py:43
  389.1 7.5 select_reduce_fusion.5
  397.5 7.5 select_reduce_fusion.5
  405.9 7.5 select_reduce_fusion.5
  414.3 7.5 select_reduce_fusion.5
  424.8 12.4 %convolution_convert_fusion = bf16[1024,6144]{1,0:T(8,128)(2,1)} fusion(bf16[1024,512]{1,0:T(8,128)(2,1)S(1)} %fusion.16, bf16[1,512,6144]{2,1,0:T(8,128)(2,1)} %param.12), kind=kOutput, calls=%fused_computation.11 | convolution fusion | flops 6448742400 | bytes 19922944 | tf_op jit(solution)/shard_map/dot_general | solution.py:95
  437.1 11.6 %fusion = bf16[1,512,6144]{2,1,0:T(8,128)(2,1)S(1)} fusion(bf16[1024,512]{1,0:T(8,128)(2,1)S(1)} %fusion.16, bf16[1024,6144]{1,0:T(8,128)(2,1)} %all-gather.2.cloned.1.call-done), kind=kOutput, calls=%fused_computation.13 | convolution fusion | flops 6445596672 | bytes 19922944 | tf_op jit(solution)/shard_map/dot_general | solution.py:90
  448.7 51.8 %copy.37 = bf16[1,512,6144]{2,0,1:T(2,128)(2,1)} copy(bf16[1,512,6144]{2,1,0:T(8,128)(2,1)S(1)} %fusion) | data formatting | bytes 12582912 | tf_op jit(solution)/shard_map/broadcast_in_dim | solution.py:106
  501.1 39.3 %reduce = bf16[512,6144]{1,0:T(8,128)(2,1)} reduce(bf16[512,1,6144]{2,1,0:T(2,128)(2,1)} %bitcast.63, bf16[]{:T(256)} %broadcast.26), dimensions={1}, to_apply=%bitcast.49.reduce_sub_computation | reduce | bytes 12582914
  540.3 13.0 %reshape.74 = bf16[16,2,98304]{2,1,0:T(2,128)(2,1)} reshape(bf16[512,6144]{1,0:T(8,128)(2,1)} %reduce) | data formatting | bytes 12582912
  553.3 118.5 %all_to_all.57 = bf16[16,2,98304]{2,1,0:T(2,128)(2,1)} all-to-all(bf16[16,2,98304]{2,1,0:T(2,128)(2,1)} %reshape.74), channel_id=1, replica_groups=mesh['pipe'=16,'fsdp'=8] {'pipe'}, dimensions={0} | all-to-all | bytes 12582912 | tf_op jit(solution)/shard_map/all_to_all | solution.py:109
  671.8 14.4 %reshape.75 = bf16[512,1,6144]{2,1,0:T(2,128)(2,1)} reshape(bf16[16,2,98304]{2,1,0:T(2,128)(2,1)} %all_to_all.57) | data formatting | bytes 12582912
  686.2 8.5 copy.30
  703.9 109.3 %all-to-all-done.1 = bf16[16,32,6144]{2,1,0:T(8,128)(2,1)} async-done(((bf16[16,32,6144]{2,1,0:T(8,128)(2,1)}), bf16[16,32,6144]{2,1,0:T(8,128)(2,1)}, u32[]{:S(2)}, u32[]{:S(2)}) %all-to-all-start.1) | async-done | bytes 6291488 | tf_op jit(solution)/shard_map/all_to_all | solution.py:119
  813.2 11.7 %reduce-scatter.2.cloned.1.call-done = bf16[128,6144]{1,0:T(8,128)(2,1)} async-done(((bf16[1024,6144]{1,0:T(8,128)(2,1)}), bf16[128,6144]{1,0:T(8,128)(2,1)}) %reduce-scatter.2.cloned.1.call-update) | async-done | bytes 1572880 | tf_op jit(solution)/shard_map/reduce_scatter | solution.py:94
  827.7 25.8 %psum.31 = bf16[6144]{0:T(1024)(128)(2,1)S(1)} all-reduce(f32[6144]{0:T(1024)S(1)} %get-tuple-element.50), channel_id=1, replica_groups=mesh['pipe'=16,'fsdp'=8] {'fsdp'}, use_global_device_ids=true, to_apply=%region_21.22 | all-reduce | flops 6144 | bytes 36864 | tf_op jit(solution)/shard_map/psum | solution.py:100
  854.9 14.7 %all-to-all-start.2 = ((bf16[16,2,192]{2,1,0:T(2,128)(2,1)}), bf16[16,2,192]{2,1,0:T(2,128)(2,1)S(1)}, u32[]{:S(2)}, u32[]{:S(2)}) async-start(bf16[16,2,192]{2,1,0:T(2,128)(2,1)} %reshape.76), calls=%async_computation.3 | async-start | bytes 32768 | tf_op jit(solution)/shard_map/all_to_all | solution.py:110
  869.7 7.3 all-to-all-done.2
  (83 shorter events, 73.7 us)
Async XLA Ops:
  7.2 5.1 copy-start.3
  7.2 255.4 %all-gather.2.cloned.1.call-start = ((), (), s32[]{:S(2)}) async-start(), calls=%async_computation.5 | async-start | bytes 14155776 | tf_op jit(solution)/shard_map/all_gather | solution.py:59
  9.0 3.4 copy-start.2
  12.1 375.6 %all-reduce.3.cloned.1.call-start = ((), (), s32[]{:S(2)}) async-start(), calls=%async_computation.6 | async-start | bytes 524288 | tf_op jit(solution)/shard_map/psum | solution.py:76
  315.5 72.3 %copy-start.5 = (f32[1024]{0:T(1024)S(1)}, f32[1024]{0:T(1024)}, u32[]{:S(2)}) copy-start(f32[1024]{0:T(1024)} %param.15) | copy-start | bytes 12292
  316.4 508.4 %reduce-scatter.2.cloned.1.call-start = ((), (), s32[]{:S(2)}) async-start(), calls=%async_computation.7 | async-start | bytes 14155776 | tf_op jit(solution)/shard_map/reduce_scatter | solution.py:94
  698.6 126.3 %copy-start = (bf16[128,6144]{1,0:T(8,128)(2,1)S(1)}, bf16[128,6144]{1,0:T(8,128)(2,1)}, u32[]{:S(2)}) copy-start(bf16[128,6144]{1,0:T(8,128)(2,1)} %param.10) | copy-start | bytes 4718596
  698.6 126.3 %copy-start.4 = (f32[1,6144]{1,0:T(1,128)S(1)}, f32[1,6144]{1,0:T(1,128)}, u32[]{:S(2)}) copy-start(f32[1,6144]{1,0:T(1,128)} %param.11) | copy-start | bytes 73732
  698.6 114.6 %all-to-all-start.1 = ((bf16[16,32,6144]{2,1,0:T(8,128)(2,1)}), bf16[16,32,6144]{2,1,0:T(8,128)(2,1)}, u32[]{:S(2)}, u32[]{:S(2)}) async-start(bf16[16,32,6144]{2,1,0:T(8,128)(2,1)} %add_convert_fusion), calls=%async_computation.2 | async-start | bytes 12582912 | tf_op jit(solution)/shard_map/all_to_all | solution.py:119
  824.9 57.4 %copy-start.1 = (bf16[128,6144]{1,0:T(8,128)(2,1)S(1)}, bf16[128,6144]{1,0:T(8,128)(2,1)}, u32[]{:S(2)}) copy-start(bf16[128,6144]{1,0:T(8,128)(2,1)} %reduce-scatter.2.cloned.1.call-done) | copy-start | bytes 4718596
  854.9 22.0 %all-to-all-start.2 = ((bf16[16,2,192]{2,1,0:T(2,128)(2,1)}), bf16[16,2,192]{2,1,0:T(2,128)(2,1)S(1)}, u32[]{:S(2)}, u32[]{:S(2)}) async-start(bf16[16,2,192]{2,1,0:T(2,128)(2,1)} %reshape.76), calls=%async_computation.3 | async-start | bytes 32768 | tf_op jit(solution)/shard_map/all_to_all | solution.py:110
  878.5 11.0 %all-to-all-start.3 = ((bf16[16,2,192]{2,1,0:T(2,128)(2,1)}), bf16[16,2,192]{2,1,0:T(2,128)(2,1)S(1)}, u32[]{:S(2)}, u32[]{:S(2)}) async-start(bf16[16,2,192]{2,1,0:T(2,128)(2,1)} %reshape.78), calls=%async_computation.4 | async-start | bytes 32768 | tf_op jit(solution)/shard_map/all_to_all | solution.py:120
Sparse Core Ops, SparseCore 0:
  12.3 250.2 all-gather.1
  316.6 71.1 all-reduce.2
  437.3 387.5 reduce-scatter.1
where the time goes:
time: 904 us; the launch traced here: 903 us
  waiting for transfers between devices  441 us (49%)
  blocking collectives  172 us (19%)
  other arithmetic  114 us (13%)
  local copies, waits for them, and re-layouts  102 us (11%)
  matrix products  35.6 us (4%)
  starting transfers between devices  23.2 us (3%)
  between operations  14 us (2%)
    all_gather x1, waiting for transfers between devices, body(): gathered = lax.all_gather(normed, 'fsdp', axis=0, tiled=True)  250 us
    all_to_all x1, blocking collectives, body(): lax.all_to_all(section_grad, 'pipe', split_axis=1, concat_axis=0, tiled=T...  118 us
    all_to_all x1, waiting for transfers between devices, body(): lax.all_to_all(summed_table, 'pipe', split_axis=0, concat_axis=1, tiled=T...  109 us
    psum x1, waiting for transfers between devices, body(): lax.psum((jnp.sum(expo, axis=1), jnp.sum(expo * shifted, axis=1), own_pic...  57.5 us
    broadcast_in_dim x1, local copies, waits for them, and re-layouts, body(): section_grad = grad_table[None]  51.8 us
    unnamed x22, local copies, waits for them, and re-layouts  44.8 us
    unnamed x2, other arithmetic  40 us
    reduce_sum x4, other arithmetic, spread_one_block(): return jnp.sum(jnp.where(hits, value_block[:, :, None], 0.0), axis=1)  30.1 us
  transfers between devices with their start and end apart: 6, of which 6 were waited for; matrix products, arithmetic and copies ran while one was open for 16% of the time, Pallas kernels for 0%

commit v1 on v0

v1 whole, which is shorter than its diff:
```python
import functools
import math

import jax
import jax.numpy as jnp
from jax import lax
from jax.experimental import pallas as pl
from jax.experimental.pallas import tpu as pltpu
from jax.sharding import PartitionSpec as P

smoothing = 0.1
epsilon = 1e-05
F32 = jnp.float32
BF16 = jnp.bfloat16
BIG = 60 * 1024 * 1024

RING, SIDES = 4, 2
BLOCKS = RING * SIDES
ROWS, COLUMNS = 128, 768
PARTS = (
    (0, 1, 0, 4),
    (0, 1, 4, 4),
    (1, 3, 0, 2),
    (1, 3, 2, 2),
    (1, 3, 4, 2),
    (1, 3, 6, 2),
)


def params(**kw):
    return pltpu.CompilerParams(vmem_limit_bytes=BIG, **kw)


def cost(flops, nbytes):
    return pl.CostEstimate(flops=int(flops), bytes_accessed=int(nbytes), transcendentals=0)


def norm_kernel(hidden_ref, gain_ref, normed_ref, scale_ref):
    floats = hidden_ref[...].astype(F32)
    scale = lax.rsqrt(jnp.mean(floats * floats, axis=1, keepdims=True) + epsilon)
    normed_ref[...] = (floats * scale * gain_ref[...]).astype(BF16)
    scale_ref[...] = jnp.broadcast_to(scale, scale_ref.shape)


def norm_half(hidden, gain, half):
    rows, width = hidden.shape
    step = rows // 4
    return pl.pallas_call(
        norm_kernel,
        grid=(2,),
        in_specs=[
            pl.BlockSpec((step, width), lambda i: (i + 2 * half, 0)),
            pl.BlockSpec((1, width), lambda i: (0, 0)),
        ],
        out_specs=[
            pl.BlockSpec((step, width), lambda i: (i, 0)),
            pl.BlockSpec((step, 128), lambda i: (i, 0)),
        ],
        out_shape=[
            jax.ShapeDtypeStruct((rows // 2, width), BF16),
            jax.ShapeDtypeStruct((rows // 2, 128), F32),
        ],
        compiler_params=params(),
        cost_estimate=cost(rows * width * 2, rows * width * 2),
        name="norm_half",
    )(hidden, gain)


def teacher_kernel(rest, order_ref, base_ref, index_ref, logit_ref, out_ref):
    logits = jnp.transpose(logit_ref[...])
    top = jnp.max(logits, axis=0, keepdims=True)
    shifted = logits - top
    logsum = jnp.log(jnp.sum(jnp.exp(shifted), axis=0, keepdims=True))
    value = rest - (math.log(1.0 - smoothing) + (shifted - logsum))
    entry = jnp.transpose(index_ref[...]) - base_ref[0]
    num_top, tokens = value.shape
    part = 64
    for lower in range(0, out_ref.shape[1], part):
        row = lax.broadcasted_iota(jnp.int32, (part, tokens), 0) + lower
        dense = jnp.zeros((part, tokens), F32)
        for k in range(num_top):
            dense = jnp.where(row == entry[k : k + 1, :], value[k : k + 1, :], dense)
        out_ref[0, lower : lower + part, :] = dense


def teacher_weights(order, base, index, logits, width, rest):
    rows, num_top = index.shape
    tokens = rows // BLOCKS
    return pl.pallas_call(
        functools.partial(teacher_kernel, rest),
        grid_spec=pltpu.PrefetchScalarGridSpec(
            num_scalar_prefetch=2,
            grid=(BLOCKS,),
            in_specs=[
                pl.BlockSpec((tokens, num_top), lambda j, order, base: (order[j], 0)),
                pl.BlockSpec((tokens, num_top), lambda j, order, base: (order[j], 0)),
            ],
            out_specs=pl.BlockSpec((1, width, tokens), lambda j, order, base: (j, 0, 0)),
        ),
        out_shape=jax.ShapeDtypeStruct((BLOCKS, width, tokens), F32),
        compiler_params=params(),
        cost_estimate=cost(rows * width * num_top, rows * width * 4),
        name="teacher_weights",
    )(order, base, index, logits)


def logits_kernel(count, head_ref, *refs):
    pieces, weights = refs[: 2 * count], refs[2 * count : 3 * count]
    logits_ref, sums_ref = refs[3 * count :]
    step = pl.program_id(0)
    block = jnp.concatenate([p[...] for p in pieces], axis=0)
    part = lax.dot_general(
        head_ref[0], block, (((1,), (1,)), ((), ())), preferred_element_type=F32
    )
    tokens = logits_ref.shape[2]

    @pl.when(step == 0)
    def _():
        for n in range(count):
            logits_ref[n] = part[:, n * tokens : (n + 1) * tokens]

    @pl.when(step > 0)
    def _():
        for n in range(count):
            logits_ref[n] += part[:, n * tokens : (n + 1) * tokens]

    @pl.when(step == pl.num_programs(0) - 1)
    def _():
        for n in range(count):
            logits = logits_ref[n]
            top = jnp.max(logits, axis=0, keepdims=True)
            shifted = logits - top
            expo = jnp.exp(shifted)
            total = jnp.sum(expo, axis=0, keepdims=True)
            mixed = jnp.sum(expo * (shifted + weights[n][0]), axis=0, keepdims=True)
            sums_ref[n] = jnp.concatenate(
                [top, total, mixed, jnp.zeros((5, top.shape[1]), F32)], axis=0
            )


def block_logits(slots, a, b, head, weights):
    _, width, depth = head.shape
    half = a[slots[0]].shape[0]
    tokens = 2 * half
    count = len(slots)
    step = 3072
    return pl.pallas_call(
        functools.partial(logits_kernel, count),
        grid=(depth // step,),
        in_specs=[pl.BlockSpec((1, width, step), lambda i: (0, 0, i))]
        + [pl.BlockSpec((half, step), lambda i: (0, i))] * (2 * count)
        + [pl.BlockSpec((1, width, tokens), lambda i, s=s: (s, 0, 0)) for s in slots],
        out_specs=[
            pl.BlockSpec((count, width, tokens), lambda i: (0, 0, 0)),
            pl.BlockSpec((count, 8, tokens), lambda i: (0, 0, 0)),
        ],
        out_shape=[
            jax.ShapeDtypeStruct((count, width, tokens), F32),
            jax.ShapeDtypeStruct((count, 8, tokens), F32),
        ],
        compiler_params=params(),
        cost_estimate=cost(2 * count * tokens * width * depth, width * depth * 2),
        name="block_logits",
    )(head, *[x[s] for s in slots for x in (a, b)], *([weights] * count))


def merge_sums(parts):
    top = functools.reduce(jnp.maximum, [p[0] for p in parts])
    total, mixed = 0.0, 0.0
    for one_top, one_total, one_mixed in parts:
        down = jnp.exp(one_top - top)
        total = total + one_total * down
        mixed = mixed + down * (one_mixed + (one_top - top) * one_total)
    return top, total, mixed


def dlogits_kernel(rest, where, weight_ref, cot_ref, *refs):
    sums = refs[:RING]
    logits = refs[RING:-4]
    first_ref, other_ref, low_ref, loss_ref = refs[-4:]
    tokens = cot_ref.shape[1]
    for slot in range(BLOCKS):
        side, ahead = slot // RING, slot % RING
        parts = []
        for shift in range(RING):
            found = sums[shift][side * RING + (ahead + RING - shift) % RING]
            parts.append((found[0:1], found[1:2], found[2:3]))
        top, total, mixed = merge_sums(parts)
        logtotal = jnp.log(total)
        logz = top + logtotal
        loss = mixed / total - logtotal - rest
        group, at = where[slot]
        rel = logits[group][at] - logz
        grads = cot_ref[slot : slot + 1] * jnp.exp(rel) * (rel - (rest + loss) + weight_ref[slot])
        low = grads.astype(BF16)
        here = slice(slot * tokens, (slot + 1) * tokens)
        first_ref[:, here] = low[:ROWS]
        other_ref[:, here] = low[ROWS:]
        low_ref[here, :] = jnp.transpose(grads).astype(BF16)
        loss_ref[slot : slot + 1, :] = loss


def all_dlogits(groups, found, weights, cot, sums, rest):
    blocks, width, tokens = weights.shape
    where = {s: (g, n) for g, group in enumerate(groups) for n, s in enumerate(group)}
    return pl.pallas_call(
        functools.partial(dlogits_kernel, rest, where),
        out_shape=[
            jax.ShapeDtypeStruct((ROWS, blocks * tokens), BF16),
            jax.ShapeDtypeStruct((width - ROWS, blocks * tokens), BF16),
            jax.ShapeDtypeStruct((blocks * tokens, width), BF16),
            jax.ShapeDtypeStruct((blocks, tokens), F32),
        ],
        compiler_params=params(),
        cost_estimate=cost(blocks * width * tokens * 10, blocks * width * tokens * 12),
        name="all_dlogits",
    )(weights, cot, *sums, *found)


def part_kernel(low_ref, *refs):
    normed = jnp.concatenate([p[...] for p in refs[:-1]], axis=0)
    refs[-1][...] = jnp.dot(low_ref[...], normed, preferred_element_type=F32).astype(BF16)


def table_part(low_t, pieces, lower, size):
    rows, tokens = low_t.shape
    half = pieces[0].shape[0]
    step = COLUMNS
    start = lower // step
    return pl.pallas_call(
        part_kernel,
        grid=(size // step,),
        in_specs=[pl.BlockSpec((rows, tokens), lambda i: (0, 0))]
        + [pl.BlockSpec((half, step), lambda i: (0, i + start)) for _ in pieces],
        out_specs=pl.BlockSpec((rows, step), lambda i: (0, i)),
        out_shape=jax.ShapeDtypeStruct((rows, size), BF16),
        compiler_params=params(),
        cost_estimate=cost(2 * rows * tokens * size, (rows + tokens) * size * 2),
        name="table_part",
    )(low_t, *pieces)


def table_kernel(first_ref, other_ref, head_ref, gain_ref, *refs):
    pieces, (out_ref, gain_out_ref) = refs[:-2], refs[-2:]
    normed = jnp.concatenate([p[...] for p in pieces], axis=0)
    low = jnp.concatenate([first_ref[...], other_ref[...]], axis=0)
    grads = jnp.dot(low, normed, preferred_element_type=F32)
    out_ref[...] = grads.astype(BF16)
    along = jnp.sum(head_ref[0].astype(F32) * grads, axis=0, keepdims=True) / gain_ref[...]
    gain_out_ref[...] = jnp.broadcast_to(along, gain_out_ref.shape)


def own_table(first, other, head, gain, pieces):
    _, width, depth = head.shape
    tokens = first.shape[1]
    half = pieces[0].shape[0]
    step = COLUMNS
    return pl.pallas_call(
        table_kernel,
        grid=(depth // step,),
        in_specs=[
            pl.BlockSpec(first.shape, lambda i: (0, 0)),
            pl.BlockSpec(other.shape, lambda i: (0, 0)),
            pl.BlockSpec((1, width, step), lambda i: (0, 0, i)),
            pl.BlockSpec((1, step), lambda i: (0, i)),
        ]
        + [pl.BlockSpec((half, step), lambda i: (0, i)) for _ in pieces],
        out_specs=[
            pl.BlockSpec((width, step), lambda i: (0, i)),
            pl.BlockSpec((8, step), lambda i: (0, i)),
        ],
        out_shape=[
            jax.ShapeDtypeStruct((width, depth), BF16),
            jax.ShapeDtypeStruct((8, depth), F32),
        ],
        compiler_params=params(),
        cost_estimate=cost(2 * width * tokens * depth, (tokens + 2 * width) * depth * 2),
        name="own_table",
    )(first, other, head, gain, *pieces)


def add_kernel(own_ref, other_ref, *refs):
    refs[-1][0] = (own_ref[...].astype(F32) + other_ref[...].astype(F32)).astype(BF16)


def add_part(own, other, earlier, part):
    width, depth = own.shape
    row, num_rows, column, num_columns = part
    first = earlier is None
    return pl.pallas_call(
        add_kernel,
        grid=(num_rows, num_columns),
        in_specs=[
            pl.BlockSpec((ROWS, COLUMNS), lambda i, j: (i + row, j + column)),
            pl.BlockSpec((ROWS, COLUMNS), lambda i, j: (i, j)),
        ]
        + ([] if first else [pl.BlockSpec(memory_space=pl.ANY)]),
        out_specs=pl.BlockSpec((1, ROWS, COLUMNS), lambda i, j: (0, i + row, j + column)),
        out_shape=jax.ShapeDtypeStruct((1, width, depth), BF16),
        input_output_aliases={} if first else {2: 0},
        compiler_params=params(),
        cost_estimate=cost(other.size, other.size * 6),
        name="add_part",
    )(own, other, *(() if first else (earlier,)))


def partial_kernel(counts, head_ref, *refs):
    num = len(counts)
    lows, rest, outs = refs[:num], refs[num:-num], refs[-num:]
    low = jnp.concatenate([r[...] for r in lows], axis=0)
    sums = jnp.dot(low, head_ref[0], preferred_element_type=F32)
    half = lows[0].shape[0]
    at = 0
    for n, count in enumerate(counts):
        total = sums[n * half : (n + 1) * half].astype(BF16).astype(F32)
        for r in rest[at : at + count]:
            total = total + r[...].astype(F32)
        at += count
        outs[n][...] = total.astype(outs[n].dtype)


def partials(low, head, jobs, dtype=BF16):
    _, width, depth = head.shape
    half = low.shape[0] // (2 * BLOCKS)
    step = 2048
    counts = [len(add) for _, add in jobs]
    added = [x for _, add in jobs for x in add]
    piece = pl.BlockSpec((half, step), lambda i: (0, i))
    return pl.pallas_call(
        functools.partial(partial_kernel, counts),
        grid=(depth // step,),
        in_specs=[pl.BlockSpec((1, width, step), lambda i: (0, 0, i))]
        + [pl.BlockSpec((half, width), lambda i, at=at: (at, 0)) for at, _ in jobs]
        + [piece] * len(added),
        out_specs=[piece] * len(jobs),
        out_shape=[jax.ShapeDtypeStruct((half, depth), dtype) for _ in jobs],
        compiler_params=params(),
        cost_estimate=cost(
            2 * len(jobs) * half * width * depth,
            width * depth * 2 + (len(jobs) + len(added)) * half * depth * 2,
        ),
        name="partials",
    )(head, *([low] * len(jobs)), *added)


def ring_perm(step):
    return [
        (y * SIDES + s, ((y + step) % RING) * SIDES + s)
        for y in range(RING)
        for s in range(SIDES)
    ]


def gate(values, *needed):
    found = lax.optimization_barrier((tuple(values), tuple(needed)))[0]
    return found if len(found) > 1 else found[0]


def body(hidden, gain, head, teacher_index, teacher_logits, cotangent):
    up, down, across = ring_perm(1), ring_perm(-1), ring_perm(2)
    swap = [(f, f ^ 1) for f in range(BLOCKS)]
    num_pipe = lax.axis_size("pipe")
    mirror = [(p, num_pipe - 1 - p) for p in range(num_pipe)]
    facing = [
        (p * BLOCKS + f, (num_pipe - 1 - p) * BLOCKS + (f ^ 1))
        for p in range(num_pipe)
        for f in range(BLOCKS)
    ]

    def send(x, perm):
        return lax.ppermute(x, "fsdp", perm)

    def exchange(x):
        return lax.ppermute(x, ("pipe", "fsdp"), facing)

    _, width, depth = head.shape
    rows = teacher_index.shape[0]
    tokens = rows // BLOCKS
    num_top = teacher_index.shape[1]
    rest = math.log(smoothing / (width * BLOCKS - num_top))

    a, b = {}, {}
    a[0], scale_a = norm_half(hidden, gain, 0)
    b[0], scale_b = norm_half(hidden, gain, 1)
    a[3] = send(a[0], up)
    a[1] = send(a[0], down)
    a[4] = send(a[0], swap)
    b[3] = send(b[0], up)
    b[1] = send(b[0], down)

    me = lax.axis_index("fsdp")
    slots = jnp.arange(BLOCKS, dtype=jnp.int32)
    order = ((me // SIDES + slots % RING) % RING) * SIDES + (me % SIDES) ^ (slots // RING)
    order = order.astype(jnp.int32)
    base = (me * width).astype(jnp.int32).reshape(1)
    weights = teacher_weights(order, base, teacher_index, teacher_logits, width, rest)
    cot = jnp.take(cotangent.reshape(BLOCKS, tokens), order, axis=0)

    groups = ((0,), (3, 1, 4), (5,), (2, 7), (6,))
    found = [block_logits(groups[0], a, b, head, weights)]

    b0, a4 = gate((b[0], a[4]), a[3], a[1], found[0][1])
    b[4] = send(b0, swap)
    a[7] = send(a4, up)
    a[5] = send(a4, down)
    a3, b1, b[4] = gate((a[3], b[1], b[4]), b[3])
    a[2] = send(a3, up)
    b[2] = send(b1, down)
    b[5] = send(b1, swap)
    found.append(block_logits(groups[1], a, b, head, weights))
    b3, a7, b5 = gate((b[3], a[7], b[5]), a[5], found[1][1])
    b[7] = send(b3, swap)
    a[6] = send(a7, up)
    b[6] = send(b5, down)
    found.append(block_logits(groups[2], a, b, head, weights))
    a[2], b[2], b[7] = gate((a[2], b[2], b[7]), found[2][1])
    found.append(block_logits(groups[3], a, b, head, weights))
    a[6], b[6] = gate((a[6], b[6]), found[3][1])
    found.append(block_logits(groups[4], a, b, head, weights))

    at = [s for group in groups for s in group]
    sums = jnp.concatenate([f[1] for f in found], axis=0)
    sums = jnp.stack([sums[at.index(s)] for s in range(BLOCKS)])

    def rows_of(x):
        return x[:, 0:1], x[:, 1:2], x[:, 2:3]

    other = send(sums, swap)
    other = jnp.concatenate([other[RING:], other[:RING]], axis=0)
    pair = merge_sums([rows_of(sums), rows_of(other)])
    pair = jnp.concatenate(pair + (jnp.zeros((BLOCKS, 5, tokens), F32),), axis=1)
    ring_sums = [pair, send(pair, down), send(pair, across), send(pair, up)]
    first, second, low, loss = all_dlogits(
        groups, [f[0] for f in found], weights, cot, ring_sums, rest
    )

    pieces, facing_pieces = [], []
    for slot in range(BLOCKS):
        pieces += [a[slot], b[slot]]
        other_slot = (slot + RING) % BLOCKS
        facing_pieces += [a[other_slot], b[other_slot]]

    their_first, their_second = send(first, swap), send(second, swap)
    o2a, o2b = partials(low, head, [(12, []), (13, [])])
    r_o2a, r_o2b = send(o2a, down), send(o2b, up)

    def part_of(n):
        row, _, column, num_columns = PARTS[n]
        mine = their_first if row == 0 else their_second
        return table_part(mine, facing_pieces, column * COLUMNS, num_columns * COLUMNS)

    theirs = [None] * len(PARTS)
    their_first = gate((their_first,), o2a)
    part = part_of(0)
    theirs[0] = exchange(part)
    their_first = gate((their_first,), part)
    part = part_of(1)
    theirs[1] = exchange(part)

    low = gate((low,), part)
    s2a, s2b, o3b, o0b = partials(low, head, [(4, []), (5, []), (15, []), (9, [])])
    s2a, s2b, o3b, their_second = gate((s2a, s2b, o3b, their_second), r_o2a, r_o2b)
    r_s2a, r_s2b, r_o3b = send(s2a, down), send(s2b, up), send(o3b, swap)
    part = gate((part_of(2),), theirs[0])
    theirs[2] = exchange(part)
    low = gate((low,), part)
    o3a, o1a, s1a = partials(low, head, [(14, [r_o2a]), (10, []), (2, [])])
    part = part_of(3)
    o3a, o1a, o0b = gate((o3a, o1a, o0b), r_s2a, r_s2b, r_o3b, part)
    r_o3a, r_o1a, r_o0b = send(o3a, down), send(o1a, up), send(o0b, swap)
    part = gate((part,), theirs[1], o0b)
    theirs[3] = exchange(part)
    low = gate((low,), part)
    s3a, o1b = partials(low, head, [(6, [r_s2a]), (11, [r_o2b])])
    part = part_of(4)
    s3a, s1a, o1b = gate((s3a, s1a, o1b), r_o3a, r_o1a, r_o0b, part)
    r_s3a, r_s1a, r_o1b = send(s3a, down), send(s1a, up), send(o1b, swap)
    part = gate((part,), theirs[2], o1b)
    theirs[4] = exchange(part)
    low = gate((low,), part)
    s3b, o0a = partials(low, head, [(7, [r_o3b]), (8, [r_o3a, r_o1a])])
    part = part_of(5)
    s3b, o0a = gate((s3b, o0a), r_s3a, r_s1a, r_o1b, part)
    r_s3b, r_o0a = send(s3b, down), send(o0a, swap)
    (s1b,) = partials(low, head, [(3, [r_s2b, r_o1b])])
    r_s1b = send(s1b, up)
    part = gate((part,), theirs[3], s1b)
    theirs[5] = exchange(part)
    first, second = gate((first, second), part)
    own, along = own_table(first, second, head, gain, pieces)

    along = along[:1].reshape(8, depth // 8)
    along = along + send(along, swap)
    along = along + send(along, [(f, f ^ SIDES) for f in range(BLOCKS)])
    along = along + send(along, across)
    along = along.astype(BF16)
    merged_gain = (
        along.astype(F32) + lax.ppermute(along, "pipe", mirror).astype(F32)
    ).astype(BF16).reshape(1, depth)

    merged = None
    for n in range(4):
        merged = add_part(own, theirs[n], merged, PARTS[n])
    low = gate((low,), r_s3b, r_o0a, r_s1b, merged)
    sum_a, sum_b = partials(
        low, head, [(0, [r_s3a, r_s1a, r_o0a]), (1, [r_s3b, r_s1b, r_o0b])], F32
    )

    dnormed = jnp.concatenate([sum_a, sum_b], axis=0)
    scale = jnp.concatenate([scale_a, scale_b], axis=0)[:, :1]
    unit = hidden.astype(F32) * scale
    scaled = gain * dnormed
    grad_states = scale * scaled - scale * unit * jnp.mean(unit * scaled, axis=1, keepdims=True)
    grad_states = grad_states.astype(BF16)

    theirs[4], theirs[5] = gate((theirs[4], theirs[5]), grad_states)
    for n in range(4, len(PARTS)):
        merged = add_part(own, theirs[n], merged, PARTS[n])
    return (loss[0], grad_states, merged, merged_gain)


def solution(mesh):
    in_specs = (
        P(("pipe", "fsdp"), None),
        P("pipe", None),
        P("pipe", "fsdp", None),
        P("pipe", None),
        P("pipe", None),
        P("pipe"),
    )
    out_specs = (
        P(("pipe", "fsdp")),
        P(("pipe", "fsdp"), None),
        P("pipe", "fsdp", None),
        P("pipe", None),
    )
    return jax.shard_map(body, mesh=mesh, in_specs=in_specs, out_specs=out_specs, check_vma=False)
```

time: 904 us -> 341 us (0.38)
  waiting for transfers between devices: 441 us -> 94.2 us
  blocking collectives: 172 us -> 0 us
  Pallas kernels: 0 us -> 158 us
  other arithmetic: 114 us -> 11.3 us
  local copies, waits for them, and re-layouts: 102 us -> 9.95 us
  starting transfers between devices: 23.2 us -> 64.6 us
  matrix products: 35.6 us -> 0 us
  between operations: 14 us -> 1.08 us
    all_gather x1 -> x0, waiting for transfers between devices: 250 us -> none  [body(): gathered = lax.all_gather(normed, 'fsdp', axis=0, tiled=True)]
    pallas_call x0 -> x28, Pallas kernels: none -> 158 us  [the longest x7 42.5 us: partials(): pl.pallas_call(functools.partial(partial_kernel, counts), grid=(depth //...]
    all_to_all x3 -> x0, waiting for transfers between devices: 122 us -> none  [the longest x1 109 us: body(): lax.all_to_all(summed_table, 'pipe', split_axis=0, concat_axis=1, tiled=T...]
    all_to_all x1 -> x0, blocking collectives: 118 us -> none  [body(): lax.all_to_all(section_grad, 'pipe', split_axis=1, concat_axis=0, tiled=T...]
    ppermute x0 -> x44, waiting for transfers between devices: none -> 94.2 us  [the longest x37 60.2 us: send(): return lax.ppermute(x, 'fsdp', perm)]
    ppermute x0 -> x44, starting transfers between devices: none -> 64.6 us  [the longest x37 35 us: send(): return lax.ppermute(x, 'fsdp', perm)]
    reduce_sum x13 -> x1, other arithmetic: 62.7 us -> 2.78 us  [body(): jnp.mean(unit * scaled, axis=1, keepdims=True)]
    psum x1 -> x0, waiting for transfers between devices: 57.5 us -> none  [body(): lax.psum((jnp.sum(expo, axis=1), jnp.sum(expo * shifted, axis=1), own_pic...]
  transfers between devices with their start and end apart: 6 -> 44, of which waited for: 6 -> 24; matrix products, arithmetic and copies ran while one was open for 16% -> 4% of each run, Pallas kernels for 0% -> 42%
where the time goes in v1:
time: 341 us; the launch traced here: 339 us
  Pallas kernels  158 us (46%)
  waiting for transfers between devices  94.2 us (28%)
  starting transfers between devices  64.6 us (19%)
  other arithmetic  11.3 us (3%)
  local copies, waits for them, and re-layouts  9.95 us (3%)
    ppermute x37, waiting for transfers between devices, send(): return lax.ppermute(x, 'fsdp', perm)  60.2 us
    pallas_call x7, Pallas kernels, partials(): pl.pallas_call(functools.partial(partial_kernel, counts), grid=(depth //...  42.5 us
    ppermute x37, starting transfers between devices, send(): return lax.ppermute(x, 'fsdp', perm)  35 us
    ppermute x6, waiting for transfers between devices, exchange(): return lax.ppermute(x, ('pipe', 'fsdp'), facing)  34 us
    pallas_call x6, Pallas kernels, table_part(): pl.pallas_call(part_kernel, grid=(size // step,), in_specs=[pl.BlockSpec(...  27.4 us
    pallas_call x6, Pallas kernels, add_part(): pl.pallas_call(add_kernel, grid=(num_rows, num_columns), in_specs=[pl.Blo...  26.4 us
    pallas_call x4, Pallas kernels, block_logits(): pl.pallas_call(functools.partial(logits_kernel, count), grid=(depth // st...  24.4 us
    ppermute x6, starting transfers between devices, exchange(): return lax.ppermute(x, ('pipe', 'fsdp'), facing)  22.1 us
  transfers between devices with their start and end apart: 44, of which 24 were waited for; matrix products, arithmetic and copies ran while one was open for 4% of the time, Pallas kernels for 42%

profile of v1, /device:TPU:1, one launch (start us, length us, event | category | flops | bytes accessed | tf_op | source)
XLA Modules:
  0.0 339.3 jit_solution(9760087085429592053)
XLA Ops:
  15.7 13.6 %teacher_weights.1.refs_2_.refs_6_.refs_7_.refs_8_.refs_4_.refs_5_.weight_ref = f32[8,512,128]{2,1,0:T(8,128)} custom-call(s32[8]{0:T(128)} %get-tuple-element.161.order_ref, s32[1]{0:T(128)} %bitcast.base_ref, s32[1024,64]{1,0:T(8,128)} %copy.19.index_ref, f32[1024,64]{1,0:T(8,128)} %copy.20.logit_ref), custom_call_target="tpu_custom_call" | custom-call | flops 33554432 | bytes 2097152 | tf_op jit(solution)/shard_map/teacher_weights/pallas_call | solution.py:89
  29.3 5.2 %block_logits.5 = (f32[1,512,128]{2,1,0:T(8,128)}, f32[1,8,128]{2,1,0:T(8,128)}) custom-call(bf16[1,512,6144]{2,1,0:T(8,128)(2,1)} %head_ref.24, bf16[64,6144]{1,0:T(8,128)(2,1)} %get-tuple-element.79.refs_0_.refs_8_, bf16[64,6144]{1,0:T(8,128)(2,1)} %get-tuple-element.82.refs_1_.refs_9_, ...), custom_call_target="tpu_custom_call" | custom-call | flops 805306368 | bytes 6291456 | tf_op jit(solution)/shard_map/block_logits/pallas_call | solution.py:147
  44.4 7.6 %collective-permute-done.5.refs_5_.refs_1_.refs_9_ = bf16[64,6144]{1,0:T(8,128)(2,1)S(1)} collective-permute-done((bf16[64,6144]{1,0:T(8,128)(2,1)S(1)}, bf16[64,6144]{1,0:T(8,128)(2,1)S(1)}, u32[]{:S(2)}, u32[]{:S(2)}) %collective-permute-start.5) | collective-permute-done | bytes 786464 | tf_op jit(solution)/shard_map/ppermute | solution.py:371
  55.4 8.1 %block_logits.6 = (f32[3,512,128]{2,1,0:T(8,128)}, f32[3,8,128]{2,1,0:T(8,128)}) custom-call(bf16[1,512,6144]{2,1,0:T(8,128)(2,1)} %head_ref.24, bf16[64,6144]{1,0:T(8,128)(2,1)} %copy-done.5, bf16[64,6144]{1,0:T(8,128)(2,1)} %collective-permute-done.1.refs_1_.refs_15_.refs_7_, bf16[64,6144]{1,0:T(8,128)(2,1)} %copy-done.4, ...), custom_call_target="tpu_custom_call" | custom-call | flops 2415919104 | bytes 6291456 | tf_op jit(solution)/shard_map/block_logits/pallas_call | solution.py:147
  63.4 5.3 %collective-permute-done.9.refs_1_.refs_3_.refs_11_ = bf16[64,6144]{1,0:T(8,128)(2,1)S(1)} collective-permute-done((bf16[64,6144]{1,0:T(8,128)(2,1)}, bf16[64,6144]{1,0:T(8,128)(2,1)S(1)}, u32[]{:S(2)}, u32[]{:S(2)}) %collective-permute-start.9) | collective-permute-done | bytes 786464 | tf_op jit(solution)/shard_map/ppermute | solution.py:371
  72.5 5.1 %block_logits.7 = (f32[1,512,128]{2,1,0:T(8,128)}, f32[1,8,128]{2,1,0:T(8,128)}) custom-call(bf16[1,512,6144]{2,1,0:T(8,128)(2,1)} %head_ref.24, bf16[64,6144]{1,0:T(8,128)(2,1)} %collective-permute-done.10.refs_0_.refs_2_.refs_10_, bf16[64,6144]{1,0:T(8,128)(2,1)} %copy-done.8, ...), custom_call_target="tpu_custom_call" | custom-call | flops 805306368 | bytes 6291456 | tf_op jit(solution)/shard_map/block_logits/pallas_call | solution.py:147
  78.1 6.7 %collective-permute-done.11.refs_3_.refs_7_.refs_15_ = bf16[64,6144]{1,0:T(8,128)(2,1)} collective-permute-done((bf16[64,6144]{1,0:T(8,128)(2,1)}, bf16[64,6144]{1,0:T(8,128)(2,1)}, u32[]{:S(2)}, u32[]{:S(2)}) %collective-permute-start.11) | collective-permute-done | bytes 786464 | tf_op jit(solution)/shard_map/ppermute | solution.py:371
  84.8 6.0 %block_logits.8 = (f32[2,512,128]{2,1,0:T(8,128)}, f32[2,8,128]{2,1,0:T(8,128)}) custom-call(bf16[1,512,6144]{2,1,0:T(8,128)(2,1)} %head_ref.24, bf16[64,6144]{1,0:T(8,128)(2,1)} %collective-permute-done.6.refs_0_.refs_12_.refs_4_, bf16[64,6144]{1,0:T(8,128)(2,1)} %collective-permute-done.7.refs_1_.refs_13_.refs_5_, ...), custom_call_target="tpu_custom_call" | custom-call | flops 1610612736 | bytes 6291456 | tf_op jit(solution)/shard_map/block_logits/pallas_call | solution.py:147
  113.0 5.4 %partials.7 = (bf16[64,6144]{1,0:T(8,128)(2,1)}, bf16[64,6144]{1,0:T(8,128)(2,1)}) custom-call(bf16[1,512,6144]{2,1,0:T(8,128)(2,1)} %head_ref.24, bf16[1024,512]{1,0:T(8,128)(2,1)} %get-tuple-element.148.refs_0_.refs_1_.refs_2_.refs_3_, bf16[1024,512]{1,0:T(8,128)(2,1)} %get-tuple-element.148.refs_0_.refs_1_.refs_2_.refs_3_), custom_call_target="tpu_custom_call" | custom-call | flops 805306368 | bytes 7864320 | tf_op jit(solution)/shard_map/partials/pallas_call | solution.py:329
  122.4 10.0 %collective-permute-done.18.low_ref = bf16[128,1024]{1,0:T(8,128)(2,1)S(1)} collective-permute-done((bf16[128,1024]{1,0:T(8,128)(2,1)S(1)}, bf16[128,1024]{1,0:T(8,128)(2,1)S(1)}, u32[]{:S(2)}, u32[]{:S(2)}) %collective-permute-start.18) | collective-permute-done | bytes 262176 | tf_op jit(solution)/shard_map/ppermute | solution.py:371
  133.1 5.2 %table_part.6 = bf16[128,3072]{1,0:T(8,128)(2,1)} custom-call(bf16[128,1024]{1,0:T(8,128)(2,1)} %copy-done.19, bf16[64,6144]{1,0:T(8,128)(2,1)} %copy-done.3, bf16[64,6144]{1,0:T(8,128)(2,1)} %copy-done.6, bf16[64,6144]{1,0:T(8,128)(2,1)} %collective-permute-done.10.refs_0_.refs_2_.refs_10_, bf16[64,6144]{1,0:T(8,128)(2,1)} %copy-done.8, ...), custom_call_target="tpu_custom_call" | custom-call | flops 805306368 | bytes 7077888 | tf_op jit(solution)/shard_map/table_part/pallas_call | solution.py:230
  138.3 10.7 %collective-permute-start.22 = (bf16[128,3072]{1,0:T(8,128)(2,1)}, bf16[128,3072]{1,0:T(8,128)(2,1)S(1)}, u32[]{:S(2)}, u32[]{:S(2)}) collective-permute-start(bf16[128,3072]{1,0:T(8,128)(2,1)} %table_part.6), channel_id=1, source_target_pairs={{0,121},{1,120},{2,123},{3,122},{4,125},{5,124},{6,127},{7,126},{8... | collective-permute-start | bytes 2359304 | tf_op jit(solution)/shard_map/ppermute | solution.py:374
  149.0 5.3 %table_part.7 = bf16[128,3072]{1,0:T(8,128)(2,1)} custom-call(bf16[128,1024]{1,0:T(8,128)(2,1)} %copy-done.19, bf16[64,6144]{1,0:T(8,128)(2,1)} %copy-done.3, bf16[64,6144]{1,0:T(8,128)(2,1)} %copy-done.6, bf16[64,6144]{1,0:T(8,128)(2,1)} %collective-permute-done.10.refs_0_.refs_2_.refs_10_, bf16[64,6144]{1,0:T(8,128)(2,1)} %copy-done.8, ...), custom_call_target="tpu_custom_call" | custom-call | flops 805306368 | bytes 7077888 | tf_op jit(solution)/shard_map/table_part/pallas_call | solution.py:230
  154.3 6.3 %partials.8 = (bf16[64,6144]{1,0:T(8,128)(2,1)}, bf16[64,6144]{1,0:T(8,128)(2,1)}, bf16[64,6144]{1,0:T(8,128)(2,1)}, bf16[64,6144]{1,0:T(8,128)(2,1)}) custom-call(bf16[1,512,6144]{2,1,0:T(8,128)(2,1)} %head_ref.24, bf16[1024,512]{1,0:T(8,128)(2,1)} %get-tuple-element.148.refs_0_.refs_1_.refs_2_.refs_3_, ...), custom_call_target="tpu_custom_call" | custom-call | flops 1610612736 | bytes 9437184 | tf_op jit(solution)/shard_map/partials/pallas_call | solution.py:329
  174.1 6.2 %partials.9 = (bf16[64,6144]{1,0:T(8,128)(2,1)}, bf16[64,6144]{1,0:T(8,128)(2,1)}, bf16[64,6144]{1,0:T(8,128)(2,1)}) custom-call(bf16[1,512,6144]{2,1,0:T(8,128)(2,1)} %head_ref.24, bf16[1024,512]{1,0:T(8,128)(2,1)} %get-tuple-element.148.refs_0_.refs_1_.refs_2_.refs_3_, bf16[1024,512]{1,0:T(8,128)(2,1)} %get-tuple-element.148.refs_0_.refs_1_.refs_2_.refs_3_, ...), custom_call_target="tpu_custom_call" | custom-call | flops 1207959552 | bytes 9437184 | tf_op jit(solution)/shard_map/partials/pallas_call | solution.py:329
  192.8 5.6 %partials.10 = (bf16[64,6144]{1,0:T(8,128)(2,1)}, bf16[64,6144]{1,0:T(8,128)(2,1)}) custom-call(bf16[1,512,6144]{2,1,0:T(8,128)(2,1)} %head_ref.24, bf16[1024,512]{1,0:T(8,128)(2,1)} %get-tuple-element.148.refs_0_.refs_1_.refs_2_.refs_3_, bf16[1024,512]{1,0:T(8,128)(2,1)} %get-tuple-element.148.refs_0_.refs_1_.refs_2_.refs_3_, ...), custom_call_target="tpu_custom_call" | custom-call | flops 805306368 | bytes 9437184 | tf_op jit(solution)/shard_map/partials/pallas_call | solution.py:329
  209.8 5.7 %collective-permute-done.27.other_ref = bf16[384,1536]{1,0:T(8,128)(2,1)S(1)} collective-permute-done((bf16[384,1536]{1,0:T(8,128)(2,1)}, bf16[384,1536]{1,0:T(8,128)(2,1)S(1)}, u32[]{:S(2)}, u32[]{:S(2)}) %collective-permute-start.27) | collective-permute-done | bytes 1179680 | tf_op jit(solution)/shard_map/ppermute | solution.py:374
  215.5 6.3 %partials.11 = (bf16[64,6144]{1,0:T(8,128)(2,1)}, bf16[64,6144]{1,0:T(8,128)(2,1)}) custom-call(bf16[1,512,6144]{2,1,0:T(8,128)(2,1)} %head_ref.24, bf16[1024,512]{1,0:T(8,128)(2,1)} %get-tuple-element.148.refs_0_.refs_1_.refs_2_.refs_3_, bf16[1024,512]{1,0:T(8,128)(2,1)} %get-tuple-element.148.refs_0_.refs_1_.refs_2_.refs_3_, ...), custom_call_target="tpu_custom_call" | custom-call | flops 805306368 | bytes 10223616 | tf_op jit(solution)/shard_map/partials/pallas_call | solution.py:329
  226.7 5.4 %partials.12 = bf16[64,6144]{1,0:T(8,128)(2,1)} custom-call(bf16[1,512,6144]{2,1,0:T(8,128)(2,1)} %head_ref.24, bf16[1024,512]{1,0:T(8,128)(2,1)} %get-tuple-element.148.refs_0_.refs_1_.refs_2_.refs_3_, bf16[64,6144]{1,0:T(8,128)(2,1)} %copy-done.21, bf16[64,6144]{1,0:T(8,128)(2,1)} %collective-permute-done.33.refs_2_), custom_call_target="tpu_custom_call" | custom-call | flops 402653184 | bytes 8650752 | tf_op jit(solution)/shard_map/partials/pallas_call | solution.py:329
  232.5 7.3 %collective-permute-done.37.other_ref = bf16[384,1536]{1,0:T(8,128)(2,1)S(1)} collective-permute-done((bf16[384,1536]{1,0:T(8,128)(2,1)S(1)}, bf16[384,1536]{1,0:T(8,128)(2,1)S(1)}, u32[]{:S(2)}, u32[]{:S(2)}) %collective-permute-start.37) | collective-permute-done | bytes 1179680 | tf_op jit(solution)/shard_map/ppermute | solution.py:374
  239.7 14.8 %own_table.1 = (bf16[512,6144]{1,0:T(8,128)(2,1)}, f32[8,6144]{1,0:T(8,128)}) custom-call(bf16[128,1024]{1,0:T(8,128)(2,1)} %get-tuple-element.145.first_ref, bf16[384,1024]{1,0:T(8,128)(2,1)} %get-tuple-element.146.other_ref, bf16[1,512,6144]{2,1,0:T(8,128)(2,1)} %head_ref.24, f32[1,6144]{1,0:T(1,128)} %gain_ref.5, ...), custom_call_target="tpu_custom_call" | custom-call | flops 6442450944 | bytes 25165824 | tf_op jit(solution)/shard_map/own_table/pallas_call | solution.py:258
  265.2 7.5 %collective-permute-start.43 = (bf16[8,768]{1,0:T(8,128)(2,1)S(1)}, bf16[8,768]{1,0:T(8,128)(2,1)S(1)}, u32[]{:S(2)}, u32[]{:S(2)}) collective-permute-start(bf16[8,768]{1,0:T(8,128)(2,1)S(1)} %add_convert_fusion.1), channel_id=1, source_target_pairs={{0,120},{8,112},{16,104},{24,96},{32,88},{40,80},{48,72},{56,64},{... | collective-permute-start | bytes 36872 | tf_op jit(solution)/shard_map/ppermute | solution.py:498
  296.5 7.3 %partials.13 = (f32[64,6144]{1,0:T(8,128)}, f32[64,6144]{1,0:T(8,128)}) custom-call(bf16[1,512,6144]{2,1,0:T(8,128)(2,1)} %head_ref.24, bf16[1024,512]{1,0:T(8,128)(2,1)} %get-tuple-element.148.refs_0_.refs_1_.refs_2_.refs_3_, bf16[1024,512]{1,0:T(8,128)(2,1)} %get-tuple-element.148.refs_0_.refs_1_.refs_2_.refs_3_, ...), custom_call_target="tpu_custom_call" | custom-call | flops 805306368 | bytes 12582912 | tf_op jit(solution)/shard_map/partials/pallas_call | solution.py:329
  309.6 20.1 %collective-permute-done.39.other_ref = bf16[384,1536]{1,0:T(8,128)(2,1)} collective-permute-done((bf16[384,1536]{1,0:T(8,128)(2,1)S(1)}, bf16[384,1536]{1,0:T(8,128)(2,1)}, u32[]{:S(2)}, u32[]{:S(2)}) %collective-permute-start.39) | collective-permute-done | bytes 1179680 | tf_op jit(solution)/shard_map/ppermute | solution.py:374
  (201 shorter events, 151.5 us)
Async XLA Ops:
  3.0 31.5 %collective-permute-start.4 = (bf16[64,6144]{1,0:T(8,128)(2,1)}, bf16[64,6144]{1,0:T(8,128)(2,1)S(1)}, u32[]{:S(2)}, u32[]{:S(2)}) collective-permute-start(bf16[64,6144]{1,0:T(8,128)(2,1)} %get-tuple-element.79.refs_0_.refs_8_), channel_id=1, source_target_pairs={{0,1},{1,0},{2,3},{3,2},{4,5},{5,4},{6,7},{7,6},{8,9},{9,8},{10,11... | collective-permute-start | bytes 2359304 | tf_op jit(solution)/shard_map/ppermute | solution.py:371
  5.5 29.0 %collective-permute-start.2 = (bf16[64,6144]{1,0:T(8,128)(2,1)}, bf16[64,6144]{1,0:T(8,128)(2,1)S(1)}, u32[]{:S(2)}, u32[]{:S(2)}) collective-permute-start(bf16[64,6144]{1,0:T(8,128)(2,1)} %get-tuple-element.79.refs_0_.refs_8_), channel_id=1, source_target_pairs={{0,6},{1,7},{2,0},{3,1},{4,2},{5,3},{6,4},{7,5},{8,14},{9,15},{10,... | collective-permute-start | bytes 2359304 | tf_op jit(solution)/shard_map/ppermute | solution.py:371
  8.2 26.3 %collective-permute-start = (bf16[64,6144]{1,0:T(8,128)(2,1)}, bf16[64,6144]{1,0:T(8,128)(2,1)S(1)}, u32[]{:S(2)}, u32[]{:S(2)}) collective-permute-start(bf16[64,6144]{1,0:T(8,128)(2,1)} %get-tuple-element.79.refs_0_.refs_8_), channel_id=1, source_target_pairs={{0,2},{1,3},{2,4},{3,5},{4,6},{5,7},{6,0},{7,1},{8,10},{9,11},{10,... | collective-permute-start | bytes 2359304 | tf_op jit(solution)/shard_map/ppermute | solution.py:371
  10.5 30.8 %collective-permute-start.3 = (bf16[64,6144]{1,0:T(8,128)(2,1)}, bf16[64,6144]{1,0:T(8,128)(2,1)}, u32[]{:S(2)}, u32[]{:S(2)}) collective-permute-start(bf16[64,6144]{1,0:T(8,128)(2,1)} %get-tuple-element.82.refs_1_.refs_9_), channel_id=1, source_target_pairs={{0,6},{1,7},{2,0},{3,1},{4,2},{5,3},{6,4},{7,5},{8,14},{9,15},{10,... | collective-permute-start | bytes 2359304 | tf_op jit(solution)/shard_map/ppermute | solution.py:371
  13.2 31.2 %collective-permute-start.1 = (bf16[64,6144]{1,0:T(8,128)(2,1)}, bf16[64,6144]{1,0:T(8,128)(2,1)}, u32[]{:S(2)}, u32[]{:S(2)}) collective-permute-start(bf16[64,6144]{1,0:T(8,128)(2,1)} %get-tuple-element.82.refs_1_.refs_9_), channel_id=1, source_target_pairs={{0,2},{1,3},{2,4},{3,5},{4,6},{5,7},{6,0},{7,1},{8,10},{9,11},{10,... | collective-permute-start | bytes 2359304 | tf_op jit(solution)/shard_map/ppermute | solution.py:371
  34.7 28.8 %collective-permute-start.10 = (bf16[64,6144]{1,0:T(8,128)(2,1)S(1)}, bf16[64,6144]{1,0:T(8,128)(2,1)}, u32[]{:S(2)}, u32[]{:S(2)}) collective-permute-start(bf16[64,6144]{1,0:T(8,128)(2,1)S(1)} %collective-permute-done.4.refs_4_.refs_0_.refs_8_), channel_id=1, source_target_pairs={{0,6},{1,7},{2,0},{3,1},{4,2},{5,3},{6,4},{7,5},{8,14},{9,15},{10,... | collective-permute-start | bytes 2359304 | tf_op jit(solution)/shard_map/ppermute | solution.py:371
  37.4 26.0 %collective-permute-start.8 = (bf16[64,6144]{1,0:T(8,128)(2,1)S(1)}, bf16[64,6144]{1,0:T(8,128)(2,1)}, u32[]{:S(2)}, u32[]{:S(2)}) collective-permute-start(bf16[64,6144]{1,0:T(8,128)(2,1)S(1)} %collective-permute-done.4.refs_4_.refs_0_.refs_8_), channel_id=1, source_target_pairs={{0,2},{1,3},{2,4},{3,5},{4,6},{5,7},{6,0},{7,1},{8,10},{9,11},{10,... | collective-permute-start | bytes 2359304 | tf_op jit(solution)/shard_map/ppermute | solution.py:371
  52.9 25.2 %collective-permute-start.7 = (bf16[64,6144]{1,0:T(8,128)(2,1)}, bf16[64,6144]{1,0:T(8,128)(2,1)}, u32[]{:S(2)}, u32[]{:S(2)}) collective-permute-start(bf16[64,6144]{1,0:T(8,128)(2,1)} %collective-permute-done.3.refs_3_.refs_11_), channel_id=1, source_target_pairs={{0,6},{1,7},{2,0},{3,1},{4,2},{5,3},{6,4},{7,5},{8,14},{9,15},{10,... | collective-permute-start | bytes 2359304 | tf_op jit(solution)/shard_map/ppermute | solution.py:371
  55.3 22.8 %collective-permute-start.6 = (bf16[64,6144]{1,0:T(8,128)(2,1)S(1)}, bf16[64,6144]{1,0:T(8,128)(2,1)}, u32[]{:S(2)}, u32[]{:S(2)}) collective-permute-start(bf16[64,6144]{1,0:T(8,128)(2,1)S(1)} %collective-permute-done.refs_0_.refs_14_.refs_6_), channel_id=1, source_target_pairs={{0,2},{1,3},{2,4},{3,5},{4,6},{5,7},{6,0},{7,1},{8,10},{9,11},{10,... | collective-permute-start | bytes 2359304 | tf_op jit(solution)/shard_map/ppermute | solution.py:371
  69.8 25.0 %collective-permute-start.12 = (bf16[64,6144]{1,0:T(8,128)(2,1)}, bf16[64,6144]{1,0:T(8,128)(2,1)S(1)}, u32[]{:S(2)}, u32[]{:S(2)}) collective-permute-start(bf16[64,6144]{1,0:T(8,128)(2,1)} %collective-permute-done.8.refs_2_.refs_6_.refs_14_), channel_id=1, source_target_pairs={{0,2},{1,3},{2,4},{3,5},{4,6},{5,7},{6,0},{7,1},{8,10},{9,11},{10,... | collective-permute-start | bytes 2359304 | tf_op jit(solution)/shard_map/ppermute | solution.py:371
  69.8 25.0 %collective-permute-start.13 = (bf16[64,6144]{1,0:T(8,128)(2,1)S(1)}, bf16[64,6144]{1,0:T(8,128)(2,1)}, u32[]{:S(2)}, u32[]{:S(2)}) collective-permute-start(bf16[64,6144]{1,0:T(8,128)(2,1)S(1)} %collective-permute-done.9.refs_1_.refs_3_.refs_11_), channel_id=1, source_target_pairs={{0,6},{1,7},{2,0},{3,1},{4,2},{5,3},{6,4},{7,5},{8,14},{9,15},{10,... | collective-permute-start | bytes 2359304 | tf_op jit(solution)/shard_map/ppermute | solution.py:371
  112.9 47.7 %collective-permute-start.19 = (bf16[384,1024]{1,0:T(8,128)(2,1)}, bf16[384,1024]{1,0:T(8,128)(2,1)S(1)}, u32[]{:S(2)}, u32[]{:S(2)}) collective-permute-start(bf16[384,1024]{1,0:T(8,128)(2,1)} %get-tuple-element.146.other_ref), channel_id=1, source_target_pairs={{0,1},{1,0},{2,3},{3,2},{4,5},{5,4},{6,7},{7,6},{8,9},{9,8},{10,11... | collective-permute-start | bytes 2359304 | tf_op jit(solution)/shard_map/ppermute | solution.py:371
  118.4 42.2 %collective-permute-start.21 = (bf16[64,6144]{1,0:T(8,128)(2,1)}, bf16[64,6144]{1,0:T(8,128)(2,1)S(1)}, u32[]{:S(2)}, u32[]{:S(2)}) collective-permute-start(bf16[64,6144]{1,0:T(8,128)(2,1)} %get-tuple-element.117), channel_id=1, source_target_pairs={{0,2},{1,3},{2,4},{3,5},{4,6},{5,7},{6,0},{7,1},{8,10},{9,11},{10,... | collective-permute-start | bytes 2359304 | tf_op jit(solution)/shard_map/ppermute | solution.py:371
  119.8 40.8 %collective-permute-start.20 = (bf16[64,6144]{1,0:T(8,128)(2,1)}, bf16[64,6144]{1,0:T(8,128)(2,1)S(1)}, u32[]{:S(2)}, u32[]{:S(2)}) collective-permute-start(bf16[64,6144]{1,0:T(8,128)(2,1)} %get-tuple-element.109), channel_id=1, source_target_pairs={{0,6},{1,7},{2,0},{3,1},{4,2},{5,3},{6,4},{7,5},{8,14},{9,15},{10,... | collective-permute-start | bytes 2359304 | tf_op jit(solution)/shard_map/ppermute | solution.py:371
  138.3 35.7 %collective-permute-start.22 = (bf16[128,3072]{1,0:T(8,128)(2,1)}, bf16[128,3072]{1,0:T(8,128)(2,1)S(1)}, u32[]{:S(2)}, u32[]{:S(2)}) collective-permute-start(bf16[128,3072]{1,0:T(8,128)(2,1)} %table_part.6), channel_id=1, source_target_pairs={{0,121},{1,120},{2,123},{3,122},{4,125},{5,124},{6,127},{7,126},{8... | collective-permute-start | bytes 2359304 | tf_op jit(solution)/shard_map/ppermute | solution.py:374
  164.4 23.3 %collective-permute-start.23 = (bf16[128,3072]{1,0:T(8,128)(2,1)}, bf16[128,3072]{1,0:T(8,128)(2,1)}, u32[]{:S(2)}, u32[]{:S(2)}) collective-permute-start(bf16[128,3072]{1,0:T(8,128)(2,1)} %table_part.7), channel_id=1, source_target_pairs={{0,121},{1,120},{2,123},{3,122},{4,125},{5,124},{6,127},{7,126},{8... | collective-permute-start | bytes 2359304 | tf_op jit(solution)/shard_map/ppermute | solution.py:374
  183.4 32.1 %collective-permute-start.27 = (bf16[384,1536]{1,0:T(8,128)(2,1)}, bf16[384,1536]{1,0:T(8,128)(2,1)S(1)}, u32[]{:S(2)}, u32[]{:S(2)}) collective-permute-start(bf16[384,1536]{1,0:T(8,128)(2,1)} %table_part.8), channel_id=1, source_target_pairs={{0,121},{1,120},{2,123},{3,122},{4,125},{5,124},{6,127},{7,126},{8... | collective-permute-start | bytes 3538952 | tf_op jit(solution)/shard_map/ppermute | solution.py:374
  187.7 52.1 %collective-permute-start.37 = (bf16[384,1536]{1,0:T(8,128)(2,1)S(1)}, bf16[384,1536]{1,0:T(8,128)(2,1)S(1)}, u32[]{:S(2)}, u32[]{:S(2)}) collective-permute-start(bf16[384,1536]{1,0:T(8,128)(2,1)S(1)} %copy-done.18), channel_id=1, source_target_pairs={{0,121},{1,120},{2,123},{3,122},{4,125},{5,124},{6,127},{7,126},{8... | collective-permute-start | bytes 3538952 | tf_op jit(solution)/shard_map/ppermute | solution.py:374
  225.6 70.9 %collective-permute-start.34 = (bf16[64,6144]{1,0:T(8,128)(2,1)}, bf16[64,6144]{1,0:T(8,128)(2,1)}, u32[]{:S(2)}, u32[]{:S(2)}) collective-permute-start(bf16[64,6144]{1,0:T(8,128)(2,1)} %get-tuple-element.142), channel_id=1, source_target_pairs={{0,6},{1,7},{2,0},{3,1},{4,2},{5,3},{6,4},{7,5},{8,14},{9,15},{10,... | collective-permute-start | bytes 2359304 | tf_op jit(solution)/shard_map/ppermute | solution.py:371
  226.7 69.8 %collective-permute-start.35 = (bf16[64,6144]{1,0:T(8,128)(2,1)}, bf16[64,6144]{1,0:T(8,128)(2,1)}, u32[]{:S(2)}, u32[]{:S(2)}) collective-permute-start(bf16[64,6144]{1,0:T(8,128)(2,1)} %get-tuple-element.143), channel_id=1, source_target_pairs={{0,1},{1,0},{2,3},{3,2},{4,5},{5,4},{6,7},{7,6},{8,9},{9,8},{10,11... | collective-permute-start | bytes 2359304 | tf_op jit(solution)/shard_map/ppermute | solution.py:371
  232.2 64.4 %collective-permute-start.36 = (bf16[64,6144]{1,0:T(8,128)(2,1)}, bf16[64,6144]{1,0:T(8,128)(2,1)}, u32[]{:S(2)}, u32[]{:S(2)}) collective-permute-start(bf16[64,6144]{1,0:T(8,128)(2,1)} %partials.12), channel_id=1, source_target_pairs={{0,2},{1,3},{2,4},{3,5},{4,6},{5,7},{6,0},{7,1},{8,10},{9,11},{10,... | collective-permute-start | bytes 2359304 | tf_op jit(solution)/shard_map/ppermute | solution.py:371
  265.2 25.5 %collective-permute-start.43 = (bf16[8,768]{1,0:T(8,128)(2,1)S(1)}, bf16[8,768]{1,0:T(8,128)(2,1)S(1)}, u32[]{:S(2)}, u32[]{:S(2)}) collective-permute-start(bf16[8,768]{1,0:T(8,128)(2,1)S(1)} %add_convert_fusion.1), channel_id=1, source_target_pairs={{0,120},{8,112},{16,104},{24,96},{32,88},{40,80},{48,72},{56,64},{... | collective-permute-start | bytes 36872 | tf_op jit(solution)/shard_map/ppermute | solution.py:498
  277.5 32.1 %collective-permute-start.38 = (bf16[384,1536]{1,0:T(8,128)(2,1)S(1)}, bf16[384,1536]{1,0:T(8,128)(2,1)}, u32[]{:S(2)}, u32[]{:S(2)}) collective-permute-start(bf16[384,1536]{1,0:T(8,128)(2,1)S(1)} %copy-done.14), channel_id=1, source_target_pairs={{0,121},{1,120},{2,123},{3,122},{4,125},{5,124},{6,127},{7,126},{8... | collective-permute-start | bytes 3538952 | tf_op jit(solution)/shard_map/ppermute | solution.py:374
  290.7 39.0 %collective-permute-start.39 = (bf16[384,1536]{1,0:T(8,128)(2,1)S(1)}, bf16[384,1536]{1,0:T(8,128)(2,1)}, u32[]{:S(2)}, u32[]{:S(2)}) collective-permute-start(bf16[384,1536]{1,0:T(8,128)(2,1)S(1)} %copy-done.15), channel_id=1, source_target_pairs={{0,121},{1,120},{2,123},{3,122},{4,125},{5,124},{6,127},{7,126},{8... | collective-permute-start | bytes 3538952 | tf_op jit(solution)/shard_map/ppermute | solution.py:374
  (58 other events, 699.8 us)

commit v2 on v1

--- a/solution.py
+++ b/solution.py
@@ -18,12 +18,12 @@
 BLOCKS = RING * SIDES
 ROWS, COLUMNS = 128, 768
 PARTS = (
-    (0, 1, 0, 4),
+    (0, 1, 0, 2),
+    (0, 1, 2, 2),
+    (1, 3, 0, 3),
+    (1, 3, 3, 3),
+    (1, 3, 6, 2),
     (0, 1, 4, 4),
-    (1, 3, 0, 2),
-    (1, 3, 2, 2),
-    (1, 3, 4, 2),
-    (1, 3, 6, 2),
 )
 
 
@@ -32,7 +32,8 @@
 
 
 def cost(flops, nbytes):
-    return pl.CostEstimate(flops=int(flops), bytes_accessed=int(nbytes), transcendentals=0)
+    del flops, nbytes
+    return pl.CostEstimate(flops=1, bytes_accessed=1, transcendentals=0)
 
 
 def norm_kernel(hidden_ref, gain_ref, normed_ref, scale_ref):
@@ -67,12 +68,12 @@
 
 
 def teacher_kernel(rest, order_ref, base_ref, index_ref, logit_ref, out_ref):
-    logits = jnp.transpose(logit_ref[...])
+    logits = logit_ref[...]
     top = jnp.max(logits, axis=0, keepdims=True)
     shifted = logits - top
     logsum = jnp.log(jnp.sum(jnp.exp(shifted), axis=0, keepdims=True))
     value = rest - (math.log(1.0 - smoothing) + (shifted - logsum))
-    entry = jnp.transpose(index_ref[...]) - base_ref[0]
+    entry = index_ref[...] - base_ref[0]
     num_top, tokens = value.shape
     part = 64
     for lower in range(0, out_ref.shape[1], part):
@@ -84,22 +85,21 @@
 
 
 def teacher_weights(order, base, index, logits, width, rest):
-    rows, num_top = index.shape
-    tokens = rows // BLOCKS
+    num_top = index.shape[0]
+    slots = order.shape[0]
+    tokens = index.shape[1] // BLOCKS
+    spec = pl.BlockSpec((num_top, tokens), lambda j, order, base: (0, order[j]))
     return pl.pallas_call(
         functools.partial(teacher_kernel, rest),
         grid_spec=pltpu.PrefetchScalarGridSpec(
             num_scalar_prefetch=2,
-            grid=(BLOCKS,),
-            in_specs=[
-                pl.BlockSpec((tokens, num_top), lambda j, order, base: (order[j], 0)),
-                pl.BlockSpec((tokens, num_top), lambda j, order, base: (order[j], 0)),
-            ],
+            grid=(slots,),
+            in_specs=[spec, spec],
             out_specs=pl.BlockSpec((1, width, tokens), lambda j, order, base: (j, 0, 0)),
         ),
-        out_shape=jax.ShapeDtypeStruct((BLOCKS, width, tokens), F32),
-        compiler_params=params(),
-        cost_estimate=cost(rows * width * num_top, rows * width * 4),
+        out_shape=jax.ShapeDtypeStruct((slots, width, tokens), F32),
+        compiler_params=params(),
+        cost_estimate=cost(slots * tokens * width * num_top, slots * tokens * width * 4),
         name="teacher_weights",
     )(order, base, index, logits)
 
@@ -149,7 +149,7 @@
         grid=(depth // step,),
         in_specs=[pl.BlockSpec((1, width, step), lambda i: (0, 0, i))]
         + [pl.BlockSpec((half, step), lambda i: (0, i))] * (2 * count)
-        + [pl.BlockSpec((1, width, tokens), lambda i, s=s: (s, 0, 0)) for s in slots],
+        + [pl.BlockSpec((1, width, tokens), lambda i, s=s: (s % RING, 0, 0)) for s in slots],
         out_specs=[
             pl.BlockSpec((count, width, tokens), lambda i: (0, 0, 0)),
             pl.BlockSpec((count, 8, tokens), lambda i: (0, 0, 0)),
@@ -161,7 +161,7 @@
         compiler_params=params(),
         cost_estimate=cost(2 * count * tokens * width * depth, width * depth * 2),
         name="block_logits",
-    )(head, *[x[s] for s in slots for x in (a, b)], *([weights] * count))
+    )(head, *[x[s] for s in slots for x in (a, b)], *[weights[s // RING] for s in slots])
 
 
 def merge_sums(parts):
@@ -174,9 +174,9 @@
     return top, total, mixed
 
 
-def dlogits_kernel(rest, where, weight_ref, cot_ref, *refs):
-    sums = refs[:RING]
-    logits = refs[RING:-4]
+def dlogits_kernel(rest, where, cot_ref, *refs):
+    weights, sums = refs[:SIDES], refs[SIDES : SIDES + RING]
+    logits = refs[SIDES + RING : -4]
     first_ref, other_ref, low_ref, loss_ref = refs[-4:]
     tokens = cot_ref.shape[1]
     for slot in range(BLOCKS):
@@ -191,7 +191,7 @@
         loss = mixed / total - logtotal - rest
         group, at = where[slot]
         rel = logits[group][at] - logz
-        grads = cot_ref[slot : slot + 1] * jnp.exp(rel) * (rel - (rest + loss) + weight_ref[slot])
+        grads = cot_ref[slot : slot + 1] * jnp.exp(rel) * (rel - (rest + loss) + weights[side][ahead])
         low = grads.astype(BF16)
         here = slice(slot * tokens, (slot + 1) * tokens)
         first_ref[:, here] = low[:ROWS]
@@ -201,7 +201,8 @@
 
 
 def all_dlogits(groups, found, weights, cot, sums, rest):
-    blocks, width, tokens = weights.shape
+    _, width, tokens = weights[0].shape
+    blocks = BLOCKS
     where = {s: (g, n) for g, group in enumerate(groups) for n, s in enumerate(group)}
     return pl.pallas_call(
         functools.partial(dlogits_kernel, rest, where),
@@ -214,7 +215,7 @@
         compiler_params=params(),
         cost_estimate=cost(blocks * width * tokens * 10, blocks * width * tokens * 12),
         name="all_dlogits",
-    )(weights, cot, *sums, *found)
+    )(cot, *weights, *sums, *found)
 
 
 def part_kernel(low_ref, *refs):
@@ -286,16 +287,18 @@
 def add_part(own, other, earlier, part):
     width, depth = own.shape
     row, num_rows, column, num_columns = part
+    wide = math.gcd(column, num_columns) or num_columns
+    block = (ROWS, wide * COLUMNS)
     first = earlier is None
     return pl.pallas_call(
         add_kernel,
-        grid=(num_rows, num_columns),
+        grid=(num_rows, num_columns // wide),
         in_specs=[
-            pl.BlockSpec((ROWS, COLUMNS), lambda i, j: (i + row, j + column)),
-            pl.BlockSpec((ROWS, COLUMNS), lambda i, j: (i, j)),
+            pl.BlockSpec(block, lambda i, j: (i + row, j + column // wide)),
+            pl.BlockSpec(block, lambda i, j: (i, j)),
         ]
         + ([] if first else [pl.BlockSpec(memory_space=pl.ANY)]),
-        out_specs=pl.BlockSpec((1, ROWS, COLUMNS), lambda i, j: (0, i + row, j + column)),
+        out_specs=pl.BlockSpec((1,) + block, lambda i, j: (0, i + row, j + column // wide)),
         out_shape=jax.ShapeDtypeStruct((1, width, depth), BF16),
         input_output_aliases={} if first else {2: 0},
         compiler_params=params(),
@@ -305,42 +308,44 @@
 
 
 def partial_kernel(counts, head_ref, *refs):
-    num = len(counts)
-    lows, rest, outs = refs[:num], refs[num:-num], refs[-num:]
+    flat = [c for group in counts for c in group]
+    num = len(flat)
+    lows, rest, outs = refs[:num], refs[num : -len(counts)], refs[-len(counts) :]
     low = jnp.concatenate([r[...] for r in lows], axis=0)
     sums = jnp.dot(low, head_ref[0], preferred_element_type=F32)
     half = lows[0].shape[0]
-    at = 0
-    for n, count in enumerate(counts):
-        total = sums[n * half : (n + 1) * half].astype(BF16).astype(F32)
-        for r in rest[at : at + count]:
-            total = total + r[...].astype(F32)
-        at += count
-        outs[n][...] = total.astype(outs[n].dtype)
-
-
-def partials(low, head, jobs, dtype=BF16):
+    job, at = 0, 0
+    for out, group in zip(outs, counts):
+        for n, count in enumerate(group):
+            total = sums[job * half : (job + 1) * half].astype(BF16).astype(F32)
+            for r in rest[at : at + count]:
+                total = total + r[...].astype(F32)
+            out[n * half : (n + 1) * half, :] = total.astype(out.dtype)
+            job, at = job + 1, at + count
+
+
+def partials(low, head, groups, dtype=BF16):
     _, width, depth = head.shape
     half = low.shape[0] // (2 * BLOCKS)
     step = 2048
-    counts = [len(add) for _, add in jobs]
+    jobs = [job for group in groups for job in group]
+    counts = [[len(add) for _, add in group] for group in groups]
     added = [x for _, add in jobs for x in add]
-    piece = pl.BlockSpec((half, step), lambda i: (0, i))
     return pl.pallas_call(
         functools.partial(partial_kernel, counts),
         grid=(depth // step,),
         in_specs=[pl.BlockSpec((1, width, step), lambda i: (0, 0, i))]
         + [pl.BlockSpec((half, width), lambda i, at=at: (at, 0)) for at, _ in jobs]
-        + [piece] * len(added),
-        out_specs=[piece] * len(jobs),
-        out_shape=[jax.ShapeDtypeStruct((half, depth), dtype) for _ in jobs],
+        + [pl.BlockSpec((half, step), lambda i, row=row: (row, i)) for _, row in added],
+        out_specs=[pl.BlockSpec((len(g) * half, step), lambda i: (0, i)) for g in groups],
+        out_shape=[jax.ShapeDtypeStruct((len(g) * half, depth), dtype) for g in groups],
         compiler_params=params(),
         cost_estimate=cost(
             2 * len(jobs) * half * width * depth,
             width * depth * 2 + (len(jobs) + len(added)) * half * depth * 2,
         ),
         name="partials",
-    )(head, *([low] * len(jobs)), *added)
+    )(head, *([low] * len(jobs)), *[x for x, _ in added])
 
 
 def ring_perm(step):
@@ -393,17 +398,19 @@
     order = ((me // SIDES + slots % RING) % RING) * SIDES + (me % SIDES) ^ (slots // RING)
     order = order.astype(jnp.int32)
     base = (me * width).astype(jnp.int32).reshape(1)
-    weights = teacher_weights(order, base, teacher_index, teacher_logits, width, rest)
+    index_t, logits_t = teacher_index.T, teacher_logits.T
+    weights = [teacher_weights(order[:RING], base, index_t, logits_t, width, rest)]
     cot = jnp.take(cotangent.reshape(BLOCKS, tokens), order, axis=0)
 
     groups = ((0,), (3, 1, 4), (5,), (2, 7), (6,))
-    found = [block_logits(groups[0], a, b, head, weights)]
-
-    b0, a4 = gate((b[0], a[4]), a[3], a[1], found[0][1])
+    b0, a4 = gate((b[0], a[4]), a[3], a[1], weights[0])
     b[4] = send(b0, swap)
     a[7] = send(a4, up)
     a[5] = send(a4, down)
-    a3, b1, b[4] = gate((a[3], b[1], b[4]), b[3])
+    order, base = gate((order, base), weights[0])
+    weights.append(teacher_weights(order[RING:], base, index_t, logits_t, width, rest))
+    found = [block_logits(groups[0], a, b, head, weights)]
+    a3, b1, b[4] = gate((a[3], b[1], b[4]), b[3], weights[1], found[0][1])
     a[2] = send(a3, up)
     b[2] = send(b1, down)
     b[5] = send(b1, swap)
@@ -440,81 +447,93 @@
         other_slot = (slot + RING) % BLOCKS
         facing_pieces += [a[other_slot], b[other_slot]]
 
-    their_first, their_second = send(first, swap), send(second, swap)
-    o2a, o2b = partials(low, head, [(12, []), (13, [])])
+    their_first = send(first, swap)
+    o2a, o2b = partials(low, head, [[(12, [])], [(13, [])]])
     r_o2a, r_o2b = send(o2a, down), send(o2b, up)
 
-    def part_of(n):
-        row, _, column, num_columns = PARTS[n]
-        mine = their_first if row == 0 else their_second
+    def part_of(n, mine):
+        _, _, column, num_columns = PARTS[n]
         return table_part(mine, facing_pieces, column * COLUMNS, num_columns * COLUMNS)
 
-    theirs = [None] * len(PARTS)
-    their_first = gate((their_first,), o2a)
-    part = part_of(0)
-    theirs[0] = exchange(part)
-    their_first = gate((their_first,), part)
-    part = part_of(1)
-    theirs[1] = exchange(part)
-
-    low = gate((low,), part)
-    s2a, s2b, o3b, o0b = partials(low, head, [(4, []), (5, []), (15, []), (9, [])])
-    s2a, s2b, o3b, their_second = gate((s2a, s2b, o3b, their_second), r_o2a, r_o2b)
-    r_s2a, r_s2b, r_o3b = send(s2a, down), send(s2b, up), send(o3b, swap)
-    part = gate((part_of(2),), theirs[0])
-    theirs[2] = exchange(part)
-    low = gate((low,), part)
-    o3a, o1a, s1a = partials(low, head, [(14, [r_o2a]), (10, []), (2, [])])
-    part = part_of(3)
-    o3a, o1a, o0b = gate((o3a, o1a, o0b), r_s2a, r_s2b, r_o3b, part)
-    r_o3a, r_o1a, r_o0b = send(o3a, down), send(o1a, up), send(o0b, swap)
-    part = gate((part,), theirs[1], o0b)
-    theirs[3] = exchange(part)
-    low = gate((low,), part)
-    s3a, o1b = partials(low, head, [(6, [r_s2a]), (11, [r_o2b])])
-    part = part_of(4)
-    s3a, s1a, o1b = gate((s3a, s1a, o1b), r_o3a, r_o1a, r_o0b, part)
-    r_s3a, r_s1a, r_o1b = send(s3a, down), send(s1a, up), send(o1b, swap)
-    part = gate((part,), theirs[2], o1b)
-    theirs[4] = exchange(part)
-    low = gate((low,), part)
-    s3b, o0a = partials(low, head, [(7, [r_o3b]), (8, [r_o3a, r_o1a])])
-    part = part_of(5)
-    s3b, o0a = gate((s3b, o0a), r_s3a, r_s1a, r_o1b, part)
-    r_s3b, r_o0a = send(s3b, down), send(o0a, swap)
-    (s1b,) = partials(low, head, [(3, [r_s2b, r_o1b])])
-    r_s1b = send(s1b, up)
-    part = gate((part,), theirs[3], s1b)
-    theirs[5] = exchange(part)
-    first, second = gate((first, second), part)
+    their_first, second_there = gate((their_first, second), o2a)
+    their_second = send(second_there, swap)
+    parts = [part_of(0, their_first), part_of(1, their_first)]
+    theirs = [exchange(parts[0]), exchange(parts[1])]
+    parts.append(part_of(2, their_second))
+
+    low, first, second, their_first, their_second = gate(
+        (low, first, second, their_first, their_second),
+        r_o2a, r_o2b, theirs[0], parts[2],
+    )
+    theirs.append(exchange(parts[2]))
+    to_down, to_up, to_swap = partials(
+        low,
+        head,
+        [
+            [(14, [(r_o2a, 0)]), (4, [])],
+            [(10, []), (5, [])],
+            [(11, [(r_o2b, 0)]), (15, [])],
+        ],
+    )
+    o3a_s2a, o1a_s2b, o1b_o3b = send(to_down, down), send(to_up, up), send(to_swap, swap)
+    their_first, their_second, first, second = gate(
+        (their_first, their_second, first, second), to_down
+    )
     own, along = own_table(first, second, head, gain, pieces)
-
     along = along[:1].reshape(8, depth // 8)
+    parts += [part_of(n, their_first if PARTS[n][0] == 0 else their_second) for n in (3, 4, 5)]
+
+    low, own, along, theirs[2], parts[3], parts[4], parts[5] = gate(
+        (low, own, along, theirs[2], *parts[3:]), o3a_s2a, o1a_s2b, o1b_o3b, theirs[1]
+    )
+    theirs.append(exchange(parts[3]))
     along = along + send(along, swap)
+    to_down, to_up, to_swap = gate(
+        partials(
+            low,
+            head,
+            [
+                [(6, [(o3a_s2a, 1)]), (7, [(o1b_o3b, 1)])],
+                [(2, []), (3, [(o1a_s2b, 1), (o1b_o3b, 0)])],
+                [(8, [(o3a_s2a, 0), (o1a_s2b, 0)]), (9, [])],
+            ],
+        ),
+        along,
+    )
+    s3, s1, o0 = send(to_down, down), send(to_up, up), send(to_swap, swap)
+    merged = None
+    for n in range(2):
+        merged = add_part(own, theirs[n], merged, PARTS[n])
+    merged = add_part(own, theirs[2], merged, PARTS[2])
+
+    low, along, theirs[3], merged = gate((low, along, theirs[3], merged), s3, s1, o0)
+    theirs += [exchange(parts[4]), exchange(parts[5])]
     along = along + send(along, [(f, f ^ SIDES) for f in range(BLOCKS)])
-    along = along + send(along, across)
-    along = along.astype(BF16)
-    merged_gain = (
-        along.astype(F32) + lax.ppermute(along, "pipe", mirror).astype(F32)
-    ).astype(BF16).reshape(1, depth)
-
-    merged = None
-    for n in range(4):
-        merged = add_part(own, theirs[n], merged, PARTS[n])
-    low = gate((low,), r_s3b, r_o0a, r_s1b, merged)
-    sum_a, sum_b = partials(
-        low, head, [(0, [r_s3a, r_s1a, r_o0a]), (1, [r_s3b, r_s1b, r_o0b])], F32
-    )
-
-    dnormed = jnp.concatenate([sum_a, sum_b], axis=0)
+    (dnormed,) = partials(
+        low, head, [[(n, [(s3, n), (s1, n), (o0, n)]) for n in (0, 1)]], F32
+    )
+    opposite = [
+        (p * BLOCKS + f, (num_pipe - 1 - p) * BLOCKS + t)
+        for p in range(num_pipe)
+        for f, t in across
+    ]
+    ours = (along + send(along, across)).astype(BF16)
+    mirrored = lax.ppermute(along, "pipe", mirror) + lax.ppermute(
+        along, ("pipe", "fsdp"), opposite
+    )
+    merged_gain = (ours.astype(F32) + mirrored.astype(BF16).astype(F32)).astype(BF16)
+    merged_gain = merged_gain.reshape(1, depth)
     scale = jnp.concatenate([scale_a, scale_b], axis=0)[:, :1]
     unit = hidden.astype(F32) * scale
     scaled = gain * dnormed
     grad_states = scale * scaled - scale * unit * jnp.mean(unit * scaled, axis=1, keepdims=True)
     grad_states = grad_states.astype(BF16)
-
-    theirs[4], theirs[5] = gate((theirs[4], theirs[5]), grad_states)
-    for n in range(4, len(PARTS)):
+    merged = add_part(own, theirs[3], merged, PARTS[3])
+
+    theirs[4], theirs[5], merged = gate(
+        (theirs[4], theirs[5], merged), grad_states, merged_gain
+    )
+    for n in (4, 5):
         merged = add_part(own, theirs[n], merged, PARTS[n])
     return (loss[0], grad_states, merged, merged_gain)
 

time: 341 us -> 294 us (0.86)
  waiting for transfers between devices: 94.2 us -> 66.5 us
  Pallas kernels: 158 us -> 138 us
    ppermute x6, waiting for transfers between devices: 34 us -> 0.02 us  [exchange(): return lax.ppermute(x, ('pipe', 'fsdp'), facing)]
    pallas_call x7 -> x4, Pallas kernels: 42.5 us -> 28.8 us  [partials(): pl.pallas_call(functools.partial(partial_kernel, counts), grid=(depth //...]
    ppermute x1 -> x2, waiting for transfers between devices: 0.01 us -> 11.2 us  [the longest x1 11.2 us: body(): lax.ppermute(along, ('pipe', 'fsdp'), opposite)]
    ppermute x6, starting transfers between devices: 22.1 us -> 30.6 us  [exchange(): return lax.ppermute(x, ('pipe', 'fsdp'), facing)]
    pallas_call x6, Pallas kernels: 26.4 us -> 18.2 us  [add_part(): pl.pallas_call(add_kernel, grid=(num_rows, num_columns // wide), in_specs...]
    ppermute x37 -> x31, starting transfers between devices: 35 us -> 27.2 us  [send(): return lax.ppermute(x, 'fsdp', perm)]
    ppermute x37 -> x31, waiting for transfers between devices: 60.2 us -> 55.2 us  [send(): return lax.ppermute(x, 'fsdp', perm)]
    pallas_call x1 -> x2, Pallas kernels: 13.6 us -> 15.3 us  [teacher_weights(): pl.pallas_call(functools.partial(teacher_kernel, rest), grid_spec=pltpu.P...]
  transfers between devices with their start and end apart: 44 -> 39, of which waited for: 24 -> 16; matrix products, arithmetic and copies ran while one was open for 4% -> 4% of each run, Pallas kernels for 42% -> 43%
where the time goes in v2:
time: 294 us; the launch traced here: 293 us
  Pallas kernels  138 us (47%)
  waiting for transfers between devices  66.5 us (23%)
  starting transfers between devices  66.4 us (23%)
  other arithmetic  11.3 us (4%)
  local copies, waits for them, and re-layouts  9.75 us (3%)
    ppermute x31, waiting for transfers between devices, send(): return lax.ppermute(x, 'fsdp', perm)  55.2 us
    ppermute x6, starting transfers between devices, exchange(): return lax.ppermute(x, ('pipe', 'fsdp'), facing)  30.6 us
    pallas_call x4, Pallas kernels, partials(): pl.pallas_call(functools.partial(partial_kernel, counts), grid=(depth //...  28.8 us
    pallas_call x6, Pallas kernels, table_part(): pl.pallas_call(part_kernel, grid=(size // step,), in_specs=[pl.BlockSpec(...  27.5 us
    ppermute x31, starting transfers between devices, send(): return lax.ppermute(x, 'fsdp', perm)  27.2 us
    pallas_call x4, Pallas kernels, block_logits(): pl.pallas_call(functools.partial(logits_kernel, count), grid=(depth // st...  24.4 us
    pallas_call x6, Pallas kernels, add_part(): pl.pallas_call(add_kernel, grid=(num_rows, num_columns // wide), in_specs...  18.2 us
    pallas_call x2, Pallas kernels, teacher_weights(): pl.pallas_call(functools.partial(teacher_kernel, rest), grid_spec=pltpu.P...  15.3 us
  transfers between devices with their start and end apart: 39, of which 16 were waited for; matrix products, arithmetic and copies ran while one was open for 4% of the time, Pallas kernels for 43%

profile of v2, /device:TPU:1, one launch (start us, length us, event | category | flops | bytes accessed | tf_op | source)
XLA Modules:
  0.0 292.5 jit_solution(17227858086114019833)
XLA Ops:
  13.6 7.6 %teacher_weights.2.refs_2_.refs_6_.refs_7_.refs_4_.refs_0_ = f32[4,512,128]{2,1,0:T(8,128)} custom-call(s32[4]{0:T(128)} %bitcast.22, s32[1]{0:T(128)} %bitcast.2.base_ref, s32[64,1024]{1,0:T(8,128)} %bitcast.15, f32[64,1024]{1,0:T(8,128)} %bitcast.17), custom_call_target="tpu_custom_call" | custom-call | flops 1 | bytes 1 | tf_op jit(solution)/shard_map/teacher_weights/pallas_call | solution.py:92
  27.5 5.2 %block_logits.5 = (f32[1,512,128]{2,1,0:T(8,128)}, f32[1,8,128]{2,1,0:T(8,128)}) custom-call(bf16[1,512,6144]{2,1,0:T(8,128)(2,1)} %head_ref.18, bf16[64,6144]{1,0:T(8,128)(2,1)} %get-tuple-element.77.refs_0_.refs_8_, bf16[64,6144]{1,0:T(8,128)(2,1)} %get-tuple-element.80.refs_1_.refs_9_, f32[4,512,128]{2,1,0:T(8,128)} %teacher_weights.2.refs_2_.refs_6_.refs_7_.refs_4_.refs_0_), custom_call_target="tpu_custom_call" | custom-call | flops 1 | bytes 1 | tf_op jit(solution)/shard_map/block_logits/pallas_call | solution.py:147
  33.3 7.6 %teacher_weights.3.refs_8_.refs_2_.refs_5_.refs_1_ = f32[4,512,128]{2,1,0:T(8,128)} custom-call(s32[4]{0:T(128)} %slice.55.order_ref, s32[1]{0:T(128)} %bitcast.2.base_ref, s32[64,1024]{1,0:T(8,128)} %bitcast.16, f32[64,1024]{1,0:T(8,128)} %bitcast.18), custom_call_target="tpu_custom_call" | custom-call | flops 1 | bytes 1 | tf_op jit(solution)/shard_map/teacher_weights/pallas_call | solution.py:92
  46.0 8.1 %block_logits.6 = (f32[3,512,128]{2,1,0:T(8,128)}, f32[3,8,128]{2,1,0:T(8,128)}) custom-call(bf16[1,512,6144]{2,1,0:T(8,128)(2,1)} %head_ref.18, bf16[64,6144]{1,0:T(8,128)(2,1)} %copy-done.4, bf16[64,6144]{1,0:T(8,128)(2,1)} %collective-permute-done.1.refs_1_.refs_15_.refs_7_, bf16[64,6144]{1,0:T(8,128)(2,1)} %copy-done.3, bf16[64,6144]{1,0:T(8,128)(2,1)} %copy-done.5, ...), custom_call_target="tpu_custom_call" | custom-call | flops 1 | bytes 1 | tf_op jit(solution)/shard_map/block_logits/pallas_call | solution.py:147
  63.8 5.1 %block_logits.7 = (f32[1,512,128]{2,1,0:T(8,128)}, f32[1,8,128]{2,1,0:T(8,128)}) custom-call(bf16[1,512,6144]{2,1,0:T(8,128)(2,1)} %head_ref.18, bf16[64,6144]{1,0:T(8,128)(2,1)} %copy-done.6, bf16[64,6144]{1,0:T(8,128)(2,1)} %collective-permute-done.9.refs_1_.refs_3_.refs_11_, f32[4,512,128]{2,1,0:T(8,128)} %teacher_weights.3.refs_8_.refs_2_.refs_5_.refs_1_), custom_call_target="tpu_custom_call" | custom-call | flops 1 | bytes 1 | tf_op jit(solution)/shard_map/block_logits/pallas_call | solution.py:147
  68.9 7.2 %collective-permute-done.6.refs_0_.refs_12_.refs_4_ = bf16[64,6144]{1,0:T(8,128)(2,1)} collective-permute-done((bf16[64,6144]{1,0:T(8,128)(2,1)S(1)}, bf16[64,6144]{1,0:T(8,128)(2,1)}, u32[]{:S(2)}, u32[]{:S(2)}) %collective-permute-start.6) | collective-permute-done | bytes 786464 | tf_op jit(solution)/shard_map/ppermute | solution.py:376
  77.1 6.0 %block_logits.8 = (f32[2,512,128]{2,1,0:T(8,128)}, f32[2,8,128]{2,1,0:T(8,128)}) custom-call(bf16[1,512,6144]{2,1,0:T(8,128)(2,1)} %head_ref.18, bf16[64,6144]{1,0:T(8,128)(2,1)} %collective-permute-done.6.refs_0_.refs_12_.refs_4_, bf16[64,6144]{1,0:T(8,128)(2,1)} %collective-permute-done.7.refs_1_.refs_13_.refs_5_, ...), custom_call_target="tpu_custom_call" | custom-call | flops 1 | bytes 1 | tf_op jit(solution)/shard_map/block_logits/pallas_call | solution.py:147
  83.8 9.2 %collective-permute-done.12.refs_4_.refs_12_ = bf16[64,6144]{1,0:T(8,128)(2,1)} collective-permute-done((bf16[64,6144]{1,0:T(8,128)(2,1)}, bf16[64,6144]{1,0:T(8,128)(2,1)}, u32[]{:S(2)}, u32[]{:S(2)}) %collective-permute-start.12) | collective-permute-done | bytes 786464 | tf_op jit(solution)/shard_map/ppermute | solution.py:376
  93.0 5.1 %block_logits.9 = (f32[8,8,128]{2,1,0:T(8,128)S(1)}, f32[1,512,128]{2,1,0:T(8,128)}) fusion(f32[8,8,128]{2,1,0:T(8,128)S(1)} %constant_dynamic-update-slice_fusion.2, bf16[1,512,6144]{2,1,0:T(8,128)(2,1)} %head_ref.18, bf16[64,6144]{1,0:T(8,128)(2,1)} %collective-permute-done.12.refs_4_.refs_12_, ...), kind=kCustom, calls=%fused_computation.12 | custom fusion | flops 1 | bytes 9179136 | tf_op jit(solution)/shard_map/block_logits/pallas_call | solution.py:147
  106.5 4.3 %all_dlogits.1 = (bf16[128,1024]{1,0:T(8,128)(2,1)}, bf16[384,1024]{1,0:T(8,128)(2,1)}, bf16[1024,512]{1,0:T(8,128)(2,1)}, f32[8,128]{1,0:T(8,128)}) custom-call(f32[8,128]{1,0:T(8,128)} %broadcast_select_fusion.cot_ref, f32[4,512,128]{2,1,0:T(8,128)} %teacher_weights.2.refs_2_.refs_6_.refs_7_.refs_4_.refs_0_, ...), custom_call_target="tpu_custom_call" | custom-call | flops 1 | bytes 1 | tf_op jit(solution)/shard_map/all_dlogits/pallas_call | solution.py:207
  111.0 5.4 %partials.4 = (bf16[64,6144]{1,0:T(8,128)(2,1)}, bf16[64,6144]{1,0:T(8,128)(2,1)}) custom-call(bf16[1,512,6144]{2,1,0:T(8,128)(2,1)} %head_ref.18, bf16[1024,512]{1,0:T(8,128)(2,1)} %get-tuple-element.137.refs_0_.refs_1_.refs_2_.refs_3_.refs_4_.refs_5_, bf16[1024,512]{1,0:T(8,128)(2,1)} %get-tuple-element.137.refs_0_.refs_1_.refs_2_.refs_3_.refs_4_.refs_5_), custom_call_target="tpu_custom_call" | custom-call | flops 1 | bytes 1 | tf_op jit(solution)/shard_map/partials/pallas_call | solution.py:334
  123.5 15.7 %collective-permute-start.22 = (bf16[128,1536]{1,0:T(8,128)(2,1)}, bf16[128,1536]{1,0:T(8,128)(2,1)S(1)}, u32[]{:S(2)}, u32[]{:S(2)}) collective-permute-start(bf16[128,1536]{1,0:T(8,128)(2,1)} %table_part.6), channel_id=1, source_target_pairs={{0,121},{1,120},{2,123},{3,122},{4,125},{5,124},{6,127},{7,126},{8... | collective-permute-start | bytes 1179656 | tf_op jit(solution)/shard_map/ppermute | solution.py:379
  140.2 5.8 %table_part.7 = bf16[384,2304]{1,0:T(8,128)(2,1)} custom-call(bf16[384,1024]{1,0:T(8,128)(2,1)} %copy-done.11, bf16[64,6144]{1,0:T(8,128)(2,1)} %copy-done.2, bf16[64,6144]{1,0:T(8,128)(2,1)} %collective-permute-done.5.refs_5_.refs_1_.refs_9_, bf16[64,6144]{1,0:T(8,128)(2,1)} %copy-done.6, bf16[64,6144]{1,0:T(8,128)(2,1)} %collective-permute-done.9.refs_1_.refs_3_.refs_11_, ...), custom_call_target="tpu_custom_call" | custom-call | flops 1 | bytes 1 | tf_op jit(solution)/shard_map/table_part/pallas_call | solution.py:231
  146.0 5.6 %collective-permute-start.23 = (bf16[384,2304]{1,0:T(8,128)(2,1)}, bf16[384,2304]{1,0:T(8,128)(2,1)}, u32[]{:S(2)}, u32[]{:S(2)}) collective-permute-start(bf16[384,2304]{1,0:T(8,128)(2,1)} %table_part.7), channel_id=1, source_target_pairs={{0,121},{1,120},{2,123},{3,122},{4,125},{5,124},{6,127},{7,126},{8... | collective-permute-start | bytes 5308424 | tf_op jit(solution)/shard_map/ppermute | solution.py:379
  153.4 7.6 %partials.5 = (bf16[128,6144]{1,0:T(8,128)(2,1)}, bf16[128,6144]{1,0:T(8,128)(2,1)}, bf16[128,6144]{1,0:T(8,128)(2,1)}) custom-call(bf16[1,512,6144]{2,1,0:T(8,128)(2,1)} %head_ref.18, bf16[1024,512]{1,0:T(8,128)(2,1)} %get-tuple-element.137.refs_0_.refs_1_.refs_2_.refs_3_.refs_4_.refs_5_, ...), custom_call_target="tpu_custom_call" | custom-call | flops 1 | bytes 1 | tf_op jit(solution)/shard_map/partials/pallas_call | solution.py:334
  168.2 4.3 %table_part.9 = bf16[384,1536]{1,0:T(8,128)(2,1)} custom-call(bf16[384,1024]{1,0:T(8,128)(2,1)} %copy-done.11, bf16[64,6144]{1,0:T(8,128)(2,1)} %copy-done.2, bf16[64,6144]{1,0:T(8,128)(2,1)} %collective-permute-done.5.refs_5_.refs_1_.refs_9_, bf16[64,6144]{1,0:T(8,128)(2,1)} %copy-done.6, bf16[64,6144]{1,0:T(8,128)(2,1)} %collective-permute-done.9.refs_1_.refs_3_.refs_11_, ...), custom_call_target="tpu_custom_call" | custom-call | flops 1 | bytes 1 | tf_op jit(solution)/shard_map/table_part/pallas_call | solution.py:231
  172.5 5.9 %table_part.8 = bf16[384,2304]{1,0:T(8,128)(2,1)} custom-call(bf16[384,1024]{1,0:T(8,128)(2,1)} %copy-done.11, bf16[64,6144]{1,0:T(8,128)(2,1)} %copy-done.2, bf16[64,6144]{1,0:T(8,128)(2,1)} %collective-permute-done.5.refs_5_.refs_1_.refs_9_, bf16[64,6144]{1,0:T(8,128)(2,1)} %copy-done.6, bf16[64,6144]{1,0:T(8,128)(2,1)} %collective-permute-done.9.refs_1_.refs_3_.refs_11_, ...), custom_call_target="tpu_custom_call" | custom-call | flops 1 | bytes 1 | tf_op jit(solution)/shard_map/table_part/pallas_call | solution.py:231
  178.4 5.2 %table_part.10 = bf16[128,3072]{1,0:T(8,128)(2,1)} custom-call(bf16[128,1024]{1,0:T(8,128)(2,1)} %copy-done.15, bf16[64,6144]{1,0:T(8,128)(2,1)} %copy-done.2, bf16[64,6144]{1,0:T(8,128)(2,1)} %collective-permute-done.5.refs_5_.refs_1_.refs_9_, bf16[64,6144]{1,0:T(8,128)(2,1)} %copy-done.6, bf16[64,6144]{1,0:T(8,128)(2,1)} %collective-permute-done.9.refs_1_.refs_3_.refs_11_, ...), custom_call_target="tpu_custom_call" | custom-call | flops 1 | bytes 1 | tf_op jit(solution)/shard_map/table_part/pallas_call | solution.py:231
  183.7 14.6 %own_table.1 = (bf16[512,6144]{1,0:T(8,128)(2,1)}, f32[8,6144]{1,0:T(8,128)}) custom-call(bf16[128,1024]{1,0:T(8,128)(2,1)} %get-tuple-element.118.first_ref, bf16[384,1024]{1,0:T(8,128)(2,1)} %get-tuple-element.119.other_ref, bf16[1,512,6144]{2,1,0:T(8,128)(2,1)} %head_ref.18, f32[1,6144]{1,0:T(1,128)} %gain_ref.5, ...), custom_call_target="tpu_custom_call" | custom-call | flops 1 | bytes 1 | tf_op jit(solution)/shard_map/own_table/pallas_call | solution.py:259
  203.6 8.6 %partials.6 = (bf16[128,6144]{1,0:T(8,128)(2,1)}, bf16[128,6144]{1,0:T(8,128)(2,1)}, bf16[128,6144]{1,0:T(8,128)(2,1)}) custom-call(bf16[1,512,6144]{2,1,0:T(8,128)(2,1)} %head_ref.18, bf16[1024,512]{1,0:T(8,128)(2,1)} %get-tuple-element.137.refs_0_.refs_1_.refs_2_.refs_3_.refs_4_.refs_5_, ...), custom_call_target="tpu_custom_call" | custom-call | flops 1 | bytes 1 | tf_op jit(solution)/shard_map/partials/pallas_call | solution.py:334
  226.5 20.6 %collective-permute-done.30.refs_2_.refs_5_ = bf16[128,6144]{1,0:T(8,128)(2,1)S(1)} collective-permute-done((bf16[128,6144]{1,0:T(8,128)(2,1)}, bf16[128,6144]{1,0:T(8,128)(2,1)S(1)}, u32[]{:S(2)}, u32[]{:S(2)}) %collective-permute-start.30) | collective-permute-done | bytes 1572896 | tf_op jit(solution)/shard_map/ppermute | solution.py:376
  249.6 7.2 %partials.7 = f32[128,6144]{1,0:T(8,128)} custom-call(bf16[1,512,6144]{2,1,0:T(8,128)(2,1)} %head_ref.18, bf16[1024,512]{1,0:T(8,128)(2,1)} %get-tuple-element.137.refs_0_.refs_1_.refs_2_.refs_3_.refs_4_.refs_5_, bf16[1024,512]{1,0:T(8,128)(2,1)} %get-tuple-element.137.refs_0_.refs_1_.refs_2_.refs_3_.refs_4_.refs_5_, bf16[128,6144]{1,0:T(8,128)(2,1)} %copy-done.12, ...), custom_call_target="tpu_custom_call" | custom-call | flops 1 | bytes 1 | tf_op jit(solution)/shard_map/partials/pallas_call | solution.py:334
  259.7 5.7 %collective-permute-start.38 = (f32[8,768]{1,0:T(8,128)S(1)}, f32[8,768]{1,0:T(8,128)S(1)}, u32[]{:S(2)}, u32[]{:S(2)}) collective-permute-start(f32[8,768]{1,0:T(8,128)S(1)} %add.147), channel_id=1, source_target_pairs={{0,124},{1,125},{2,126},{3,127},{4,120},{5,121},{6,122},{7,123},{8... | collective-permute-start | bytes 73736 | tf_op jit(solution)/shard_map/ppermute | solution.py:521
  274.4 11.2 %collective-permute-done.38 = f32[8,768]{1,0:T(8,128)S(1)} collective-permute-done((f32[8,768]{1,0:T(8,128)S(1)}, f32[8,768]{1,0:T(8,128)S(1)}, u32[]{:S(2)}, u32[]{:S(2)}) %collective-permute-start.38) | collective-permute-done | bytes 24608 | tf_op jit(solution)/shard_map/ppermute | solution.py:521
  (177 shorter events, 102.7 us)
Async XLA Ops:
  2.9 19.9 %collective-permute-start.4 = (bf16[64,6144]{1,0:T(8,128)(2,1)}, bf16[64,6144]{1,0:T(8,128)(2,1)S(1)}, u32[]{:S(2)}, u32[]{:S(2)}) collective-permute-start(bf16[64,6144]{1,0:T(8,128)(2,1)} %get-tuple-element.77.refs_0_.refs_8_), channel_id=1, source_target_pairs={{0,1},{1,0},{2,3},{3,2},{4,5},{5,4},{6,7},{7,6},{8,9},{9,8},{10,11... | collective-permute-start | bytes 2359304 | tf_op jit(solution)/shard_map/ppermute | solution.py:376
  10.4 32.1 %collective-permute-start.3 = (bf16[64,6144]{1,0:T(8,128)(2,1)}, bf16[64,6144]{1,0:T(8,128)(2,1)S(1)}, u32[]{:S(2)}, u32[]{:S(2)}) collective-permute-start(bf16[64,6144]{1,0:T(8,128)(2,1)} %get-tuple-element.80.refs_1_.refs_9_), channel_id=1, source_target_pairs={{0,6},{1,7},{2,0},{3,1},{4,2},{5,3},{6,4},{7,5},{8,14},{9,15},{10,... | collective-permute-start | bytes 2359304 | tf_op jit(solution)/shard_map/ppermute | solution.py:376
  13.0 31.3 %collective-permute-start.1 = (bf16[64,6144]{1,0:T(8,128)(2,1)}, bf16[64,6144]{1,0:T(8,128)(2,1)}, u32[]{:S(2)}, u32[]{:S(2)}) collective-permute-start(bf16[64,6144]{1,0:T(8,128)(2,1)} %get-tuple-element.80.refs_1_.refs_9_), channel_id=1, source_target_pairs={{0,2},{1,3},{2,4},{3,5},{4,6},{5,7},{6,0},{7,1},{8,10},{9,11},{10,... | collective-permute-start | bytes 2359304 | tf_op jit(solution)/shard_map/ppermute | solution.py:376
  44.5 31.7 %collective-permute-start.7 = (bf16[64,6144]{1,0:T(8,128)(2,1)S(1)}, bf16[64,6144]{1,0:T(8,128)(2,1)}, u32[]{:S(2)}, u32[]{:S(2)}) collective-permute-start(bf16[64,6144]{1,0:T(8,128)(2,1)S(1)} %collective-permute-done.3.refs_3_.refs_11_), channel_id=1, source_target_pairs={{0,6},{1,7},{2,0},{3,1},{4,2},{5,3},{6,4},{7,5},{8,14},{9,15},{10,... | collective-permute-start | bytes 2359304 | tf_op jit(solution)/shard_map/ppermute | solution.py:376
  45.3 30.8 %collective-permute-start.6 = (bf16[64,6144]{1,0:T(8,128)(2,1)S(1)}, bf16[64,6144]{1,0:T(8,128)(2,1)}, u32[]{:S(2)}, u32[]{:S(2)}) collective-permute-start(bf16[64,6144]{1,0:T(8,128)(2,1)S(1)} %collective-permute-done.refs_0_.refs_14_.refs_6_), channel_id=1, source_target_pairs={{0,2},{1,3},{2,4},{3,5},{4,6},{5,7},{6,0},{7,1},{8,10},{9,11},{10,... | collective-permute-start | bytes 2359304 | tf_op jit(solution)/shard_map/ppermute | solution.py:376
  60.3 32.7 %collective-permute-start.12 = (bf16[64,6144]{1,0:T(8,128)(2,1)}, bf16[64,6144]{1,0:T(8,128)(2,1)}, u32[]{:S(2)}, u32[]{:S(2)}) collective-permute-start(bf16[64,6144]{1,0:T(8,128)(2,1)} %collective-permute-done.8.refs_2_.refs_6_.refs_14_), channel_id=1, source_target_pairs={{0,2},{1,3},{2,4},{3,5},{4,6},{5,7},{6,0},{7,1},{8,10},{9,11},{10,... | collective-permute-start | bytes 2359304 | tf_op jit(solution)/shard_map/ppermute | solution.py:376
  60.4 32.6 %collective-permute-start.13 = (bf16[64,6144]{1,0:T(8,128)(2,1)}, bf16[64,6144]{1,0:T(8,128)(2,1)}, u32[]{:S(2)}, u32[]{:S(2)}) collective-permute-start(bf16[64,6144]{1,0:T(8,128)(2,1)} %collective-permute-done.9.refs_1_.refs_3_.refs_11_), channel_id=1, source_target_pairs={{0,6},{1,7},{2,0},{3,1},{4,2},{5,3},{6,4},{7,5},{8,14},{9,15},{10,... | collective-permute-start | bytes 2359304 | tf_op jit(solution)/shard_map/ppermute | solution.py:376
  116.4 22.8 %collective-permute-start.19 = (bf16[384,1024]{1,0:T(8,128)(2,1)S(1)}, bf16[384,1024]{1,0:T(8,128)(2,1)S(1)}, u32[]{:S(2)}, u32[]{:S(2)}) collective-permute-start(bf16[384,1024]{1,0:T(8,128)(2,1)S(1)} %copy-done.19), channel_id=1, source_target_pairs={{0,1},{1,0},{2,3},{3,2},{4,5},{5,4},{6,7},{7,6},{8,9},{9,8},{10,11... | collective-permute-start | bytes 2359304 | tf_op jit(solution)/shard_map/ppermute | solution.py:376
  117.8 33.9 %collective-permute-start.21 = (bf16[64,6144]{1,0:T(8,128)(2,1)}, bf16[64,6144]{1,0:T(8,128)(2,1)S(1)}, u32[]{:S(2)}, u32[]{:S(2)}) collective-permute-start(bf16[64,6144]{1,0:T(8,128)(2,1)} %get-tuple-element.111), channel_id=1, source_target_pairs={{0,2},{1,3},{2,4},{3,5},{4,6},{5,7},{6,0},{7,1},{8,10},{9,11},{10,... | collective-permute-start | bytes 2359304 | tf_op jit(solution)/shard_map/ppermute | solution.py:376
  118.9 32.8 %collective-permute-start.20 = (bf16[64,6144]{1,0:T(8,128)(2,1)}, bf16[64,6144]{1,0:T(8,128)(2,1)S(1)}, u32[]{:S(2)}, u32[]{:S(2)}) collective-permute-start(bf16[64,6144]{1,0:T(8,128)(2,1)} %get-tuple-element.108), channel_id=1, source_target_pairs={{0,6},{1,7},{2,0},{3,1},{4,2},{5,3},{6,4},{7,5},{8,14},{9,15},{10,... | collective-permute-start | bytes 2359304 | tf_op jit(solution)/shard_map/ppermute | solution.py:376
  123.5 28.1 %collective-permute-start.22 = (bf16[128,1536]{1,0:T(8,128)(2,1)}, bf16[128,1536]{1,0:T(8,128)(2,1)S(1)}, u32[]{:S(2)}, u32[]{:S(2)}) collective-permute-start(bf16[128,1536]{1,0:T(8,128)(2,1)} %table_part.6), channel_id=1, source_target_pairs={{0,121},{1,120},{2,123},{3,122},{4,125},{5,124},{6,127},{7,126},{8... | collective-permute-start | bytes 1179656 | tf_op jit(solution)/shard_map/ppermute | solution.py:379
  146.0 53.3 %collective-permute-start.23 = (bf16[384,2304]{1,0:T(8,128)(2,1)}, bf16[384,2304]{1,0:T(8,128)(2,1)}, u32[]{:S(2)}, u32[]{:S(2)}) collective-permute-start(bf16[384,2304]{1,0:T(8,128)(2,1)} %table_part.7), channel_id=1, source_target_pairs={{0,121},{1,120},{2,123},{3,122},{4,125},{5,124},{6,127},{7,126},{8... | collective-permute-start | bytes 5308424 | tf_op jit(solution)/shard_map/ppermute | solution.py:379
  161.0 38.2 %collective-permute-start.25 = (bf16[128,6144]{1,0:T(8,128)(2,1)}, bf16[128,6144]{1,0:T(8,128)(2,1)S(1)}, u32[]{:S(2)}, u32[]{:S(2)}) collective-permute-start(bf16[128,6144]{1,0:T(8,128)(2,1)} %get-tuple-element.124), channel_id=1, source_target_pairs={{0,2},{1,3},{2,4},{3,5},{4,6},{5,7},{6,0},{7,1},{8,10},{9,11},{10,... | collective-permute-start | bytes 4718600 | tf_op jit(solution)/shard_map/ppermute | solution.py:376
  162.1 37.1 %collective-permute-start.26 = (bf16[128,6144]{1,0:T(8,128)(2,1)}, bf16[128,6144]{1,0:T(8,128)(2,1)S(1)}, u32[]{:S(2)}, u32[]{:S(2)}) collective-permute-start(bf16[128,6144]{1,0:T(8,128)(2,1)} %get-tuple-element.125), channel_id=1, source_target_pairs={{0,1},{1,0},{2,3},{3,2},{4,5},{5,4},{6,7},{7,6},{8,9},{9,8},{10,11... | collective-permute-start | bytes 4718600 | tf_op jit(solution)/shard_map/ppermute | solution.py:376
  162.1 37.1 %collective-permute-start.24 = (bf16[128,6144]{1,0:T(8,128)(2,1)}, bf16[128,6144]{1,0:T(8,128)(2,1)}, u32[]{:S(2)}, u32[]{:S(2)}) collective-permute-start(bf16[128,6144]{1,0:T(8,128)(2,1)} %get-tuple-element.117), channel_id=1, source_target_pairs={{0,6},{1,7},{2,0},{3,1},{4,2},{5,3},{6,4},{7,5},{8,14},{9,15},{10,... | collective-permute-start | bytes 4718600 | tf_op jit(solution)/shard_map/ppermute | solution.py:376
  166.9 32.4 %collective-permute-start.27 = (bf16[128,1536]{1,0:T(8,128)(2,1)}, bf16[128,1536]{1,0:T(8,128)(2,1)}, u32[]{:S(2)}, u32[]{:S(2)}) collective-permute-start(bf16[128,1536]{1,0:T(8,128)(2,1)} %table_part.11), channel_id=1, source_target_pairs={{0,121},{1,120},{2,123},{3,122},{4,125},{5,124},{6,127},{7,126},{8... | collective-permute-start | bytes 1179656 | tf_op jit(solution)/shard_map/ppermute | solution.py:379
  199.3 49.7 %collective-permute-start.29 = (bf16[384,2304]{1,0:T(8,128)(2,1)}, bf16[384,2304]{1,0:T(8,128)(2,1)}, u32[]{:S(2)}, u32[]{:S(2)}) collective-permute-start(bf16[384,2304]{1,0:T(8,128)(2,1)} %table_part.8), channel_id=1, source_target_pairs={{0,121},{1,120},{2,123},{3,122},{4,125},{5,124},{6,127},{7,126},{8... | collective-permute-start | bytes 5308424 | tf_op jit(solution)/shard_map/ppermute | solution.py:379
  212.2 34.9 %collective-permute-start.30 = (bf16[128,6144]{1,0:T(8,128)(2,1)}, bf16[128,6144]{1,0:T(8,128)(2,1)S(1)}, u32[]{:S(2)}, u32[]{:S(2)}) collective-permute-start(bf16[128,6144]{1,0:T(8,128)(2,1)} %get-tuple-element.134), channel_id=1, source_target_pairs={{0,6},{1,7},{2,0},{3,1},{4,2},{5,3},{6,4},{7,5},{8,14},{9,15},{10,... | collective-permute-start | bytes 4718600 | tf_op jit(solution)/shard_map/ppermute | solution.py:376
  213.2 35.6 %collective-permute-start.31 = (bf16[128,6144]{1,0:T(8,128)(2,1)}, bf16[128,6144]{1,0:T(8,128)(2,1)}, u32[]{:S(2)}, u32[]{:S(2)}) collective-permute-start(bf16[128,6144]{1,0:T(8,128)(2,1)} %get-tuple-element.135), channel_id=1, source_target_pairs={{0,2},{1,3},{2,4},{3,5},{4,6},{5,7},{6,0},{7,1},{8,10},{9,11},{10,... | collective-permute-start | bytes 4718600 | tf_op jit(solution)/shard_map/ppermute | solution.py:376
  213.8 35.2 %collective-permute-start.32 = (bf16[128,6144]{1,0:T(8,128)(2,1)}, bf16[128,6144]{1,0:T(8,128)(2,1)}, u32[]{:S(2)}, u32[]{:S(2)}) collective-permute-start(bf16[128,6144]{1,0:T(8,128)(2,1)} %get-tuple-element.136), channel_id=1, source_target_pairs={{0,1},{1,0},{2,3},{3,2},{4,5},{5,4},{6,7},{7,6},{8,9},{9,8},{10,11... | collective-permute-start | bytes 4718600 | tf_op jit(solution)/shard_map/ppermute | solution.py:376
  218.2 68.0 %collective-permute-start.34 = (bf16[128,3072]{1,0:T(8,128)(2,1)}, bf16[128,3072]{1,0:T(8,128)(2,1)S(1)}, u32[]{:S(2)}, u32[]{:S(2)}) collective-permute-start(bf16[128,3072]{1,0:T(8,128)(2,1)} %table_part.10), channel_id=1, source_target_pairs={{0,121},{1,120},{2,123},{3,122},{4,125},{5,124},{6,127},{7,126},{8... | collective-permute-start | bytes 2359304 | tf_op jit(solution)/shard_map/ppermute | solution.py:379
  247.1 39.2 %collective-permute-start.33 = (bf16[384,1536]{1,0:T(8,128)(2,1)}, bf16[384,1536]{1,0:T(8,128)(2,1)}, u32[]{:S(2)}, u32[]{:S(2)}) collective-permute-start(bf16[384,1536]{1,0:T(8,128)(2,1)} %table_part.9), channel_id=1, source_target_pairs={{0,121},{1,120},{2,123},{3,122},{4,125},{5,124},{6,127},{7,126},{8... | collective-permute-start | bytes 3538952 | tf_op jit(solution)/shard_map/ppermute | solution.py:379
  259.7 25.9 %collective-permute-start.38 = (f32[8,768]{1,0:T(8,128)S(1)}, f32[8,768]{1,0:T(8,128)S(1)}, u32[]{:S(2)}, u32[]{:S(2)}) collective-permute-start(f32[8,768]{1,0:T(8,128)S(1)} %add.147), channel_id=1, source_target_pairs={{0,124},{1,125},{2,126},{3,127},{4,120},{5,121},{6,122},{7,123},{8... | collective-permute-start | bytes 73736 | tf_op jit(solution)/shard_map/ppermute | solution.py:521
  265.4 20.3 %collective-permute-start.37 = (f32[8,768]{1,0:T(8,128)S(1)}, f32[8,768]{1,0:T(8,128)S(1)}, u32[]{:S(2)}, u32[]{:S(2)}) collective-permute-start(f32[8,768]{1,0:T(8,128)S(1)} %add.147), channel_id=1, source_target_pairs={{0,120},{8,112},{16,104},{24,96},{32,88},{40,80},{48,72},{56,64},{... | collective-permute-start | bytes 73736 | tf_op jit(solution)/shard_map/ppermute | solution.py:521
  (48 other events, 558.5 us)

commit v3 on v2

--- a/solution.py
+++ b/solution.py
@@ -12,18 +12,17 @@
 epsilon = 1e-05
 F32 = jnp.float32
 BF16 = jnp.bfloat16
-BIG = 60 * 1024 * 1024
+BIG = 63 * 1024 * 1024
 
 RING, SIDES = 4, 2
 BLOCKS = RING * SIDES
 ROWS, COLUMNS = 128, 768
 PARTS = (
-    (0, 1, 0, 2),
-    (0, 1, 2, 2),
+    (0, 1, 3, 5),
     (1, 3, 0, 3),
     (1, 3, 3, 3),
     (1, 3, 6, 2),
-    (0, 1, 4, 4),
+    (0, 1, 0, 3),
 )
 
 
@@ -176,8 +175,8 @@
 
 def dlogits_kernel(rest, where, cot_ref, *refs):
     weights, sums = refs[:SIDES], refs[SIDES : SIDES + RING]
-    logits = refs[SIDES + RING : -4]
-    first_ref, other_ref, low_ref, loss_ref = refs[-4:]
+    logits = refs[SIDES + RING : -3]
+    low_t_ref, low_ref, loss_ref = refs[-3:]
     tokens = cot_ref.shape[1]
     for slot in range(BLOCKS):
         side, ahead = slot // RING, slot % RING
@@ -191,30 +190,47 @@
         loss = mixed / total - logtotal - rest
         group, at = where[slot]
         rel = logits[group][at] - logz
-        grads = cot_ref[slot : slot + 1] * jnp.exp(rel) * (rel - (rest + loss) + weights[side][ahead])
-        low = grads.astype(BF16)
+        grads = cot_ref[slot : slot + 1] * jnp.exp(rel) * (
+            rel - (rest + loss) + weights[side][ahead]
+        )
         here = slice(slot * tokens, (slot + 1) * tokens)
-        first_ref[:, here] = low[:ROWS]
-        other_ref[:, here] = low[ROWS:]
+        low_t_ref[:, here] = grads.astype(BF16)
         low_ref[here, :] = jnp.transpose(grads).astype(BF16)
         loss_ref[slot : slot + 1, :] = loss
 
 
-def all_dlogits(groups, found, weights, cot, sums, rest):
+def some_dlogits(lower, rows, groups, found, weights, cot, sums, rest):
     _, width, tokens = weights[0].shape
-    blocks = BLOCKS
     where = {s: (g, n) for g, group in enumerate(groups) for n, s in enumerate(group)}
+    step = math.gcd(lower, rows)
+    at = lower // step
+
+    def whole(x):
+        return pl.BlockSpec(x.shape, lambda i: (0,) * x.ndim)
+
+    def some(x):
+        return pl.BlockSpec((x.shape[0], step, tokens), lambda i: (0, i + at, 0))
+
     return pl.pallas_call(
         functools.partial(dlogits_kernel, rest, where),
+        grid=(rows // step,),
+        in_specs=[whole(cot)]
+        + [some(x) for x in weights]
+        + [whole(x) for x in sums]
+        + [some(x) for x in found],
+        out_specs=[
+            pl.BlockSpec((step, BLOCKS * tokens), lambda i: (i, 0)),
+            pl.BlockSpec((BLOCKS * tokens, step), lambda i: (0, i)),
+            pl.BlockSpec((BLOCKS, tokens), lambda i: (0, 0)),
+        ],
         out_shape=[
-            jax.ShapeDtypeStruct((ROWS, blocks * tokens), BF16),
-            jax.ShapeDtypeStruct((width - ROWS, blocks * tokens), BF16),
-            jax.ShapeDtypeStruct((blocks * tokens, width), BF16),
-            jax.ShapeDtypeStruct((blocks, tokens), F32),
-        ],
-        compiler_params=params(),
-        cost_estimate=cost(blocks * width * tokens * 10, blocks * width * tokens * 12),
-        name="all_dlogits",
+            jax.ShapeDtypeStruct((rows, BLOCKS * tokens), BF16),
+            jax.ShapeDtypeStruct((BLOCKS * tokens, rows), BF16),
+            jax.ShapeDtypeStruct((BLOCKS, tokens), F32),
+        ],
+        compiler_params=params(),
+        cost_estimate=cost(0, 0),
+        name="some_dlogits",
     )(cot, *weights, *sums, *found)
 
 
@@ -310,10 +326,12 @@
 def partial_kernel(counts, head_ref, *refs):
     flat = [c for group in counts for c in group]
     num = len(flat)
-    lows, rest, outs = refs[:num], refs[num : -len(counts)], refs[-len(counts) :]
-    low = jnp.concatenate([r[...] for r in lows], axis=0)
+    lows, rest, outs = refs[: 2 * num], refs[2 * num : -len(counts)], refs[-len(counts) :]
+    half = lows[0].shape[0]
+    low = jnp.concatenate(
+        [jnp.concatenate([r[...] for r in lows[n::num]], axis=1) for n in range(num)], axis=0
+    )
     sums = jnp.dot(low, head_ref[0], preferred_element_type=F32)
-    half = lows[0].shape[0]
     job, at = 0, 0
     for out, group in zip(outs, counts):
         for n, count in enumerate(group):
@@ -326,7 +344,7 @@
 
 def partials(low, head, groups, dtype=BF16):
     _, width, depth = head.shape
-    half = low.shape[0] // (2 * BLOCKS)
+    half = low[0].shape[0] // (2 * BLOCKS)
     step = 2048
     jobs = [job for group in groups for job in group]
     counts = [[len(add) for _, add in group] for group in groups]
@@ -335,7 +353,7 @@
         functools.partial(partial_kernel, counts),
         grid=(depth // step,),
         in_specs=[pl.BlockSpec((1, width, step), lambda i: (0, 0, i))]
-        + [pl.BlockSpec((half, width), lambda i, at=at: (at, 0)) for at, _ in jobs]
+        + [pl.BlockSpec((half, x.shape[1]), lambda i, at=at: (at, 0)) for x in low for at, _ in jobs]
         + [pl.BlockSpec((half, step), lambda i, row=row: (row, i)) for _, row in added],
         out_specs=[pl.BlockSpec((len(g) * half, step), lambda i: (0, i)) for g in groups],
         out_shape=[jax.ShapeDtypeStruct((len(g) * half, depth), dtype) for g in groups],
@@ -345,7 +363,74 @@
             width * depth * 2 + (len(jobs) + len(added)) * half * depth * 2,
         ),
         name="partials",
-    )(head, *([low] * len(jobs)), *[x for x, _ in added])
+    )(head, *[x for x in low for _ in jobs], *[x for x, _ in added])
+
+
+def join_kernel(counts, *refs):
+    given, outs = refs[: -len(counts)], refs[-len(counts) :]
+    sums, rest = given[: len(counts)], given[len(counts) :]
+    at = 0
+    for out, own, group in zip(outs, sums, counts):
+        half = out.shape[0] // len(group)
+        for n, count in enumerate(group):
+            here = slice(n * half, (n + 1) * half)
+            total = own[here, :].astype(F32)
+            for r in rest[at : at + count]:
+                total = total + r[...].astype(F32)
+            at += count
+            out[here, :] = total.astype(out.dtype)
+
+
+def join(own, groups):
+    rows, depth = own[0].shape
+    step = depth // 2
+    counts = [[len(add) for add in group] for group in groups]
+    added = [x for group in groups for add in group for x in add]
+    whole = pl.BlockSpec((rows, step), lambda i: (0, i))
+    return pl.pallas_call(
+        functools.partial(join_kernel, counts),
+        grid=(depth // step,),
+        in_specs=[whole] * len(own)
+        + [pl.BlockSpec((rows // 2, step), lambda i, row=row: (row, i)) for _, row in added],
+        out_specs=[whole] * len(own),
+        out_shape=[jax.ShapeDtypeStruct(x.shape, x.dtype) for x in own],
+        compiler_params=params(),
+        cost_estimate=cost(0, 0),
+        name="join",
+    )(*own, *[x for x, _ in added])
+
+
+def states_kernel(hidden_ref, scale_ref, gain_ref, *refs):
+    parts, out_ref = refs[:-1], refs[-1]
+    dnormed = parts[0][...].astype(F32)
+    for r in parts[1:]:
+        dnormed = dnormed + r[...].astype(F32)
+    scale = scale_ref[:, 0:1]
+    unit = hidden_ref[...].astype(F32) * scale
+    scaled = gain_ref[...] * dnormed
+    along = jnp.mean(unit * scaled, axis=1, keepdims=True)
+    out_ref[...] = (scale * scaled - scale * unit * along).astype(BF16)
+
+
+def states_gradient(hidden, scale, gain, parts):
+    rows, width = hidden.shape
+    step = rows // 4
+    block = pl.BlockSpec((step, width), lambda i: (i, 0))
+    return pl.pallas_call(
+        states_kernel,
+        grid=(rows // step,),
+        in_specs=[
+            block,
+            pl.BlockSpec((step, scale.shape[1]), lambda i: (i, 0)),
+            pl.BlockSpec((1, width), lambda i: (0, 0)),
+        ]
+        + [block] * len(parts),
+        out_specs=block,
+        out_shape=jax.ShapeDtypeStruct((rows, width), BF16),
+        compiler_params=params(),
+        cost_estimate=cost(0, 0),
+        name="states_gradient",
+    )(hidden, scale, gain, *parts)
 
 
 def ring_perm(step):
@@ -437,9 +522,12 @@
     pair = merge_sums([rows_of(sums), rows_of(other)])
     pair = jnp.concatenate(pair + (jnp.zeros((BLOCKS, 5, tokens), F32),), axis=1)
     ring_sums = [pair, send(pair, down), send(pair, across), send(pair, up)]
-    first, second, low, loss = all_dlogits(
-        groups, [f[0] for f in found], weights, cot, ring_sums, rest
-    )
+    given = (groups, [f[0] for f in found], weights, cot)
+    first, low_first, loss = some_dlogits(0, ROWS, *given, ring_sums, rest)
+    their_first = send(first, swap)
+    ring_sums = [gate((ring_sums[0],), first)] + ring_sums[1:]
+    second, low_second, _ = some_dlogits(ROWS, width - ROWS, *given, ring_sums, rest)
+    low = (low_first, low_second)
 
     pieces, facing_pieces = [], []
     for slot in range(BLOCKS):
@@ -447,71 +535,71 @@
         other_slot = (slot + RING) % BLOCKS
         facing_pieces += [a[other_slot], b[other_slot]]
 
-    their_first = send(first, swap)
-    o2a, o2b = partials(low, head, [[(12, [])], [(13, [])]])
+    def part_of(n, low_t):
+        _, _, column, num_columns = PARTS[n]
+        return table_part(low_t, facing_pieces, column * COLUMNS, num_columns * COLUMNS)
+
+    their_first, second_there = gate((their_first, second), second)
+    their_second = send(second_there, swap)
+    parts = [part_of(0, their_first)]
+    theirs = [exchange(parts[0])]
+    o2a, o2b = partials(gate(low, parts[0]), head, [[(12, [])], [(13, [])]])
     r_o2a, r_o2b = send(o2a, down), send(o2b, up)
-
-    def part_of(n, mine):
-        _, _, column, num_columns = PARTS[n]
-        return table_part(mine, facing_pieces, column * COLUMNS, num_columns * COLUMNS)
-
-    their_first, second_there = gate((their_first, second), o2a)
-    their_second = send(second_there, swap)
-    parts = [part_of(0, their_first), part_of(1, their_first)]
-    theirs = [exchange(parts[0]), exchange(parts[1])]
-    parts.append(part_of(2, their_second))
-
-    low, first, second, their_first, their_second = gate(
-        (low, first, second, their_first, their_second),
-        r_o2a, r_o2b, theirs[0], parts[2],
-    )
+    ahead = partials(
+        gate(low, o2a),
+        head,
+        [[(14, []), (4, [])], [(10, []), (5, [])], [(11, []), (15, [])]],
+    )
+    their_second = gate((their_second,), *ahead)
+    parts.append(part_of(1, their_second))
+
+    *low, first, second, their_first, their_second, a0, a1, a2 = gate(
+        (*low, first, second, their_first, their_second, *ahead),
+        r_o2a, r_o2b, theirs[0], parts[1],
+    )
+    theirs.append(exchange(parts[1]))
+    to_down, to_swap = join([a0, a2], [[[(r_o2a, 0)], []], [[(r_o2b, 0)], []]])
+    o3a_s2a, o1a_s2b, o1b_o3b = send(to_down, down), send(a1, up), send(to_swap, swap)
+    their_first, their_second = gate((their_first, their_second), to_down)
+    parts += [part_of(2, their_second), part_of(3, their_second), part_of(4, their_first)]
     theirs.append(exchange(parts[2]))
-    to_down, to_up, to_swap = partials(
-        low,
-        head,
+    ahead = partials(
+        gate(low, to_down), head, [[(6, []), (7, [])], [(2, []), (3, [])], [(8, []), (9, [])]]
+    )
+
+    *low, first, second, theirs[1], parts[3], parts[4], a0, a1, a2 = gate(
+        (*low, first, second, theirs[1], parts[3], parts[4], *ahead),
+        o3a_s2a, o1a_s2b, o1b_o3b,
+    )
+    theirs.append(exchange(parts[3]))
+    to_down, to_up, to_swap = join(
+        [a0, a1, a2],
         [
-            [(14, [(r_o2a, 0)]), (4, [])],
-            [(10, []), (5, [])],
-            [(11, [(r_o2b, 0)]), (15, [])],
-        ],
-    )
-    o3a_s2a, o1a_s2b, o1b_o3b = send(to_down, down), send(to_up, up), send(to_swap, swap)
-    their_first, their_second, first, second = gate(
-        (their_first, their_second, first, second), to_down
-    )
+            [[(o3a_s2a, 1)], [(o1b_o3b, 1)]],
+            [[], [(o1a_s2b, 1), (o1b_o3b, 0)]],
+            [[(o3a_s2a, 0), (o1a_s2b, 0)], []],
+        ],
+    )
+    s3, s1, o0 = send(to_down, down), send(to_up, up), send(to_swap, swap)
+    *low, first, second = gate((*low, first, second), to_down)
     own, along = own_table(first, second, head, gain, pieces)
     along = along[:1].reshape(8, depth // 8)
-    parts += [part_of(n, their_first if PARTS[n][0] == 0 else their_second) for n in (3, 4, 5)]
-
-    low, own, along, theirs[2], parts[3], parts[4], parts[5] = gate(
-        (low, own, along, theirs[2], *parts[3:]), o3a_s2a, o1a_s2b, o1b_o3b, theirs[1]
-    )
-    theirs.append(exchange(parts[3]))
-    along = along + send(along, swap)
-    to_down, to_up, to_swap = gate(
-        partials(
-            low,
-            head,
-            [
-                [(6, [(o3a_s2a, 1)]), (7, [(o1b_o3b, 1)])],
-                [(2, []), (3, [(o1a_s2b, 1), (o1b_o3b, 0)])],
-                [(8, [(o3a_s2a, 0), (o1a_s2b, 0)]), (9, [])],
-            ],
-        ),
-        along,
-    )
-    s3, s1, o0 = send(to_down, down), send(to_up, up), send(to_swap, swap)
+    (mine,) = partials(low, head, [[(0, []), (1, [])]])
     merged = None
     for n in range(2):
         merged = add_part(own, theirs[n], merged, PARTS[n])
+    parts[4] = gate((parts[4],), theirs[2], merged)
+    theirs.append(exchange(parts[4]))
     merged = add_part(own, theirs[2], merged, PARTS[2])
 
-    low, along, theirs[3], merged = gate((low, along, theirs[3], merged), s3, s1, o0)
-    theirs += [exchange(parts[4]), exchange(parts[5])]
+    mine, along, merged = gate((mine, along, merged), s3, s1, o0)
+    along = along + send(along, swap)
+    scale = jnp.concatenate([scale_a, scale_b], axis=0)
+    grad_states = states_gradient(hidden, scale, gain, [mine, s3, s1, o0])
+    merged = add_part(own, theirs[3], merged, PARTS[3])
+    along = gate((along,), grad_states)
     along = along + send(along, [(f, f ^ SIDES) for f in range(BLOCKS)])
-    (dnormed,) = partials(
-        low, head, [[(n, [(s3, n), (s1, n), (o0, n)]) for n in (0, 1)]], F32
-    )
+    along = gate((along,), merged)
     opposite = [
         (p * BLOCKS + f, (num_pipe - 1 - p) * BLOCKS + t)
         for p in range(num_pipe)
@@ -523,18 +611,8 @@
     )
     merged_gain = (ours.astype(F32) + mirrored.astype(BF16).astype(F32)).astype(BF16)
     merged_gain = merged_gain.reshape(1, depth)
-    scale = jnp.concatenate([scale_a, scale_b], axis=0)[:, :1]
-    unit = hidden.astype(F32) * scale
-    scaled = gain * dnormed
-    grad_states = scale * scaled - scale * unit * jnp.mean(unit * scaled, axis=1, keepdims=True)
-    grad_states = grad_states.astype(BF16)
-    merged = add_part(own, theirs[3], merged, PARTS[3])
-
-    theirs[4], theirs[5], merged = gate(
-        (theirs[4], theirs[5], merged), grad_states, merged_gain
-    )
-    for n in (4, 5):
-        merged = add_part(own, theirs[n], merged, PARTS[n])
+    theirs[4], merged = gate((theirs[4], merged), grad_states)
+    merged = add_part(own, theirs[4], merged, PARTS[4])
     return (loss[0], grad_states, merged, merged_gain)
 
 

time: 294 us -> 283 us (0.963)
  Pallas kernels: 138 us -> 156 us
  waiting for transfers between devices: 66.5 us -> 51.9 us
  other arithmetic: 11.3 us -> 1.98 us
  starting transfers between devices: 66.4 us -> 61.4 us
    pallas_call x1 -> x5, Pallas kernels: 4.31 us -> 21.8 us  [the longest x2 9.43 us: join(): pl.pallas_call(functools.partial(join_kernel, counts), grid=(depth // ste...]
    ppermute x1, waiting for transfers between devices: 11.2 us -> 0.01 us  [body(): lax.ppermute(along, ('pipe', 'fsdp'), opposite)]
    ppermute x31, waiting for transfers between devices: 55.2 us -> 44.5 us  [send(): return lax.ppermute(x, 'fsdp', perm)]
    ppermute x6 -> x5, waiting for transfers between devices: 0.02 us -> 7.41 us  [exchange(): return lax.ppermute(x, ('pipe', 'fsdp'), facing)]
    ppermute x6 -> x5, starting transfers between devices: 30.6 us -> 25.4 us  [exchange(): return lax.ppermute(x, ('pipe', 'fsdp'), facing)]
    pallas_call x1 -> x0, other arithmetic: 5.05 us -> none  [block_logits(): pl.pallas_call(functools.partial(logits_kernel, count), grid=(depth // st...]
    pallas_call x4 -> x5, Pallas kernels: 24.4 us -> 29.4 us  [block_logits(): pl.pallas_call(functools.partial(logits_kernel, count), grid=(depth // st...]
    pallas_call x4, Pallas kernels: 28.8 us -> 25.2 us  [partials(): pl.pallas_call(functools.partial(partial_kernel, counts), grid=(depth //...]
  transfers between devices with their start and end apart: 39 -> 38, of which waited for: 16 -> 21; matrix products, arithmetic and copies ran while one was open for 4% -> 2% of each run, Pallas kernels for 43% -> 50%
where the time goes in v3:
time: 283 us; the launch traced here: 281 us
  Pallas kernels  156 us (55%)
  starting transfers between devices  61.4 us (22%)
  waiting for transfers between devices  51.9 us (18%)
  local copies, waits for them, and re-layouts  9.27 us (3%)
    ppermute x31, waiting for transfers between devices, send(): return lax.ppermute(x, 'fsdp', perm)  44.5 us
    ppermute x31, starting transfers between devices, send(): return lax.ppermute(x, 'fsdp', perm)  29.7 us
    pallas_call x5, Pallas kernels, block_logits(): pl.pallas_call(functools.partial(logits_kernel, count), grid=(depth // st...  29.4 us
    pallas_call x5, Pallas kernels, table_part(): pl.pallas_call(part_kernel, grid=(size // step,), in_specs=[pl.BlockSpec(...  27.1 us
    ppermute x5, starting transfers between devices, exchange(): return lax.ppermute(x, ('pipe', 'fsdp'), facing)  25.4 us
    pallas_call x4, Pallas kernels, partials(): pl.pallas_call(functools.partial(partial_kernel, counts), grid=(depth //...  25.2 us
    pallas_call x5, Pallas kernels, add_part(): pl.pallas_call(add_kernel, grid=(num_rows, num_columns // wide), in_specs...  18.1 us
    pallas_call x2, Pallas kernels, teacher_weights(): pl.pallas_call(functools.partial(teacher_kernel, rest), grid_spec=pltpu.P...  15.3 us
  transfers between devices with their start and end apart: 38, of which 21 were waited for; matrix products, arithmetic and copies ran while one was open for 2% of the time, Pallas kernels for 50%

profile of v3, /device:TPU:1, one launch (start us, length us, event | category | flops | bytes accessed | tf_op | source)
XLA Modules:
  0.0 281.1 jit_solution(15678148933838695043)
XLA Ops:
  13.6 7.6 %teacher_weights.2.refs_2_.refs_6_.refs_7_.refs_4_.refs_0_ = f32[4,512,128]{2,1,0:T(8,128)} custom-call(s32[4]{0:T(128)} %bitcast.19, s32[1]{0:T(128)} %bitcast.2.base_ref, s32[64,1024]{1,0:T(8,128)} %bitcast.14, f32[64,1024]{1,0:T(8,128)} %bitcast.16), custom_call_target="tpu_custom_call" | custom-call | flops 1 | bytes 1 | tf_op jit(solution)/shard_map/teacher_weights/pallas_call | solution.py:91
  27.6 5.1 %block_logits.5 = (f32[1,512,128]{2,1,0:T(8,128)}, f32[1,8,128]{2,1,0:T(8,128)}) custom-call(bf16[1,512,6144]{2,1,0:T(8,128)(2,1)} %head_ref.19, bf16[64,6144]{1,0:T(8,128)(2,1)} %get-tuple-element.98.refs_0_.refs_8_, bf16[64,6144]{1,0:T(8,128)(2,1)} %get-tuple-element.101.refs_1_.refs_9_, f32[4,512,128]{2,1,0:T(8,128)} %teacher_weights.2.refs_2_.refs_6_.refs_7_.refs_4_.refs_0_), custom_call_target="tpu_custom_call" | custom-call | flops 1 | bytes 1 | tf_op jit(solution)/shard_map/block_logits/pallas_call | solution.py:146
  33.3 7.6 %teacher_weights.3.refs_8_.refs_2_.refs_5_.refs_1_ = f32[4,512,128]{2,1,0:T(8,128)} custom-call(s32[4]{0:T(128)} %slice.52.order_ref, s32[1]{0:T(128)} %bitcast.2.base_ref, s32[64,1024]{1,0:T(8,128)} %bitcast.15, f32[64,1024]{1,0:T(8,128)} %bitcast.17), custom_call_target="tpu_custom_call" | custom-call | flops 1 | bytes 1 | tf_op jit(solution)/shard_map/teacher_weights/pallas_call | solution.py:91
  46.0 8.1 %block_logits.6 = (f32[3,512,128]{2,1,0:T(8,128)}, f32[3,8,128]{2,1,0:T(8,128)}) custom-call(bf16[1,512,6144]{2,1,0:T(8,128)(2,1)} %head_ref.19, bf16[64,6144]{1,0:T(8,128)(2,1)} %collective-permute-done.refs_0_.refs_14_.refs_6_, bf16[64,6144]{1,0:T(8,128)(2,1)} %collective-permute-done.1.refs_1_.refs_15_.refs_7_, ...), custom_call_target="tpu_custom_call" | custom-call | flops 1 | bytes 1 | tf_op jit(solution)/shard_map/block_logits/pallas_call | solution.py:146
  63.7 5.1 %block_logits.7 = (f32[1,512,128]{2,1,0:T(8,128)}, f32[1,8,128]{2,1,0:T(8,128)}) custom-call(bf16[1,512,6144]{2,1,0:T(8,128)(2,1)} %head_ref.19, bf16[64,6144]{1,0:T(8,128)(2,1)} %collective-permute-done.10.refs_0_.refs_2_.refs_10_, bf16[64,6144]{1,0:T(8,128)(2,1)} %collective-permute-done.9.refs_1_.refs_3_.refs_11_, ...), custom_call_target="tpu_custom_call" | custom-call | flops 1 | bytes 1 | tf_op jit(solution)/shard_map/block_logits/pallas_call | solution.py:146
  68.9 7.5 %collective-permute-done.6.refs_0_.refs_12_.refs_4_ = bf16[64,6144]{1,0:T(8,128)(2,1)} collective-permute-done((bf16[64,6144]{1,0:T(8,128)(2,1)}, bf16[64,6144]{1,0:T(8,128)(2,1)}, u32[]{:S(2)}, u32[]{:S(2)}) %collective-permute-start.6) | collective-permute-done | bytes 786464 | tf_op jit(solution)/shard_map/ppermute | solution.py:461
  77.3 5.9 %block_logits.8 = (f32[2,512,128]{2,1,0:T(8,128)}, f32[2,8,128]{2,1,0:T(8,128)}) custom-call(bf16[1,512,6144]{2,1,0:T(8,128)(2,1)} %head_ref.19, bf16[64,6144]{1,0:T(8,128)(2,1)} %collective-permute-done.6.refs_0_.refs_12_.refs_4_, bf16[64,6144]{1,0:T(8,128)(2,1)} %collective-permute-done.7.refs_1_.refs_13_.refs_5_, ...), custom_call_target="tpu_custom_call" | custom-call | flops 1 | bytes 1 | tf_op jit(solution)/shard_map/block_logits/pallas_call | solution.py:146
  84.0 9.3 %collective-permute-done.12.refs_0_.refs_4_.refs_12_ = bf16[64,6144]{1,0:T(8,128)(2,1)} collective-permute-done((bf16[64,6144]{1,0:T(8,128)(2,1)}, bf16[64,6144]{1,0:T(8,128)(2,1)}, u32[]{:S(2)}, u32[]{:S(2)}) %collective-permute-start.12) | collective-permute-done | bytes 786464 | tf_op jit(solution)/shard_map/ppermute | solution.py:461
  93.3 5.1 %block_logits.9 = (f32[1,512,128]{2,1,0:T(8,128)}, f32[1,8,128]{2,1,0:T(8,128)}) custom-call(bf16[1,512,6144]{2,1,0:T(8,128)(2,1)} %head_ref.19, bf16[64,6144]{1,0:T(8,128)(2,1)} %collective-permute-done.12.refs_0_.refs_4_.refs_12_, bf16[64,6144]{1,0:T(8,128)(2,1)} %collective-permute-done.13.refs_1_.refs_5_.refs_13_, ...), custom_call_target="tpu_custom_call" | custom-call | flops 1 | bytes 1 | tf_op jit(solution)/shard_map/block_logits/pallas_call | solution.py:146
  116.0 6.5 %table_part.5 = bf16[128,3840]{1,0:T(8,128)(2,1)} custom-call(bf16[128,1024]{1,0:T(8,128)(2,1)} %copy-done.5, bf16[64,6144]{1,0:T(8,128)(2,1)} %copy-done.2, bf16[64,6144]{1,0:T(8,128)(2,1)} %collective-permute-done.5.refs_5_.refs_1_.refs_9_, bf16[64,6144]{1,0:T(8,128)(2,1)} %collective-permute-done.10.refs_0_.refs_2_.refs_10_, ...), custom_call_target="tpu_custom_call" | custom-call | flops 1 | bytes 1 | tf_op jit(solution)/shard_map/table_part/pallas_call | solution.py:247
  122.4 12.3 %collective-permute-start.22 = (bf16[128,3840]{1,0:T(8,128)(2,1)}, bf16[128,3840]{1,0:T(8,128)(2,1)}, u32[]{:S(2)}, u32[]{:S(2)}) collective-permute-start(bf16[128,3840]{1,0:T(8,128)(2,1)} %table_part.5), channel_id=1, source_target_pairs={{0,121},{1,120},{2,123},{3,122},{4,125},{5,124},{6,127},{7,126},{8... | collective-permute-start | bytes 2949128 | tf_op jit(solution)/shard_map/ppermute | solution.py:464
  135.1 5.3 %partials.4 = (bf16[64,6144]{1,0:T(8,128)(2,1)}, bf16[64,6144]{1,0:T(8,128)(2,1)}) custom-call(bf16[1,512,6144]{2,1,0:T(8,128)(2,1)} %head_ref.19, bf16[1024,128]{1,0:T(8,128)(2,1)} %get-tuple-element.169.refs_0_.refs_1_.refs_2_.refs_3_.refs_4_.refs_5_, bf16[1024,128]{1,0:T(8,128)(2,1)} %get-tuple-element.169.refs_0_.refs_1_.refs_2_.refs_3_.refs_4_.refs_5_, ...), custom_call_target="tpu_custom_call" | custom-call | flops 1 | bytes 1 | tf_op jit(solution)/shard_map/partials/pallas_call | solution.py:352
  143.1 7.2 %partials.5 = (bf16[128,6144]{1,0:T(8,128)(2,1)}, bf16[128,6144]{1,0:T(8,128)(2,1)}, bf16[128,6144]{1,0:T(8,128)(2,1)}) custom-call(bf16[1,512,6144]{2,1,0:T(8,128)(2,1)} %head_ref.19, bf16[1024,128]{1,0:T(8,128)(2,1)} %get-tuple-element.169.refs_0_.refs_1_.refs_2_.refs_3_.refs_4_.refs_5_, ...), custom_call_target="tpu_custom_call" | custom-call | flops 1 | bytes 1 | tf_op jit(solution)/shard_map/partials/pallas_call | solution.py:352
  151.4 5.8 %table_part.6 = bf16[384,2304]{1,0:T(8,128)(2,1)} custom-call(bf16[384,1024]{1,0:T(8,128)(2,1)} %copy-done.4, bf16[64,6144]{1,0:T(8,128)(2,1)} %copy-done.2, bf16[64,6144]{1,0:T(8,128)(2,1)} %collective-permute-done.5.refs_5_.refs_1_.refs_9_, bf16[64,6144]{1,0:T(8,128)(2,1)} %collective-permute-done.10.refs_0_.refs_2_.refs_10_, ...), custom_call_target="tpu_custom_call" | custom-call | flops 1 | bytes 1 | tf_op jit(solution)/shard_map/table_part/pallas_call | solution.py:247
  157.2 4.4 %collective-permute-start.23 = (bf16[384,2304]{1,0:T(8,128)(2,1)}, bf16[384,2304]{1,0:T(8,128)(2,1)}, u32[]{:S(2)}, u32[]{:S(2)}) collective-permute-start(bf16[384,2304]{1,0:T(8,128)(2,1)} %table_part.6), channel_id=1, source_target_pairs={{0,121},{1,120},{2,123},{3,122},{4,125},{5,124},{6,127},{7,126},{8... | collective-permute-start | bytes 5308424 | tf_op jit(solution)/shard_map/ppermute | solution.py:464
  168.1 5.9 %table_part.9 = bf16[384,2304]{1,0:T(8,128)(2,1)} custom-call(bf16[384,1024]{1,0:T(8,128)(2,1)} %copy-done.4, bf16[64,6144]{1,0:T(8,128)(2,1)} %copy-done.2, bf16[64,6144]{1,0:T(8,128)(2,1)} %collective-permute-done.5.refs_5_.refs_1_.refs_9_, bf16[64,6144]{1,0:T(8,128)(2,1)} %collective-permute-done.10.refs_0_.refs_2_.refs_10_, ...), custom_call_target="tpu_custom_call" | custom-call | flops 1 | bytes 1 | tf_op jit(solution)/shard_map/table_part/pallas_call | solution.py:247
  176.4 7.2 %partials.6 = (bf16[128,6144]{1,0:T(8,128)(2,1)}, bf16[128,6144]{1,0:T(8,128)(2,1)}, bf16[128,6144]{1,0:T(8,128)(2,1)}) custom-call(bf16[1,512,6144]{2,1,0:T(8,128)(2,1)} %head_ref.19, bf16[1024,128]{1,0:T(8,128)(2,1)} %get-tuple-element.169.refs_0_.refs_1_.refs_2_.refs_3_.refs_4_.refs_5_, ...), custom_call_target="tpu_custom_call" | custom-call | flops 1 | bytes 1 | tf_op jit(solution)/shard_map/partials/pallas_call | solution.py:352
  183.6 4.3 %table_part.7 = bf16[384,1536]{1,0:T(8,128)(2,1)} custom-call(bf16[384,1024]{1,0:T(8,128)(2,1)} %copy-done.4, bf16[64,6144]{1,0:T(8,128)(2,1)} %copy-done.2, bf16[64,6144]{1,0:T(8,128)(2,1)} %collective-permute-done.5.refs_5_.refs_1_.refs_9_, bf16[64,6144]{1,0:T(8,128)(2,1)} %collective-permute-done.10.refs_0_.refs_2_.refs_10_, ...), custom_call_target="tpu_custom_call" | custom-call | flops 1 | bytes 1 | tf_op jit(solution)/shard_map/table_part/pallas_call | solution.py:247
  187.9 4.7 %table_part.8 = bf16[128,2304]{1,0:T(8,128)(2,1)} custom-call(bf16[128,1024]{1,0:T(8,128)(2,1)} %copy-done.5, bf16[64,6144]{1,0:T(8,128)(2,1)} %copy-done.2, bf16[64,6144]{1,0:T(8,128)(2,1)} %collective-permute-done.5.refs_5_.refs_1_.refs_9_, bf16[64,6144]{1,0:T(8,128)(2,1)} %collective-permute-done.10.refs_0_.refs_2_.refs_10_, ...), custom_call_target="tpu_custom_call" | custom-call | flops 1 | bytes 1 | tf_op jit(solution)/shard_map/table_part/pallas_call | solution.py:247
  192.5 7.0 %collective-permute-done.25.refs_5_.refs_8_ = bf16[128,6144]{1,0:T(8,128)(2,1)} collective-permute-done((bf16[128,6144]{1,0:T(8,128)(2,1)}, bf16[128,6144]{1,0:T(8,128)(2,1)}, u32[]{:S(2)}, u32[]{:S(2)}) %collective-permute-start.25) | collective-permute-done | bytes 1572896 | tf_op jit(solution)/shard_map/ppermute | solution.py:461
  203.2 5.8 %join.3 = (bf16[128,6144]{1,0:T(8,128)(2,1)}, bf16[128,6144]{1,0:T(8,128)(2,1)}, bf16[128,6144]{1,0:T(8,128)(2,1)}) custom-call(bf16[128,6144]{1,0:T(8,128)(2,1)} %get-tuple-element.165.refs_0_, bf16[128,6144]{1,0:T(8,128)(2,1)} %get-tuple-element.166.refs_1_, bf16[128,6144]{1,0:T(8,128)(2,1)} %get-tuple-element.167.refs_2_, ...), custom_call_target="tpu_custom_call" | custom-call | flops 1 | bytes 1 | tf_op jit(solution)/shard_map/join/pallas_call | solution.py:390
  215.1 14.4 %own_table.1 = (bf16[512,6144]{1,0:T(8,128)(2,1)}, f32[8,6144]{1,0:T(8,128)}) custom-call(bf16[128,1024]{1,0:T(8,128)(2,1)} %get-tuple-element.171.first_ref, bf16[384,1024]{1,0:T(8,128)(2,1)} %get-tuple-element.172.other_ref, bf16[1,512,6144]{2,1,0:T(8,128)(2,1)} %head_ref.19, f32[1,6144]{1,0:T(1,128)} %gain_ref.7, ...), custom_call_target="tpu_custom_call" | custom-call | flops 1 | bytes 1 | tf_op jit(solution)/shard_map/own_table/pallas_call | solution.py:275
  244.0 5.4 %partials.7.refs_0_ = bf16[128,6144]{1,0:T(8,128)(2,1)} custom-call(bf16[1,512,6144]{2,1,0:T(8,128)(2,1)} %head_ref.19, bf16[1024,128]{1,0:T(8,128)(2,1)} %get-tuple-element.169.refs_0_.refs_1_.refs_2_.refs_3_.refs_4_.refs_5_, bf16[1024,128]{1,0:T(8,128)(2,1)} %get-tuple-element.169.refs_0_.refs_1_.refs_2_.refs_3_.refs_4_.refs_5_, ...), custom_call_target="tpu_custom_call" | custom-call | flops 1 | bytes 1 | tf_op jit(solution)/shard_map/partials/pallas_call | solution.py:352
  255.4 6.0 %states_gradient.1 = bf16[128,6144]{1,0:T(8,128)(2,1)} custom-call(bf16[128,6144]{1,0:T(8,128)(2,1)} %hidden_ref.5, f32[128,128]{1,0:T(8,128)} %pad_maximum_fusion.scale_ref, f32[1,6144]{1,0:T(1,128)} %gain_ref.7, bf16[128,6144]{1,0:T(8,128)(2,1)} %partials.7.refs_0_, bf16[128,6144]{1,0:T(8,128)(2,1)} %collective-permute-done.28.refs_1_, ...), custom_call_target="tpu_custom_call" | custom-call | flops 1 | bytes 1 | tf_op jit(solution)/shard_map/states_gradient/pallas_call | solution.py:419
  (145 shorter events, 116.5 us)
Async XLA Ops:
  2.9 20.0 %collective-permute-start.4 = (bf16[64,6144]{1,0:T(8,128)(2,1)}, bf16[64,6144]{1,0:T(8,128)(2,1)S(1)}, u32[]{:S(2)}, u32[]{:S(2)}) collective-permute-start(bf16[64,6144]{1,0:T(8,128)(2,1)} %get-tuple-element.98.refs_0_.refs_8_), channel_id=1, source_target_pairs={{0,1},{1,0},{2,3},{3,2},{4,5},{5,4},{6,7},{7,6},{8,9},{9,8},{10,11... | collective-permute-start | bytes 2359304 | tf_op jit(solution)/shard_map/ppermute | solution.py:461
  5.4 18.9 %collective-permute-start.2 = (bf16[64,6144]{1,0:T(8,128)(2,1)}, bf16[64,6144]{1,0:T(8,128)(2,1)}, u32[]{:S(2)}, u32[]{:S(2)}) collective-permute-start(bf16[64,6144]{1,0:T(8,128)(2,1)} %get-tuple-element.98.refs_0_.refs_8_), channel_id=1, source_target_pairs={{0,6},{1,7},{2,0},{3,1},{4,2},{5,3},{6,4},{7,5},{8,14},{9,15},{10,... | collective-permute-start | bytes 2359304 | tf_op jit(solution)/shard_map/ppermute | solution.py:461
  8.1 19.3 %collective-permute-start = (bf16[64,6144]{1,0:T(8,128)(2,1)}, bf16[64,6144]{1,0:T(8,128)(2,1)}, u32[]{:S(2)}, u32[]{:S(2)}) collective-permute-start(bf16[64,6144]{1,0:T(8,128)(2,1)} %get-tuple-element.98.refs_0_.refs_8_), channel_id=1, source_target_pairs={{0,2},{1,3},{2,4},{3,5},{4,6},{5,7},{6,0},{7,1},{8,10},{9,11},{10,... | collective-permute-start | bytes 2359304 | tf_op jit(solution)/shard_map/ppermute | solution.py:461
  10.4 32.1 %collective-permute-start.3 = (bf16[64,6144]{1,0:T(8,128)(2,1)}, bf16[64,6144]{1,0:T(8,128)(2,1)}, u32[]{:S(2)}, u32[]{:S(2)}) collective-permute-start(bf16[64,6144]{1,0:T(8,128)(2,1)} %get-tuple-element.101.refs_1_.refs_9_), channel_id=1, source_target_pairs={{0,6},{1,7},{2,0},{3,1},{4,2},{5,3},{6,4},{7,5},{8,14},{9,15},{10,... | collective-permute-start | bytes 2359304 | tf_op jit(solution)/shard_map/ppermute | solution.py:461
  13.1 31.3 %collective-permute-start.1 = (bf16[64,6144]{1,0:T(8,128)(2,1)}, bf16[64,6144]{1,0:T(8,128)(2,1)}, u32[]{:S(2)}, u32[]{:S(2)}) collective-permute-start(bf16[64,6144]{1,0:T(8,128)(2,1)} %get-tuple-element.101.refs_1_.refs_9_), channel_id=1, source_target_pairs={{0,2},{1,3},{2,4},{3,5},{4,6},{5,7},{6,0},{7,1},{8,10},{9,11},{10,... | collective-permute-start | bytes 2359304 | tf_op jit(solution)/shard_map/ppermute | solution.py:461
  27.5 16.9 %collective-permute-start.5 = (bf16[64,6144]{1,0:T(8,128)(2,1)}, bf16[64,6144]{1,0:T(8,128)(2,1)}, u32[]{:S(2)}, u32[]{:S(2)}) collective-permute-start(bf16[64,6144]{1,0:T(8,128)(2,1)} %get-tuple-element.101.refs_1_.refs_9_), channel_id=1, source_target_pairs={{0,1},{1,0},{2,3},{3,2},{4,5},{5,4},{6,7},{7,6},{8,9},{9,8},{10,11... | collective-permute-start | bytes 2359304 | tf_op jit(solution)/shard_map/ppermute | solution.py:461
  41.3 18.3 %collective-permute-start.8 = (bf16[64,6144]{1,0:T(8,128)(2,1)S(1)}, bf16[64,6144]{1,0:T(8,128)(2,1)}, u32[]{:S(2)}, u32[]{:S(2)}) collective-permute-start(bf16[64,6144]{1,0:T(8,128)(2,1)S(1)} %collective-permute-done.4.refs_4_.refs_0_.refs_8_), channel_id=1, source_target_pairs={{0,2},{1,3},{2,4},{3,5},{4,6},{5,7},{6,0},{7,1},{8,10},{9,11},{10,... | collective-permute-start | bytes 2359304 | tf_op jit(solution)/shard_map/ppermute | solution.py:461
  44.5 31.9 %collective-permute-start.7 = (bf16[64,6144]{1,0:T(8,128)(2,1)}, bf16[64,6144]{1,0:T(8,128)(2,1)}, u32[]{:S(2)}, u32[]{:S(2)}) collective-permute-start(bf16[64,6144]{1,0:T(8,128)(2,1)} %collective-permute-done.3.refs_3_.refs_11_), channel_id=1, source_target_pairs={{0,6},{1,7},{2,0},{3,1},{4,2},{5,3},{6,4},{7,5},{8,14},{9,15},{10,... | collective-permute-start | bytes 2359304 | tf_op jit(solution)/shard_map/ppermute | solution.py:461
  45.3 31.1 %collective-permute-start.6 = (bf16[64,6144]{1,0:T(8,128)(2,1)}, bf16[64,6144]{1,0:T(8,128)(2,1)}, u32[]{:S(2)}, u32[]{:S(2)}) collective-permute-start(bf16[64,6144]{1,0:T(8,128)(2,1)} %collective-permute-done.refs_0_.refs_14_.refs_6_), channel_id=1, source_target_pairs={{0,2},{1,3},{2,4},{3,5},{4,6},{5,7},{6,0},{7,1},{8,10},{9,11},{10,... | collective-permute-start | bytes 2359304 | tf_op jit(solution)/shard_map/ppermute | solution.py:461
  60.3 33.0 %collective-permute-start.12 = (bf16[64,6144]{1,0:T(8,128)(2,1)}, bf16[64,6144]{1,0:T(8,128)(2,1)}, u32[]{:S(2)}, u32[]{:S(2)}) collective-permute-start(bf16[64,6144]{1,0:T(8,128)(2,1)} %collective-permute-done.8.refs_2_.refs_6_.refs_14_), channel_id=1, source_target_pairs={{0,2},{1,3},{2,4},{3,5},{4,6},{5,7},{6,0},{7,1},{8,10},{9,11},{10,... | collective-permute-start | bytes 2359304 | tf_op jit(solution)/shard_map/ppermute | solution.py:461
  60.4 32.9 %collective-permute-start.13 = (bf16[64,6144]{1,0:T(8,128)(2,1)}, bf16[64,6144]{1,0:T(8,128)(2,1)}, u32[]{:S(2)}, u32[]{:S(2)}) collective-permute-start(bf16[64,6144]{1,0:T(8,128)(2,1)} %collective-permute-done.9.refs_1_.refs_3_.refs_11_), channel_id=1, source_target_pairs={{0,6},{1,7},{2,0},{3,1},{4,2},{5,3},{6,4},{7,5},{8,14},{9,15},{10,... | collective-permute-start | bytes 2359304 | tf_op jit(solution)/shard_map/ppermute | solution.py:461
  122.4 39.1 %collective-permute-start.22 = (bf16[128,3840]{1,0:T(8,128)(2,1)}, bf16[128,3840]{1,0:T(8,128)(2,1)}, u32[]{:S(2)}, u32[]{:S(2)}) collective-permute-start(bf16[128,3840]{1,0:T(8,128)(2,1)} %table_part.5), channel_id=1, source_target_pairs={{0,121},{1,120},{2,123},{3,122},{4,125},{5,124},{6,127},{7,126},{8... | collective-permute-start | bytes 2949128 | tf_op jit(solution)/shard_map/ppermute | solution.py:464
  140.4 21.2 %collective-permute-start.21 = (bf16[64,6144]{1,0:T(8,128)(2,1)}, bf16[64,6144]{1,0:T(8,128)(2,1)}, u32[]{:S(2)}, u32[]{:S(2)}) collective-permute-start(bf16[64,6144]{1,0:T(8,128)(2,1)} %get-tuple-element.142), channel_id=1, source_target_pairs={{0,2},{1,3},{2,4},{3,5},{4,6},{5,7},{6,0},{7,1},{8,10},{9,11},{10,... | collective-permute-start | bytes 2359304 | tf_op jit(solution)/shard_map/ppermute | solution.py:461
  141.8 19.8 %collective-permute-start.20 = (bf16[64,6144]{1,0:T(8,128)(2,1)}, bf16[64,6144]{1,0:T(8,128)(2,1)}, u32[]{:S(2)}, u32[]{:S(2)}) collective-permute-start(bf16[64,6144]{1,0:T(8,128)(2,1)} %get-tuple-element.135), channel_id=1, source_target_pairs={{0,6},{1,7},{2,0},{3,1},{4,2},{5,3},{6,4},{7,5},{8,14},{9,15},{10,... | collective-permute-start | bytes 2359304 | tf_op jit(solution)/shard_map/ppermute | solution.py:461
  157.2 45.0 %collective-permute-start.23 = (bf16[384,2304]{1,0:T(8,128)(2,1)}, bf16[384,2304]{1,0:T(8,128)(2,1)}, u32[]{:S(2)}, u32[]{:S(2)}) collective-permute-start(bf16[384,2304]{1,0:T(8,128)(2,1)} %table_part.6), channel_id=1, source_target_pairs={{0,121},{1,120},{2,123},{3,122},{4,125},{5,124},{6,127},{7,126},{8... | collective-permute-start | bytes 5308424 | tf_op jit(solution)/shard_map/ppermute | solution.py:464
  161.6 38.0 %collective-permute-start.25 = (bf16[128,6144]{1,0:T(8,128)(2,1)}, bf16[128,6144]{1,0:T(8,128)(2,1)}, u32[]{:S(2)}, u32[]{:S(2)}) collective-permute-start(bf16[128,6144]{1,0:T(8,128)(2,1)} %get-tuple-element.159), channel_id=1, source_target_pairs={{0,2},{1,3},{2,4},{3,5},{4,6},{5,7},{6,0},{7,1},{8,10},{9,11},{10,... | collective-permute-start | bytes 4718600 | tf_op jit(solution)/shard_map/ppermute | solution.py:461
  166.7 36.4 %collective-permute-start.26 = (bf16[128,6144]{1,0:T(8,128)(2,1)}, bf16[128,6144]{1,0:T(8,128)(2,1)}, u32[]{:S(2)}, u32[]{:S(2)}) collective-permute-start(bf16[128,6144]{1,0:T(8,128)(2,1)} %get-tuple-element.160), channel_id=1, source_target_pairs={{0,1},{1,0},{2,3},{3,2},{4,5},{5,4},{6,7},{7,6},{8,9},{9,8},{10,11... | collective-permute-start | bytes 4718600 | tf_op jit(solution)/shard_map/ppermute | solution.py:461
  166.7 36.5 %collective-permute-start.24 = (bf16[128,6144]{1,0:T(8,128)(2,1)}, bf16[128,6144]{1,0:T(8,128)(2,1)}, u32[]{:S(2)}, u32[]{:S(2)}) collective-permute-start(bf16[128,6144]{1,0:T(8,128)(2,1)} %get-tuple-element.151), channel_id=1, source_target_pairs={{0,6},{1,7},{2,0},{3,1},{4,2},{5,3},{6,4},{7,5},{8,14},{9,15},{10,... | collective-permute-start | bytes 4718600 | tf_op jit(solution)/shard_map/ppermute | solution.py:461
  174.0 66.1 %collective-permute-start.27 = (bf16[384,2304]{1,0:T(8,128)(2,1)}, bf16[384,2304]{1,0:T(8,128)(2,1)}, u32[]{:S(2)}, u32[]{:S(2)}) collective-permute-start(bf16[384,2304]{1,0:T(8,128)(2,1)} %table_part.9), channel_id=1, source_target_pairs={{0,121},{1,120},{2,123},{3,122},{4,125},{5,124},{6,127},{7,126},{8... | collective-permute-start | bytes 5308424 | tf_op jit(solution)/shard_map/ppermute | solution.py:464
  209.0 45.6 %collective-permute-start.29 = (bf16[128,6144]{1,0:T(8,128)(2,1)}, bf16[128,6144]{1,0:T(8,128)(2,1)}, u32[]{:S(2)}, u32[]{:S(2)}) collective-permute-start(bf16[128,6144]{1,0:T(8,128)(2,1)} %get-tuple-element.176), channel_id=1, source_target_pairs={{0,2},{1,3},{2,4},{3,5},{4,6},{5,7},{6,0},{7,1},{8,10},{9,11},{10,... | collective-permute-start | bytes 4718600 | tf_op jit(solution)/shard_map/ppermute | solution.py:461
  209.4 45.2 %collective-permute-start.30 = (bf16[128,6144]{1,0:T(8,128)(2,1)}, bf16[128,6144]{1,0:T(8,128)(2,1)}, u32[]{:S(2)}, u32[]{:S(2)}) collective-permute-start(bf16[128,6144]{1,0:T(8,128)(2,1)} %get-tuple-element.177), channel_id=1, source_target_pairs={{0,1},{1,0},{2,3},{3,2},{4,5},{5,4},{6,7},{7,6},{8,9},{9,8},{10,11... | collective-permute-start | bytes 4718600 | tf_op jit(solution)/shard_map/ppermute | solution.py:461
  210.5 44.1 %collective-permute-start.28 = (bf16[128,6144]{1,0:T(8,128)(2,1)}, bf16[128,6144]{1,0:T(8,128)(2,1)}, u32[]{:S(2)}, u32[]{:S(2)}) collective-permute-start(bf16[128,6144]{1,0:T(8,128)(2,1)} %get-tuple-element.168), channel_id=1, source_target_pairs={{0,6},{1,7},{2,0},{3,1},{4,2},{5,3},{6,4},{7,5},{8,14},{9,15},{10,... | collective-permute-start | bytes 4718600 | tf_op jit(solution)/shard_map/ppermute | solution.py:461
  212.8 52.6 %collective-permute-start.32 = (bf16[384,1536]{1,0:T(8,128)(2,1)}, bf16[384,1536]{1,0:T(8,128)(2,1)}, u32[]{:S(2)}, u32[]{:S(2)}) collective-permute-start(bf16[384,1536]{1,0:T(8,128)(2,1)} %table_part.7), channel_id=1, source_target_pairs={{0,121},{1,120},{2,123},{3,122},{4,125},{5,124},{6,127},{7,126},{8... | collective-permute-start | bytes 3538952 | tf_op jit(solution)/shard_map/ppermute | solution.py:464
  240.1 38.1 %collective-permute-start.31 = (bf16[128,2304]{1,0:T(8,128)(2,1)S(1)}, bf16[128,2304]{1,0:T(8,128)(2,1)}, u32[]{:S(2)}, u32[]{:S(2)}) collective-permute-start(bf16[128,2304]{1,0:T(8,128)(2,1)S(1)} %copy-done.6), channel_id=1, source_target_pairs={{0,121},{1,120},{2,123},{3,122},{4,125},{5,124},{6,127},{7,126},{8... | collective-permute-start | bytes 1769480 | tf_op jit(solution)/shard_map/ppermute | solution.py:464
  (32 other events, 322.4 us)

commit v4 on v3

--- a/solution.py
+++ b/solution.py
@@ -103,9 +103,10 @@
     )(order, base, index, logits)
 
 
-def logits_kernel(count, head_ref, *refs):
-    pieces, weights = refs[: 2 * count], refs[2 * count : 3 * count]
-    logits_ref, sums_ref = refs[3 * count :]
+def logits_kernel(slots, earlier, head_ref, *refs):
+    count = len(slots)
+    pieces, weights, before = refs[: 2 * count], refs[2 * count : 3 * count], refs[3 * count : -2]
+    logits_ref, sums_ref = refs[-2:]
     step = pl.program_id(0)
     block = jnp.concatenate([p[...] for p in pieces], axis=0)
     part = lax.dot_general(
@@ -132,35 +133,40 @@
             expo = jnp.exp(shifted)
             total = jnp.sum(expo, axis=0, keepdims=True)
             mixed = jnp.sum(expo * (shifted + weights[n][0]), axis=0, keepdims=True)
-            sums_ref[n] = jnp.concatenate(
-                [top, total, mixed, jnp.zeros((5, top.shape[1]), F32)], axis=0
-            )
-
-
-def block_logits(slots, a, b, head, weights):
+            for at, value in enumerate((top, total, mixed)):
+                row = at * BLOCKS + slots[n]
+                sums_ref[row : row + 1, :] = value
+        for group, ref in zip(earlier, before):
+            for slot in group:
+                for row in range(slot, 3 * BLOCKS, BLOCKS):
+                    sums_ref[row : row + 1, :] = ref[row : row + 1, :]
+
+
+def block_logits(slots, a, b, head, weights, earlier=(), before=()):
     _, width, depth = head.shape
     half = a[slots[0]].shape[0]
     tokens = 2 * half
     count = len(slots)
     step = 3072
     return pl.pallas_call(
-        functools.partial(logits_kernel, count),
+        functools.partial(logits_kernel, slots, earlier),
         grid=(depth // step,),
         in_specs=[pl.BlockSpec((1, width, step), lambda i: (0, 0, i))]
         + [pl.BlockSpec((half, step), lambda i: (0, i))] * (2 * count)
-        + [pl.BlockSpec((1, width, tokens), lambda i, s=s: (s % RING, 0, 0)) for s in slots],
+        + [pl.BlockSpec((1, width, tokens), lambda i, s=s: (s % RING, 0, 0)) for s in slots]
+        + [pl.BlockSpec((3 * BLOCKS, tokens), lambda i: (0, 0))] * len(before),
         out_specs=[
             pl.BlockSpec((count, width, tokens), lambda i: (0, 0, 0)),
-            pl.BlockSpec((count, 8, tokens), lambda i: (0, 0, 0)),
+            pl.BlockSpec((3 * BLOCKS, tokens), lambda i: (0, 0)),
         ],
         out_shape=[
             jax.ShapeDtypeStruct((count, width, tokens), F32),
-            jax.ShapeDtypeStruct((count, 8, tokens), F32),
+            jax.ShapeDtypeStruct((3 * BLOCKS, tokens), F32),
         ],
         compiler_params=params(),
         cost_estimate=cost(2 * count * tokens * width * depth, width * depth * 2),
         name="block_logits",
-    )(head, *[x[s] for s in slots for x in (a, b)], *[weights[s // RING] for s in slots])
+    )(head, *[x[s] for s in slots for x in (a, b)], *[weights[s // RING] for s in slots], *before)
 
 
 def merge_sums(parts):
@@ -178,16 +184,23 @@
     logits = refs[SIDES + RING : -3]
     low_t_ref, low_ref, loss_ref = refs[-3:]
     tokens = cot_ref.shape[1]
+    parts = []
+    for shift in range(RING):
+        found = []
+        for lower in range(0, 3 * BLOCKS, RING):
+            if shift:
+                found.append(sums[shift][lower + RING - shift : lower + RING, :])
+            found.append(sums[shift][lower : lower + RING - shift, :])
+        found = jnp.concatenate(found, axis=0)
+        parts.append([found[n * BLOCKS : (n + 1) * BLOCKS] for n in range(3)])
+    top, total, mixed = merge_sums(parts)
+    logtotals = jnp.log(total)
+    logzs = top + logtotals
+    losses = mixed / total - logtotals - rest
+    loss_ref[...] = losses
     for slot in range(BLOCKS):
         side, ahead = slot // RING, slot % RING
-        parts = []
-        for shift in range(RING):
-            found = sums[shift][side * RING + (ahead + RING - shift) % RING]
-            parts.append((found[0:1], found[1:2], found[2:3]))
-        top, total, mixed = merge_sums(parts)
-        logtotal = jnp.log(total)
-        logz = top + logtotal
-        loss = mixed / total - logtotal - rest
+        logz, loss = logzs[slot : slot + 1], losses[slot : slot + 1]
         group, at = where[slot]
         rel = logits[group][at] - logz
         grads = cot_ref[slot : slot + 1] * jnp.exp(rel) * (
@@ -196,7 +209,6 @@
         here = slice(slot * tokens, (slot + 1) * tokens)
         low_t_ref[:, here] = grads.astype(BF16)
         low_ref[here, :] = jnp.transpose(grads).astype(BF16)
-        loss_ref[slot : slot + 1, :] = loss
 
 
 def some_dlogits(lower, rows, groups, found, weights, cot, sums, rest):
@@ -488,14 +500,14 @@
     cot = jnp.take(cotangent.reshape(BLOCKS, tokens), order, axis=0)
 
     groups = ((0,), (3, 1, 4), (5,), (2, 7), (6,))
-    b0, a4 = gate((b[0], a[4]), a[3], a[1], weights[0])
+    b0, a[4] = gate((b[0], a[4]), a[3], a[1], weights[0])
     b[4] = send(b0, swap)
+    found = [block_logits(groups[0], a, b, head, weights)]
+    a4, order, base = gate((a[4], order, base), found[0][1])
     a[7] = send(a4, up)
     a[5] = send(a4, down)
-    order, base = gate((order, base), weights[0])
     weights.append(teacher_weights(order[RING:], base, index_t, logits_t, width, rest))
-    found = [block_logits(groups[0], a, b, head, weights)]
-    a3, b1, b[4] = gate((a[3], b[1], b[4]), b[3], weights[1], found[0][1])
+    a3, b1, b[4] = gate((a[3], b[1], b[4]), b[3])
     a[2] = send(a3, up)
     b[2] = send(b1, down)
     b[5] = send(b1, swap)
@@ -508,19 +520,15 @@
     a[2], b[2], b[7] = gate((a[2], b[2], b[7]), found[2][1])
     found.append(block_logits(groups[3], a, b, head, weights))
     a[6], b[6] = gate((a[6], b[6]), found[3][1])
-    found.append(block_logits(groups[4], a, b, head, weights))
-
-    at = [s for group in groups for s in group]
-    sums = jnp.concatenate([f[1] for f in found], axis=0)
-    sums = jnp.stack([sums[at.index(s)] for s in range(BLOCKS)])
-
-    def rows_of(x):
-        return x[:, 0:1], x[:, 1:2], x[:, 2:3]
-
-    other = send(sums, swap)
-    other = jnp.concatenate([other[RING:], other[:RING]], axis=0)
-    pair = merge_sums([rows_of(sums), rows_of(other)])
-    pair = jnp.concatenate(pair + (jnp.zeros((BLOCKS, 5, tokens), F32),), axis=1)
+    found.append(
+        block_logits(groups[4], a, b, head, weights, groups[:4], [f[1] for f in found])
+    )
+    sums = found[-1][1]
+    other = send(sums, swap).reshape(3, SIDES, RING, tokens)[:, ::-1].reshape(sums.shape)
+    pair = jnp.concatenate(
+        merge_sums([[x[n : n + BLOCKS] for n in range(0, 3 * BLOCKS, BLOCKS)] for x in (sums, other)]),
+        axis=0,
+    )
     ring_sums = [pair, send(pair, down), send(pair, across), send(pair, up)]
     given = (groups, [f[0] for f in found], weights, cot)
     first, low_first, loss = some_dlogits(0, ROWS, *given, ring_sums, rest)

time: 283 us -> 281 us (level)
  starting transfers between devices: 61.4 us -> 66 us
  waiting for transfers between devices: 51.9 us -> 48.3 us
  local copies, waits for them, and re-layouts: 9.27 us -> 6.2 us
    ppermute x31, waiting for transfers between devices: 44.5 us -> 38.1 us  [send(): return lax.ppermute(x, 'fsdp', perm)]
    ppermute x31, starting transfers between devices: 29.7 us -> 35.7 us  [send(): return lax.ppermute(x, 'fsdp', perm)]
    unnamed x44 -> x29, local copies, waits for them, and re-layouts: 5.87 us -> 2.87 us
  transfers between devices with their start and end apart: 38 -> 38, of which waited for: 21 -> 16; matrix products, arithmetic and copies ran while one was open for 2% -> 2% of each run, Pallas kernels for 50% -> 50%
where the time goes in v4:
time: 281 us; the launch traced here: 280 us
  Pallas kernels  156 us (56%)
  starting transfers between devices  66 us (23%)
  waiting for transfers between devices  48.3 us (17%)
  local copies, waits for them, and re-layouts  6.2 us (2%)
    ppermute x31, waiting for transfers between devices, send(): return lax.ppermute(x, 'fsdp', perm)  38.1 us
    ppermute x31, starting transfers between devices, send(): return lax.ppermute(x, 'fsdp', perm)  35.7 us
    pallas_call x5, Pallas kernels, block_logits(): pl.pallas_call(functools.partial(logits_kernel, slots, earlier), grid=(de...  29.5 us
    pallas_call x5, Pallas kernels, table_part(): pl.pallas_call(part_kernel, grid=(size // step,), in_specs=[pl.BlockSpec(...  27.2 us
    pallas_call x4, Pallas kernels, partials(): pl.pallas_call(functools.partial(partial_kernel, counts), grid=(depth //...  25.1 us
    ppermute x5, starting transfers between devices, exchange(): return lax.ppermute(x, ('pipe', 'fsdp'), facing)  23.7 us
    pallas_call x5, Pallas kernels, add_part(): pl.pallas_call(add_kernel, grid=(num_rows, num_columns // wide), in_specs...  18.1 us
    pallas_call x2, Pallas kernels, teacher_weights(): pl.pallas_call(functools.partial(teacher_kernel, rest), grid_spec=pltpu.P...  15.3 us
  transfers between devices with their start and end apart: 38, of which 16 were waited for; matrix products, arithmetic and copies ran while one was open for 2% of the time, Pallas kernels for 50%

profile of v4, /device:TPU:1, one launch (start us, length us, event | category | flops | bytes accessed | tf_op | source)
XLA Modules:
  0.0 279.6 jit_solution(12752247758035435020)
XLA Ops:
  13.6 7.6 %teacher_weights.2.refs_2_.refs_6_.refs_7_.refs_4_.refs_0_ = f32[4,512,128]{2,1,0:T(8,128)} custom-call(s32[4]{0:T(128)} %bitcast.31, s32[1]{0:T(128)} %bitcast.2.base_ref, s32[64,1024]{1,0:T(8,128)} %bitcast.20, f32[64,1024]{1,0:T(8,128)} %bitcast.22), custom_call_target="tpu_custom_call" | custom-call | flops 1 | bytes 1 | tf_op jit(solution)/shard_map/teacher_weights/pallas_call | solution.py:91
  27.8 5.1 %block_logits.5 = (f32[1,512,128]{2,1,0:T(8,128)}, f32[24,128]{1,0:T(8,128)}) custom-call(bf16[1,512,6144]{2,1,0:T(8,128)(2,1)} %head_ref.19, bf16[64,6144]{1,0:T(8,128)(2,1)} %get-tuple-element.98.refs_0_.refs_8_, bf16[64,6144]{1,0:T(8,128)(2,1)} %get-tuple-element.104.refs_1_.refs_9_, f32[4,512,128]{2,1,0:T(8,128)} %teacher_weights.2.refs_2_.refs_6_.refs_7_.refs_4_.refs_0_), custom_call_target="tpu_custom_call" | custom-call | flops 1 | bytes 1 | tf_op jit(solution)/shard_map/block_logits/pallas_call | solution.py:151
  34.4 5.5 %collective-permute-done.5.refs_3_.refs_11_ = bf16[64,6144]{1,0:T(8,128)(2,1)} collective-permute-done((bf16[64,6144]{1,0:T(8,128)(2,1)}, bf16[64,6144]{1,0:T(8,128)(2,1)}, u32[]{:S(2)}, u32[]{:S(2)}) %collective-permute-start.5) | collective-permute-done | bytes 786464 | tf_op jit(solution)/shard_map/ppermute | solution.py:473
  45.2 7.6 %teacher_weights.3.refs_8_.refs_2_.refs_5_.refs_1_ = f32[4,512,128]{2,1,0:T(8,128)} custom-call(s32[4]{0:T(128)} %slice.58.order_ref, s32[1]{0:T(128)} %bitcast.2.base_ref, s32[64,1024]{1,0:T(8,128)} %bitcast.21, f32[64,1024]{1,0:T(8,128)} %bitcast.23), custom_call_target="tpu_custom_call" | custom-call | flops 1 | bytes 1 | tf_op jit(solution)/shard_map/teacher_weights/pallas_call | solution.py:91
  54.3 8.1 %block_logits.6 = (f32[3,512,128]{2,1,0:T(8,128)}, f32[24,128]{1,0:T(8,128)}) custom-call(bf16[1,512,6144]{2,1,0:T(8,128)(2,1)} %head_ref.19, bf16[64,6144]{1,0:T(8,128)(2,1)} %collective-permute-done.1.refs_0_.refs_14_.refs_6_, bf16[64,6144]{1,0:T(8,128)(2,1)} %collective-permute-done.3.refs_1_.refs_15_.refs_7_, bf16[64,6144]{1,0:T(8,128)(2,1)} %copy-done.2, ...), custom_call_target="tpu_custom_call" | custom-call | flops 1 | bytes 1 | tf_op jit(solution)/shard_map/block_logits/pallas_call | solution.py:151
  65.7 5.2 %block_logits.7 = (f32[1,512,128]{2,1,0:T(8,128)}, f32[24,128]{1,0:T(8,128)}) custom-call(bf16[1,512,6144]{2,1,0:T(8,128)(2,1)} %head_ref.19, bf16[64,6144]{1,0:T(8,128)(2,1)} %copy-done.3, bf16[64,6144]{1,0:T(8,128)(2,1)} %collective-permute-done.7.refs_1_.refs_3_.refs_11_, f32[4,512,128]{2,1,0:T(8,128)} %teacher_weights.3.refs_8_.refs_2_.refs_5_.refs_1_), custom_call_target="tpu_custom_call" | custom-call | flops 1 | bytes 1 | tf_op jit(solution)/shard_map/block_logits/pallas_call | solution.py:151
  70.9 5.8 %collective-permute-done.11.refs_0_.refs_12_.refs_4_ = bf16[64,6144]{1,0:T(8,128)(2,1)} collective-permute-done((bf16[64,6144]{1,0:T(8,128)(2,1)}, bf16[64,6144]{1,0:T(8,128)(2,1)}, u32[]{:S(2)}, u32[]{:S(2)}) %collective-permute-start.11) | collective-permute-done | bytes 786464 | tf_op jit(solution)/shard_map/ppermute | solution.py:473
  77.7 5.9 %block_logits.8 = (f32[2,512,128]{2,1,0:T(8,128)}, f32[24,128]{1,0:T(8,128)}) custom-call(bf16[1,512,6144]{2,1,0:T(8,128)(2,1)} %head_ref.19, bf16[64,6144]{1,0:T(8,128)(2,1)} %collective-permute-done.11.refs_0_.refs_12_.refs_4_, bf16[64,6144]{1,0:T(8,128)(2,1)} %collective-permute-done.12.refs_1_.refs_13_.refs_5_, ...), custom_call_target="tpu_custom_call" | custom-call | flops 1 | bytes 1 | tf_op jit(solution)/shard_map/block_logits/pallas_call | solution.py:151
  83.6 9.9 %collective-permute-done.9.refs_0_.refs_4_.refs_12_ = bf16[64,6144]{1,0:T(8,128)(2,1)} collective-permute-done((bf16[64,6144]{1,0:T(8,128)(2,1)}, bf16[64,6144]{1,0:T(8,128)(2,1)}, u32[]{:S(2)}, u32[]{:S(2)}) %collective-permute-start.9) | collective-permute-done | bytes 786464 | tf_op jit(solution)/shard_map/ppermute | solution.py:473
  93.5 5.2 %block_logits.9 = (f32[1,512,128]{2,1,0:T(8,128)}, f32[24,128]{1,0:T(8,128)}) custom-call(bf16[1,512,6144]{2,1,0:T(8,128)(2,1)} %head_ref.19, bf16[64,6144]{1,0:T(8,128)(2,1)} %collective-permute-done.9.refs_0_.refs_4_.refs_12_, bf16[64,6144]{1,0:T(8,128)(2,1)} %collective-permute-done.10.refs_1_.refs_5_.refs_13_, ...), custom_call_target="tpu_custom_call" | custom-call | flops 1 | bytes 1 | tf_op jit(solution)/shard_map/block_logits/pallas_call | solution.py:151
  115.9 6.5 %table_part.5 = bf16[128,3840]{1,0:T(8,128)(2,1)} custom-call(bf16[128,1024]{1,0:T(8,128)(2,1)} %copy-done.5, bf16[64,6144]{1,0:T(8,128)(2,1)} %collective-permute-done.refs_4_.refs_0_.refs_8_, bf16[64,6144]{1,0:T(8,128)(2,1)} %collective-permute-done.6.refs_5_.refs_1_.refs_9_, bf16[64,6144]{1,0:T(8,128)(2,1)} %copy-done.3, ...), custom_call_target="tpu_custom_call" | custom-call | flops 1 | bytes 1 | tf_op jit(solution)/shard_map/table_part/pallas_call | solution.py:259
  122.4 11.3 %collective-permute-start.22 = (bf16[128,3840]{1,0:T(8,128)(2,1)}, bf16[128,3840]{1,0:T(8,128)(2,1)}, u32[]{:S(2)}, u32[]{:S(2)}) collective-permute-start(bf16[128,3840]{1,0:T(8,128)(2,1)} %table_part.5), channel_id=1, source_target_pairs={{0,121},{1,120},{2,123},{3,122},{4,125},{5,124},{6,127},{7,126},{8... | collective-permute-start | bytes 2949128 | tf_op jit(solution)/shard_map/ppermute | solution.py:476
  133.7 5.3 %partials.4 = (bf16[64,6144]{1,0:T(8,128)(2,1)}, bf16[64,6144]{1,0:T(8,128)(2,1)}) custom-call(bf16[1,512,6144]{2,1,0:T(8,128)(2,1)} %head_ref.19, bf16[1024,128]{1,0:T(8,128)(2,1)} %get-tuple-element.171.refs_0_.refs_1_.refs_2_.refs_3_.refs_4_.refs_5_, bf16[1024,128]{1,0:T(8,128)(2,1)} %get-tuple-element.171.refs_0_.refs_1_.refs_2_.refs_3_.refs_4_.refs_5_, ...), custom_call_target="tpu_custom_call" | custom-call | flops 1 | bytes 1 | tf_op jit(solution)/shard_map/partials/pallas_call | solution.py:364
  141.8 7.2 %partials.5 = (bf16[128,6144]{1,0:T(8,128)(2,1)}, bf16[128,6144]{1,0:T(8,128)(2,1)}, bf16[128,6144]{1,0:T(8,128)(2,1)}) custom-call(bf16[1,512,6144]{2,1,0:T(8,128)(2,1)} %head_ref.19, bf16[1024,128]{1,0:T(8,128)(2,1)} %get-tuple-element.171.refs_0_.refs_1_.refs_2_.refs_3_.refs_4_.refs_5_, ...), custom_call_target="tpu_custom_call" | custom-call | flops 1 | bytes 1 | tf_op jit(solution)/shard_map/partials/pallas_call | solution.py:364
  149.9 5.8 %table_part.6 = bf16[384,2304]{1,0:T(8,128)(2,1)} custom-call(bf16[384,1024]{1,0:T(8,128)(2,1)} %copy-done.4, bf16[64,6144]{1,0:T(8,128)(2,1)} %collective-permute-done.refs_4_.refs_0_.refs_8_, bf16[64,6144]{1,0:T(8,128)(2,1)} %collective-permute-done.6.refs_5_.refs_1_.refs_9_, bf16[64,6144]{1,0:T(8,128)(2,1)} %copy-done.3, ...), custom_call_target="tpu_custom_call" | custom-call | flops 1 | bytes 1 | tf_op jit(solution)/shard_map/table_part/pallas_call | solution.py:259
  166.2 5.9 %table_part.9 = bf16[384,2304]{1,0:T(8,128)(2,1)} custom-call(bf16[384,1024]{1,0:T(8,128)(2,1)} %copy-done.4, bf16[64,6144]{1,0:T(8,128)(2,1)} %collective-permute-done.refs_4_.refs_0_.refs_8_, bf16[64,6144]{1,0:T(8,128)(2,1)} %collective-permute-done.6.refs_5_.refs_1_.refs_9_, bf16[64,6144]{1,0:T(8,128)(2,1)} %copy-done.3, ...), custom_call_target="tpu_custom_call" | custom-call | flops 1 | bytes 1 | tf_op jit(solution)/shard_map/table_part/pallas_call | solution.py:259
  175.1 7.2 %partials.6 = (bf16[128,6144]{1,0:T(8,128)(2,1)}, bf16[128,6144]{1,0:T(8,128)(2,1)}, bf16[128,6144]{1,0:T(8,128)(2,1)}) custom-call(bf16[1,512,6144]{2,1,0:T(8,128)(2,1)} %head_ref.19, bf16[1024,128]{1,0:T(8,128)(2,1)} %get-tuple-element.171.refs_0_.refs_1_.refs_2_.refs_3_.refs_4_.refs_5_, ...), custom_call_target="tpu_custom_call" | custom-call | flops 1 | bytes 1 | tf_op jit(solution)/shard_map/partials/pallas_call | solution.py:364
  186.6 4.6 %table_part.8 = bf16[128,2304]{1,0:T(8,128)(2,1)} custom-call(bf16[128,1024]{1,0:T(8,128)(2,1)} %copy-done.5, bf16[64,6144]{1,0:T(8,128)(2,1)} %collective-permute-done.refs_4_.refs_0_.refs_8_, bf16[64,6144]{1,0:T(8,128)(2,1)} %collective-permute-done.6.refs_5_.refs_1_.refs_9_, bf16[64,6144]{1,0:T(8,128)(2,1)} %copy-done.3, ...), custom_call_target="tpu_custom_call" | custom-call | flops 1 | bytes 1 | tf_op jit(solution)/shard_map/table_part/pallas_call | solution.py:259
  191.3 5.0 %collective-permute-done.25.refs_5_.refs_8_ = bf16[128,6144]{1,0:T(8,128)(2,1)} collective-permute-done((bf16[128,6144]{1,0:T(8,128)(2,1)}, bf16[128,6144]{1,0:T(8,128)(2,1)}, u32[]{:S(2)}, u32[]{:S(2)}) %collective-permute-start.25) | collective-permute-done | bytes 1572896 | tf_op jit(solution)/shard_map/ppermute | solution.py:473
  196.2 4.5 %collective-permute-done.23.other_ref = bf16[384,2304]{1,0:T(8,128)(2,1)} collective-permute-done((bf16[384,2304]{1,0:T(8,128)(2,1)}, bf16[384,2304]{1,0:T(8,128)(2,1)}, u32[]{:S(2)}, u32[]{:S(2)}) %collective-permute-start.23) | collective-permute-done | bytes 1769504 | tf_op jit(solution)/shard_map/ppermute | solution.py:476
  201.6 5.7 %join.3 = (bf16[128,6144]{1,0:T(8,128)(2,1)}, bf16[128,6144]{1,0:T(8,128)(2,1)}, bf16[128,6144]{1,0:T(8,128)(2,1)}) custom-call(bf16[128,6144]{1,0:T(8,128)(2,1)} %get-tuple-element.167.refs_0_, bf16[128,6144]{1,0:T(8,128)(2,1)} %get-tuple-element.168.refs_1_, bf16[128,6144]{1,0:T(8,128)(2,1)} %get-tuple-element.169.refs_2_, ...), custom_call_target="tpu_custom_call" | custom-call | flops 1 | bytes 1 | tf_op jit(solution)/shard_map/join/pallas_call | solution.py:402
  213.0 14.5 %own_table.1 = (bf16[512,6144]{1,0:T(8,128)(2,1)}, f32[8,6144]{1,0:T(8,128)}) custom-call(bf16[128,1024]{1,0:T(8,128)(2,1)} %get-tuple-element.173.first_ref, bf16[384,1024]{1,0:T(8,128)(2,1)} %get-tuple-element.174.other_ref, bf16[1,512,6144]{2,1,0:T(8,128)(2,1)} %head_ref.19, f32[1,6144]{1,0:T(1,128)} %gain_ref.7, ...), custom_call_target="tpu_custom_call" | custom-call | flops 1 | bytes 1 | tf_op jit(solution)/shard_map/own_table/pallas_call | solution.py:287
  242.0 5.4 %partials.7.refs_0_ = bf16[128,6144]{1,0:T(8,128)(2,1)} custom-call(bf16[1,512,6144]{2,1,0:T(8,128)(2,1)} %head_ref.19, bf16[1024,128]{1,0:T(8,128)(2,1)} %get-tuple-element.171.refs_0_.refs_1_.refs_2_.refs_3_.refs_4_.refs_5_, bf16[1024,128]{1,0:T(8,128)(2,1)} %get-tuple-element.171.refs_0_.refs_1_.refs_2_.refs_3_.refs_4_.refs_5_, ...), custom_call_target="tpu_custom_call" | custom-call | flops 1 | bytes 1 | tf_op jit(solution)/shard_map/partials/pallas_call | solution.py:364
  253.2 6.0 %states_gradient.1 = bf16[128,6144]{1,0:T(8,128)(2,1)} custom-call(bf16[128,6144]{1,0:T(8,128)(2,1)} %hidden_ref.5, f32[128,128]{1,0:T(8,128)} %pad_maximum_fusion.scale_ref, f32[1,6144]{1,0:T(1,128)} %gain_ref.7, bf16[128,6144]{1,0:T(8,128)(2,1)} %partials.7.refs_0_, bf16[128,6144]{1,0:T(8,128)(2,1)} %collective-permute-done.28.refs_1_, ...), custom_call_target="tpu_custom_call" | custom-call | flops 1 | bytes 1 | tf_op jit(solution)/shard_map/states_gradient/pallas_call | solution.py:431
  (129 shorter events, 117.8 us)
Async XLA Ops:
  2.9 20.1 %collective-permute-start.2 = (bf16[64,6144]{1,0:T(8,128)(2,1)}, bf16[64,6144]{1,0:T(8,128)(2,1)S(1)}, u32[]{:S(2)}, u32[]{:S(2)}) collective-permute-start(bf16[64,6144]{1,0:T(8,128)(2,1)} %get-tuple-element.98.refs_0_.refs_8_), channel_id=1, source_target_pairs={{0,6},{1,7},{2,0},{3,1},{4,2},{5,3},{6,4},{7,5},{8,14},{9,15},{10,... | collective-permute-start | bytes 2359304 | tf_op jit(solution)/shard_map/ppermute | solution.py:473
  6.5 19.6 %collective-permute-start.1 = (bf16[64,6144]{1,0:T(8,128)(2,1)}, bf16[64,6144]{1,0:T(8,128)(2,1)}, u32[]{:S(2)}, u32[]{:S(2)}) collective-permute-start(bf16[64,6144]{1,0:T(8,128)(2,1)} %get-tuple-element.98.refs_0_.refs_8_), channel_id=1, source_target_pairs={{0,2},{1,3},{2,4},{3,5},{4,6},{5,7},{6,0},{7,1},{8,10},{9,11},{10,... | collective-permute-start | bytes 2359304 | tf_op jit(solution)/shard_map/ppermute | solution.py:473
  6.5 19.6 %collective-permute-start = (bf16[64,6144]{1,0:T(8,128)(2,1)}, bf16[64,6144]{1,0:T(8,128)(2,1)}, u32[]{:S(2)}, u32[]{:S(2)}) collective-permute-start(bf16[64,6144]{1,0:T(8,128)(2,1)} %get-tuple-element.98.refs_0_.refs_8_), channel_id=1, source_target_pairs={{0,1},{1,0},{2,3},{3,2},{4,5},{5,4},{6,7},{7,6},{8,9},{9,8},{10,11... | collective-permute-start | bytes 2359304 | tf_op jit(solution)/shard_map/ppermute | solution.py:473
  10.4 29.5 %collective-permute-start.5 = (bf16[64,6144]{1,0:T(8,128)(2,1)}, bf16[64,6144]{1,0:T(8,128)(2,1)}, u32[]{:S(2)}, u32[]{:S(2)}) collective-permute-start(bf16[64,6144]{1,0:T(8,128)(2,1)} %get-tuple-element.104.refs_1_.refs_9_), channel_id=1, source_target_pairs={{0,6},{1,7},{2,0},{3,1},{4,2},{5,3},{6,4},{7,5},{8,14},{9,15},{10,... | collective-permute-start | bytes 2359304 | tf_op jit(solution)/shard_map/ppermute | solution.py:473
  13.1 29.9 %collective-permute-start.3 = (bf16[64,6144]{1,0:T(8,128)(2,1)}, bf16[64,6144]{1,0:T(8,128)(2,1)}, u32[]{:S(2)}, u32[]{:S(2)}) collective-permute-start(bf16[64,6144]{1,0:T(8,128)(2,1)} %get-tuple-element.104.refs_1_.refs_9_), channel_id=1, source_target_pairs={{0,2},{1,3},{2,4},{3,5},{4,6},{5,7},{6,0},{7,1},{8,10},{9,11},{10,... | collective-permute-start | bytes 2359304 | tf_op jit(solution)/shard_map/ppermute | solution.py:473
  32.9 29.6 %collective-permute-start.8 = (bf16[64,6144]{1,0:T(8,128)(2,1)}, bf16[64,6144]{1,0:T(8,128)(2,1)S(1)}, u32[]{:S(2)}, u32[]{:S(2)}) collective-permute-start(bf16[64,6144]{1,0:T(8,128)(2,1)} %collective-permute-done.refs_4_.refs_0_.refs_8_), channel_id=1, source_target_pairs={{0,6},{1,7},{2,0},{3,1},{4,2},{5,3},{6,4},{7,5},{8,14},{9,15},{10,... | collective-permute-start | bytes 2359304 | tf_op jit(solution)/shard_map/ppermute | solution.py:473
  34.0 28.4 %collective-permute-start.4 = (bf16[64,6144]{1,0:T(8,128)(2,1)}, bf16[64,6144]{1,0:T(8,128)(2,1)}, u32[]{:S(2)}, u32[]{:S(2)}) collective-permute-start(bf16[64,6144]{1,0:T(8,128)(2,1)} %collective-permute-done.refs_4_.refs_0_.refs_8_), channel_id=1, source_target_pairs={{0,2},{1,3},{2,4},{3,5},{4,6},{5,7},{6,0},{7,1},{8,10},{9,11},{10,... | collective-permute-start | bytes 2359304 | tf_op jit(solution)/shard_map/ppermute | solution.py:473
  43.0 19.5 %collective-permute-start.7 = (bf16[64,6144]{1,0:T(8,128)(2,1)}, bf16[64,6144]{1,0:T(8,128)(2,1)}, u32[]{:S(2)}, u32[]{:S(2)}) collective-permute-start(bf16[64,6144]{1,0:T(8,128)(2,1)} %collective-permute-done.5.refs_3_.refs_11_), channel_id=1, source_target_pairs={{0,1},{1,0},{2,3},{3,2},{4,5},{5,4},{6,7},{7,6},{8,9},{9,8},{10,11... | collective-permute-start | bytes 2359304 | tf_op jit(solution)/shard_map/ppermute | solution.py:473
  52.8 23.9 %collective-permute-start.12 = (bf16[64,6144]{1,0:T(8,128)(2,1)}, bf16[64,6144]{1,0:T(8,128)(2,1)}, u32[]{:S(2)}, u32[]{:S(2)}) collective-permute-start(bf16[64,6144]{1,0:T(8,128)(2,1)} %collective-permute-done.5.refs_3_.refs_11_), channel_id=1, source_target_pairs={{0,6},{1,7},{2,0},{3,1},{4,2},{5,3},{6,4},{7,5},{8,14},{9,15},{10,... | collective-permute-start | bytes 2359304 | tf_op jit(solution)/shard_map/ppermute | solution.py:473
  54.3 22.3 %collective-permute-start.11 = (bf16[64,6144]{1,0:T(8,128)(2,1)}, bf16[64,6144]{1,0:T(8,128)(2,1)}, u32[]{:S(2)}, u32[]{:S(2)}) collective-permute-start(bf16[64,6144]{1,0:T(8,128)(2,1)} %collective-permute-done.1.refs_0_.refs_14_.refs_6_), channel_id=1, source_target_pairs={{0,2},{1,3},{2,4},{3,5},{4,6},{5,7},{6,0},{7,1},{8,10},{9,11},{10,... | collective-permute-start | bytes 2359304 | tf_op jit(solution)/shard_map/ppermute | solution.py:473
  63.0 30.5 %collective-permute-start.9 = (bf16[64,6144]{1,0:T(8,128)(2,1)}, bf16[64,6144]{1,0:T(8,128)(2,1)}, u32[]{:S(2)}, u32[]{:S(2)}) collective-permute-start(bf16[64,6144]{1,0:T(8,128)(2,1)} %collective-permute-done.4.refs_2_.refs_6_.refs_14_), channel_id=1, source_target_pairs={{0,2},{1,3},{2,4},{3,5},{4,6},{5,7},{6,0},{7,1},{8,10},{9,11},{10,... | collective-permute-start | bytes 2359304 | tf_op jit(solution)/shard_map/ppermute | solution.py:473
  63.0 30.5 %collective-permute-start.10 = (bf16[64,6144]{1,0:T(8,128)(2,1)}, bf16[64,6144]{1,0:T(8,128)(2,1)}, u32[]{:S(2)}, u32[]{:S(2)}) collective-permute-start(bf16[64,6144]{1,0:T(8,128)(2,1)} %collective-permute-done.7.refs_1_.refs_3_.refs_11_), channel_id=1, source_target_pairs={{0,6},{1,7},{2,0},{3,1},{4,2},{5,3},{6,4},{7,5},{8,14},{9,15},{10,... | collective-permute-start | bytes 2359304 | tf_op jit(solution)/shard_map/ppermute | solution.py:473
  122.4 37.1 %collective-permute-start.22 = (bf16[128,3840]{1,0:T(8,128)(2,1)}, bf16[128,3840]{1,0:T(8,128)(2,1)}, u32[]{:S(2)}, u32[]{:S(2)}) collective-permute-start(bf16[128,3840]{1,0:T(8,128)(2,1)} %table_part.5), channel_id=1, source_target_pairs={{0,121},{1,120},{2,123},{3,122},{4,125},{5,124},{6,127},{7,126},{8... | collective-permute-start | bytes 2949128 | tf_op jit(solution)/shard_map/ppermute | solution.py:476
  139.1 20.4 %collective-permute-start.21 = (bf16[64,6144]{1,0:T(8,128)(2,1)}, bf16[64,6144]{1,0:T(8,128)(2,1)}, u32[]{:S(2)}, u32[]{:S(2)}) collective-permute-start(bf16[64,6144]{1,0:T(8,128)(2,1)} %get-tuple-element.144), channel_id=1, source_target_pairs={{0,2},{1,3},{2,4},{3,5},{4,6},{5,7},{6,0},{7,1},{8,10},{9,11},{10,... | collective-permute-start | bytes 2359304 | tf_op jit(solution)/shard_map/ppermute | solution.py:473
  155.7 45.0 %collective-permute-start.23 = (bf16[384,2304]{1,0:T(8,128)(2,1)}, bf16[384,2304]{1,0:T(8,128)(2,1)}, u32[]{:S(2)}, u32[]{:S(2)}) collective-permute-start(bf16[384,2304]{1,0:T(8,128)(2,1)} %table_part.6), channel_id=1, source_target_pairs={{0,121},{1,120},{2,123},{3,122},{4,125},{5,124},{6,127},{7,126},{8... | collective-permute-start | bytes 5308424 | tf_op jit(solution)/shard_map/ppermute | solution.py:476
  159.5 36.8 %collective-permute-start.25 = (bf16[128,6144]{1,0:T(8,128)(2,1)}, bf16[128,6144]{1,0:T(8,128)(2,1)}, u32[]{:S(2)}, u32[]{:S(2)}) collective-permute-start(bf16[128,6144]{1,0:T(8,128)(2,1)} %get-tuple-element.161), channel_id=1, source_target_pairs={{0,2},{1,3},{2,4},{3,5},{4,6},{5,7},{6,0},{7,1},{8,10},{9,11},{10,... | collective-permute-start | bytes 4718600 | tf_op jit(solution)/shard_map/ppermute | solution.py:473
  164.8 35.9 %collective-permute-start.26 = (bf16[128,6144]{1,0:T(8,128)(2,1)}, bf16[128,6144]{1,0:T(8,128)(2,1)}, u32[]{:S(2)}, u32[]{:S(2)}) collective-permute-start(bf16[128,6144]{1,0:T(8,128)(2,1)} %get-tuple-element.162), channel_id=1, source_target_pairs={{0,1},{1,0},{2,3},{3,2},{4,5},{5,4},{6,7},{7,6},{8,9},{9,8},{10,11... | collective-permute-start | bytes 4718600 | tf_op jit(solution)/shard_map/ppermute | solution.py:473
  165.2 36.4 %collective-permute-start.24 = (bf16[128,6144]{1,0:T(8,128)(2,1)}, bf16[128,6144]{1,0:T(8,128)(2,1)}, u32[]{:S(2)}, u32[]{:S(2)}) collective-permute-start(bf16[128,6144]{1,0:T(8,128)(2,1)} %get-tuple-element.153), channel_id=1, source_target_pairs={{0,6},{1,7},{2,0},{3,1},{4,2},{5,3},{6,4},{7,5},{8,14},{9,15},{10,... | collective-permute-start | bytes 4718600 | tf_op jit(solution)/shard_map/ppermute | solution.py:473
  172.1 66.5 %collective-permute-start.27 = (bf16[384,2304]{1,0:T(8,128)(2,1)}, bf16[384,2304]{1,0:T(8,128)(2,1)}, u32[]{:S(2)}, u32[]{:S(2)}) collective-permute-start(bf16[384,2304]{1,0:T(8,128)(2,1)} %table_part.9), channel_id=1, source_target_pairs={{0,121},{1,120},{2,123},{3,122},{4,125},{5,124},{6,127},{7,126},{8... | collective-permute-start | bytes 5308424 | tf_op jit(solution)/shard_map/ppermute | solution.py:476
  207.3 45.1 %collective-permute-start.29 = (bf16[128,6144]{1,0:T(8,128)(2,1)}, bf16[128,6144]{1,0:T(8,128)(2,1)}, u32[]{:S(2)}, u32[]{:S(2)}) collective-permute-start(bf16[128,6144]{1,0:T(8,128)(2,1)} %get-tuple-element.178), channel_id=1, source_target_pairs={{0,2},{1,3},{2,4},{3,5},{4,6},{5,7},{6,0},{7,1},{8,10},{9,11},{10,... | collective-permute-start | bytes 4718600 | tf_op jit(solution)/shard_map/ppermute | solution.py:473
  208.0 44.4 %collective-permute-start.30 = (bf16[128,6144]{1,0:T(8,128)(2,1)}, bf16[128,6144]{1,0:T(8,128)(2,1)}, u32[]{:S(2)}, u32[]{:S(2)}) collective-permute-start(bf16[128,6144]{1,0:T(8,128)(2,1)} %get-tuple-element.179), channel_id=1, source_target_pairs={{0,1},{1,0},{2,3},{3,2},{4,5},{5,4},{6,7},{7,6},{8,9},{9,8},{10,11... | collective-permute-start | bytes 4718600 | tf_op jit(solution)/shard_map/ppermute | solution.py:473
  208.1 44.3 %collective-permute-start.28 = (bf16[128,6144]{1,0:T(8,128)(2,1)}, bf16[128,6144]{1,0:T(8,128)(2,1)}, u32[]{:S(2)}, u32[]{:S(2)}) collective-permute-start(bf16[128,6144]{1,0:T(8,128)(2,1)} %get-tuple-element.170), channel_id=1, source_target_pairs={{0,6},{1,7},{2,0},{3,1},{4,2},{5,3},{6,4},{7,5},{8,14},{9,15},{10,... | collective-permute-start | bytes 4718600 | tf_op jit(solution)/shard_map/ppermute | solution.py:473
  210.7 53.2 %collective-permute-start.32 = (bf16[384,1536]{1,0:T(8,128)(2,1)}, bf16[384,1536]{1,0:T(8,128)(2,1)}, u32[]{:S(2)}, u32[]{:S(2)}) collective-permute-start(bf16[384,1536]{1,0:T(8,128)(2,1)} %table_part.7), channel_id=1, source_target_pairs={{0,121},{1,120},{2,123},{3,122},{4,125},{5,124},{6,127},{7,126},{8... | collective-permute-start | bytes 3538952 | tf_op jit(solution)/shard_map/ppermute | solution.py:476
  238.6 38.1 %collective-permute-start.31 = (bf16[128,2304]{1,0:T(8,128)(2,1)S(1)}, bf16[128,2304]{1,0:T(8,128)(2,1)}, u32[]{:S(2)}, u32[]{:S(2)}) collective-permute-start(bf16[128,2304]{1,0:T(8,128)(2,1)S(1)} %copy-done.6), channel_id=1, source_target_pairs={{0,121},{1,120},{2,123},{3,122},{4,125},{5,124},{6,127},{7,126},{8... | collective-permute-start | bytes 1769480 | tf_op jit(solution)/shard_map/ppermute | solution.py:476
  (28 other events, 286.9 us)

commit v5 on v4

--- a/solution.py
+++ b/solution.py
@@ -12,17 +12,17 @@
 epsilon = 1e-05
 F32 = jnp.float32
 BF16 = jnp.bfloat16
-BIG = 63 * 1024 * 1024
+BIG = 65408 * 1024
 
 RING, SIDES = 4, 2
 BLOCKS = RING * SIDES
 ROWS, COLUMNS = 128, 768
 PARTS = (
-    (0, 1, 3, 5),
+    (0, 1, 2, 6),
     (1, 3, 0, 3),
     (1, 3, 3, 3),
     (1, 3, 6, 2),
-    (0, 1, 0, 3),
+    (0, 1, 0, 2),
 )
 
 
@@ -568,30 +568,36 @@
     theirs.append(exchange(parts[1]))
     to_down, to_swap = join([a0, a2], [[[(r_o2a, 0)], []], [[(r_o2b, 0)], []]])
     o3a_s2a, o1a_s2b, o1b_o3b = send(to_down, down), send(a1, up), send(to_swap, swap)
-    their_first, their_second = gate((their_first, their_second), to_down)
-    parts += [part_of(2, their_second), part_of(3, their_second), part_of(4, their_first)]
+    their_first, their_second, first, second = gate(
+        (their_first, their_second, first, second), to_down
+    )
+    parts += [part_of(2, their_second), part_of(3, their_second)]
     theirs.append(exchange(parts[2]))
     ahead = partials(
         gate(low, to_down), head, [[(6, []), (7, [])], [(2, []), (3, [])], [(8, []), (9, [])]]
     )
 
-    *low, first, second, theirs[1], parts[3], parts[4], a0, a1, a2 = gate(
-        (*low, first, second, theirs[1], parts[3], parts[4], *ahead),
+    own, along = own_table(first, second, head, gain, pieces)
+    along = along[:1].reshape(8, depth // 8)
+    scale = jnp.concatenate([scale_a, scale_b], axis=0)
+
+    *low, own, along, scale, own_loss, theirs[1], parts[3], their_first, a0, a1, a2 = gate(
+        (*low, own, along, scale, loss[0], theirs[1], parts[3], their_first, *ahead),
         o3a_s2a, o1a_s2b, o1b_o3b,
     )
     theirs.append(exchange(parts[3]))
-    to_down, to_up, to_swap = join(
+    along = along + send(along, swap)
+    to_down, to_up, to_swap = gate(join(
         [a0, a1, a2],
         [
             [[(o3a_s2a, 1)], [(o1b_o3b, 1)]],
             [[], [(o1a_s2b, 1), (o1b_o3b, 0)]],
             [[(o3a_s2a, 0), (o1a_s2b, 0)], []],
         ],
-    )
+    ), along)
     s3, s1, o0 = send(to_down, down), send(to_up, up), send(to_swap, swap)
-    *low, first, second = gate((*low, first, second), to_down)
-    own, along = own_table(first, second, head, gain, pieces)
-    along = along[:1].reshape(8, depth // 8)
+    *low, their_first = gate((*low, their_first), to_down)
+    parts.append(part_of(4, their_first))
     (mine,) = partials(low, head, [[(0, []), (1, [])]])
     merged = None
     for n in range(2):
@@ -601,13 +607,10 @@
     merged = add_part(own, theirs[2], merged, PARTS[2])
 
     mine, along, merged = gate((mine, along, merged), s3, s1, o0)
-    along = along + send(along, swap)
-    scale = jnp.concatenate([scale_a, scale_b], axis=0)
     grad_states = states_gradient(hidden, scale, gain, [mine, s3, s1, o0])
     merged = add_part(own, theirs[3], merged, PARTS[3])
+    along = along + send(along, [(f, f ^ SIDES) for f in range(BLOCKS)])
     along = gate((along,), grad_states)
-    along = along + send(along, [(f, f ^ SIDES) for f in range(BLOCKS)])
-    along = gate((along,), merged)
     opposite = [
         (p * BLOCKS + f, (num_pipe - 1 - p) * BLOCKS + t)
         for p in range(num_pipe)
@@ -621,7 +624,7 @@
     merged_gain = merged_gain.reshape(1, depth)
     theirs[4], merged = gate((theirs[4], merged), grad_states)
     merged = add_part(own, theirs[4], merged, PARTS[4])
-    return (loss[0], grad_states, merged, merged_gain)
+    return (own_loss, grad_states, merged, merged_gain)
 
 
 def solution(mesh):

time: 281 us -> 277 us (0.986)
  starting transfers between devices: 66 us -> 61.3 us
  other arithmetic: 2.55 us -> 5.54 us
    ppermute x31, starting transfers between devices: 35.7 us -> 29.5 us  [send(): return lax.ppermute(x, 'fsdp', perm)]
  transfers between devices with their start and end apart: 38 -> 38, of which waited for: 16 -> 14; matrix products, arithmetic and copies ran while one was open for 2% -> 3% of each run, Pallas kernels for 50% -> 50%
where the time goes in v5:
time: 277 us; the launch traced here: 275 us
  Pallas kernels  154 us (56%)
  starting transfers between devices  61.3 us (22%)
  waiting for transfers between devices  48.7 us (18%)
  other arithmetic  5.54 us (2%)
  local copies, waits for them, and re-layouts  4.59 us (2%)
    ppermute x31, waiting for transfers between devices, send(): return lax.ppermute(x, 'fsdp', perm)  36.7 us
    pallas_call x5, Pallas kernels, block_logits(): pl.pallas_call(functools.partial(logits_kernel, slots, earlier), grid=(de...  29.6 us
    ppermute x31, starting transfers between devices, send(): return lax.ppermute(x, 'fsdp', perm)  29.5 us
    pallas_call x5, Pallas kernels, table_part(): pl.pallas_call(part_kernel, grid=(size // step,), in_specs=[pl.BlockSpec(...  26.3 us
    ppermute x5, starting transfers between devices, exchange(): return lax.ppermute(x, ('pipe', 'fsdp'), facing)  25.5 us
    pallas_call x4, Pallas kernels, partials(): pl.pallas_call(functools.partial(partial_kernel, counts), grid=(depth //...  25.1 us
    pallas_call x5, Pallas kernels, add_part(): pl.pallas_call(add_kernel, grid=(num_rows, num_columns // wide), in_specs...  17.1 us
    pallas_call x2, Pallas kernels, teacher_weights(): pl.pallas_call(functools.partial(teacher_kernel, rest), grid_spec=pltpu.P...  15.3 us
  transfers between devices with their start and end apart: 38, of which 14 were waited for; matrix products, arithmetic and copies ran while one was open for 3% of the time, Pallas kernels for 50%

profile of v5, /device:TPU:1, one launch (start us, length us, event | category | flops | bytes accessed | tf_op | source)
XLA Modules:
  0.0 274.8 jit_solution(5336465008652445103)
XLA Ops:
  13.6 7.6 %teacher_weights.2.refs_2_.refs_6_.refs_7_.refs_4_.refs_0_ = f32[4,512,128]{2,1,0:T(8,128)} custom-call(s32[4]{0:T(128)} %bitcast.31, s32[1]{0:T(128)} %bitcast.2.base_ref, s32[64,1024]{1,0:T(8,128)} %bitcast.20, f32[64,1024]{1,0:T(8,128)} %bitcast.22), custom_call_target="tpu_custom_call" | custom-call | flops 1 | bytes 1 | tf_op jit(solution)/shard_map/teacher_weights/pallas_call | solution.py:91
  25.5 5.1 %block_logits.5 = (f32[1,512,128]{2,1,0:T(8,128)}, f32[24,128]{1,0:T(8,128)}) custom-call(bf16[1,512,6144]{2,1,0:T(8,128)(2,1)} %head_ref.19, bf16[64,6144]{1,0:T(8,128)(2,1)} %get-tuple-element.103.refs_0_.refs_8_, bf16[64,6144]{1,0:T(8,128)(2,1)} %get-tuple-element.109.refs_1_.refs_9_, f32[4,512,128]{2,1,0:T(8,128)} %teacher_weights.2.refs_2_.refs_6_.refs_7_.refs_4_.refs_0_), custom_call_target="tpu_custom_call" | custom-call | flops 1 | bytes 1 | tf_op jit(solution)/shard_map/block_logits/pallas_call | solution.py:151
  33.3 8.7 %collective-permute-done.3.refs_1_.refs_15_.refs_7_ = bf16[64,6144]{1,0:T(8,128)(2,1)} collective-permute-done((bf16[64,6144]{1,0:T(8,128)(2,1)}, bf16[64,6144]{1,0:T(8,128)(2,1)}, u32[]{:S(2)}, u32[]{:S(2)}) %collective-permute-start.3) | collective-permute-done | bytes 786464 | tf_op jit(solution)/shard_map/ppermute | solution.py:473
  42.9 7.6 %teacher_weights.3.refs_8_.refs_2_.refs_5_.refs_1_ = f32[4,512,128]{2,1,0:T(8,128)} custom-call(s32[4]{0:T(128)} %slice.58.order_ref, s32[1]{0:T(128)} %bitcast.2.base_ref, s32[64,1024]{1,0:T(8,128)} %bitcast.21, f32[64,1024]{1,0:T(8,128)} %bitcast.23), custom_call_target="tpu_custom_call" | custom-call | flops 1 | bytes 1 | tf_op jit(solution)/shard_map/teacher_weights/pallas_call | solution.py:91
  53.0 8.2 %block_logits.6 = (f32[3,512,128]{2,1,0:T(8,128)}, f32[24,128]{1,0:T(8,128)}) custom-call(bf16[1,512,6144]{2,1,0:T(8,128)(2,1)} %head_ref.19, bf16[64,6144]{1,0:T(8,128)(2,1)} %collective-permute-done.1.refs_0_.refs_14_.refs_6_, bf16[64,6144]{1,0:T(8,128)(2,1)} %collective-permute-done.3.refs_1_.refs_15_.refs_7_, ...), custom_call_target="tpu_custom_call" | custom-call | flops 1 | bytes 1 | tf_op jit(solution)/shard_map/block_logits/pallas_call | solution.py:151
  65.0 5.2 %block_logits.7 = (f32[1,512,128]{2,1,0:T(8,128)}, f32[24,128]{1,0:T(8,128)}) custom-call(bf16[1,512,6144]{2,1,0:T(8,128)(2,1)} %head_ref.19, bf16[64,6144]{1,0:T(8,128)(2,1)} %collective-permute-done.8.refs_0_.refs_2_.refs_10_, bf16[64,6144]{1,0:T(8,128)(2,1)} %collective-permute-done.7.refs_1_.refs_3_.refs_11_, ...), custom_call_target="tpu_custom_call" | custom-call | flops 1 | bytes 1 | tf_op jit(solution)/shard_map/block_logits/pallas_call | solution.py:151
  70.1 5.5 %collective-permute-done.11.refs_0_.refs_12_.refs_4_ = bf16[64,6144]{1,0:T(8,128)(2,1)} collective-permute-done((bf16[64,6144]{1,0:T(8,128)(2,1)}, bf16[64,6144]{1,0:T(8,128)(2,1)}, u32[]{:S(2)}, u32[]{:S(2)}) %collective-permute-start.11) | collective-permute-done | bytes 786464 | tf_op jit(solution)/shard_map/ppermute | solution.py:473
  76.7 5.9 %block_logits.8 = (f32[2,512,128]{2,1,0:T(8,128)}, f32[24,128]{1,0:T(8,128)}) custom-call(bf16[1,512,6144]{2,1,0:T(8,128)(2,1)} %head_ref.19, bf16[64,6144]{1,0:T(8,128)(2,1)} %collective-permute-done.11.refs_0_.refs_12_.refs_4_, bf16[64,6144]{1,0:T(8,128)(2,1)} %collective-permute-done.12.refs_1_.refs_13_.refs_5_, ...), custom_call_target="tpu_custom_call" | custom-call | flops 1 | bytes 1 | tf_op jit(solution)/shard_map/block_logits/pallas_call | solution.py:151
  82.6 9.9 %collective-permute-done.9.refs_0_.refs_4_.refs_12_ = bf16[64,6144]{1,0:T(8,128)(2,1)} collective-permute-done((bf16[64,6144]{1,0:T(8,128)(2,1)}, bf16[64,6144]{1,0:T(8,128)(2,1)}, u32[]{:S(2)}, u32[]{:S(2)}) %collective-permute-start.9) | collective-permute-done | bytes 786464 | tf_op jit(solution)/shard_map/ppermute | solution.py:473
  92.5 5.2 %block_logits.9 = (f32[1,512,128]{2,1,0:T(8,128)}, f32[24,128]{1,0:T(8,128)}) custom-call(bf16[1,512,6144]{2,1,0:T(8,128)(2,1)} %head_ref.19, bf16[64,6144]{1,0:T(8,128)(2,1)} %collective-permute-done.9.refs_0_.refs_4_.refs_12_, bf16[64,6144]{1,0:T(8,128)(2,1)} %collective-permute-done.10.refs_1_.refs_5_.refs_13_, ...), custom_call_target="tpu_custom_call" | custom-call | flops 1 | bytes 1 | tf_op jit(solution)/shard_map/block_logits/pallas_call | solution.py:151
  116.2 7.2 %table_part.5 = bf16[128,4608]{1,0:T(8,128)(2,1)} custom-call(bf16[128,1024]{1,0:T(8,128)(2,1)} %collective-permute-done.18.low_ref, bf16[64,6144]{1,0:T(8,128)(2,1)} %collective-permute-done.refs_4_.refs_0_.refs_8_, bf16[64,6144]{1,0:T(8,128)(2,1)} %collective-permute-done.6.refs_5_.refs_1_.refs_9_, ...), custom_call_target="tpu_custom_call" | custom-call | flops 1 | bytes 1 | tf_op jit(solution)/shard_map/table_part/pallas_call | solution.py:259
  123.3 10.5 %collective-permute-start.22 = (bf16[128,4608]{1,0:T(8,128)(2,1)}, bf16[128,4608]{1,0:T(8,128)(2,1)}, u32[]{:S(2)}, u32[]{:S(2)}) collective-permute-start(bf16[128,4608]{1,0:T(8,128)(2,1)} %table_part.5), channel_id=1, source_target_pairs={{0,121},{1,120},{2,123},{3,122},{4,125},{5,124},{6,127},{7,126},{8... | collective-permute-start | bytes 3538952 | tf_op jit(solution)/shard_map/ppermute | solution.py:476
  134.6 5.3 %partials.4 = (bf16[64,6144]{1,0:T(8,128)(2,1)}, bf16[64,6144]{1,0:T(8,128)(2,1)}) custom-call(bf16[1,512,6144]{2,1,0:T(8,128)(2,1)} %head_ref.19, bf16[1024,128]{1,0:T(8,128)(2,1)} %get-tuple-element.185.refs_0_.refs_1_.refs_2_.refs_3_.refs_4_.refs_5_, bf16[1024,128]{1,0:T(8,128)(2,1)} %get-tuple-element.185.refs_0_.refs_1_.refs_2_.refs_3_.refs_4_.refs_5_, ...), custom_call_target="tpu_custom_call" | custom-call | flops 1 | bytes 1 | tf_op jit(solution)/shard_map/partials/pallas_call | solution.py:364
  141.4 7.2 %partials.5 = (bf16[128,6144]{1,0:T(8,128)(2,1)}, bf16[128,6144]{1,0:T(8,128)(2,1)}, bf16[128,6144]{1,0:T(8,128)(2,1)}) custom-call(bf16[1,512,6144]{2,1,0:T(8,128)(2,1)} %head_ref.19, bf16[1024,128]{1,0:T(8,128)(2,1)} %get-tuple-element.185.refs_0_.refs_1_.refs_2_.refs_3_.refs_4_.refs_5_, ...), custom_call_target="tpu_custom_call" | custom-call | flops 1 | bytes 1 | tf_op jit(solution)/shard_map/partials/pallas_call | solution.py:364
  150.0 5.8 %table_part.6 = bf16[384,2304]{1,0:T(8,128)(2,1)} custom-call(bf16[384,1024]{1,0:T(8,128)(2,1)} %collective-permute-done.19.low_ref, bf16[64,6144]{1,0:T(8,128)(2,1)} %collective-permute-done.refs_4_.refs_0_.refs_8_, bf16[64,6144]{1,0:T(8,128)(2,1)} %collective-permute-done.6.refs_5_.refs_1_.refs_9_, ...), custom_call_target="tpu_custom_call" | custom-call | flops 1 | bytes 1 | tf_op jit(solution)/shard_map/table_part/pallas_call | solution.py:259
  155.8 4.5 %collective-permute-start.23 = (bf16[384,2304]{1,0:T(8,128)(2,1)}, bf16[384,2304]{1,0:T(8,128)(2,1)}, u32[]{:S(2)}, u32[]{:S(2)}) collective-permute-start(bf16[384,2304]{1,0:T(8,128)(2,1)} %table_part.6), channel_id=1, source_target_pairs={{0,121},{1,120},{2,123},{3,122},{4,125},{5,124},{6,127},{7,126},{8... | collective-permute-start | bytes 5308424 | tf_op jit(solution)/shard_map/ppermute | solution.py:476
  166.0 5.9 %table_part.8 = bf16[384,2304]{1,0:T(8,128)(2,1)} custom-call(bf16[384,1024]{1,0:T(8,128)(2,1)} %collective-permute-done.19.low_ref, bf16[64,6144]{1,0:T(8,128)(2,1)} %collective-permute-done.refs_4_.refs_0_.refs_8_, bf16[64,6144]{1,0:T(8,128)(2,1)} %collective-permute-done.6.refs_5_.refs_1_.refs_9_, ...), custom_call_target="tpu_custom_call" | custom-call | flops 1 | bytes 1 | tf_op jit(solution)/shard_map/table_part/pallas_call | solution.py:259
  177.1 7.2 %partials.6 = (bf16[128,6144]{1,0:T(8,128)(2,1)}, bf16[128,6144]{1,0:T(8,128)(2,1)}, bf16[128,6144]{1,0:T(8,128)(2,1)}) custom-call(bf16[1,512,6144]{2,1,0:T(8,128)(2,1)} %head_ref.19, bf16[1024,128]{1,0:T(8,128)(2,1)} %get-tuple-element.185.refs_0_.refs_1_.refs_2_.refs_3_.refs_4_.refs_5_, ...), custom_call_target="tpu_custom_call" | custom-call | flops 1 | bytes 1 | tf_op jit(solution)/shard_map/partials/pallas_call | solution.py:364
  184.3 4.3 %table_part.7 = bf16[384,1536]{1,0:T(8,128)(2,1)} custom-call(bf16[384,1024]{1,0:T(8,128)(2,1)} %collective-permute-done.19.low_ref, bf16[64,6144]{1,0:T(8,128)(2,1)} %collective-permute-done.refs_4_.refs_0_.refs_8_, bf16[64,6144]{1,0:T(8,128)(2,1)} %collective-permute-done.6.refs_5_.refs_1_.refs_9_, ...), custom_call_target="tpu_custom_call" | custom-call | flops 1 | bytes 1 | tf_op jit(solution)/shard_map/table_part/pallas_call | solution.py:259
  188.6 14.5 %own_table.1 = (bf16[512,6144]{1,0:T(8,128)(2,1)}, f32[8,6144]{1,0:T(8,128)}) custom-call(bf16[128,1024]{1,0:T(8,128)(2,1)} %get-tuple-element.156.first_ref, bf16[384,1024]{1,0:T(8,128)(2,1)} %get-tuple-element.157.other_ref, bf16[1,512,6144]{2,1,0:T(8,128)(2,1)} %head_ref.19, f32[1,6144]{1,0:T(1,128)} %gain_ref.7, ...), custom_call_target="tpu_custom_call" | custom-call | flops 1 | bytes 1 | tf_op jit(solution)/shard_map/own_table/pallas_call | solution.py:287
  204.3 5.7 %join.3 = (bf16[128,6144]{1,0:T(8,128)(2,1)}, bf16[128,6144]{1,0:T(8,128)(2,1)}, bf16[128,6144]{1,0:T(8,128)(2,1)}) custom-call(bf16[128,6144]{1,0:T(8,128)(2,1)} %get-tuple-element.177.refs_0_, bf16[128,6144]{1,0:T(8,128)(2,1)} %get-tuple-element.178.refs_1_, bf16[128,6144]{1,0:T(8,128)(2,1)} %get-tuple-element.179.refs_2_, ...), custom_call_target="tpu_custom_call" | custom-call | flops 1 | bytes 1 | tf_op jit(solution)/shard_map/join/pallas_call | solution.py:402
  228.2 10.5 %collective-permute-done.28.other_ref = bf16[384,2304]{1,0:T(8,128)(2,1)} collective-permute-done((bf16[384,2304]{1,0:T(8,128)(2,1)}, bf16[384,2304]{1,0:T(8,128)(2,1)}, u32[]{:S(2)}, u32[]{:S(2)}) %collective-permute-start.28) | collective-permute-done | bytes 1769504 | tf_op jit(solution)/shard_map/ppermute | solution.py:476
  242.7 5.4 %partials.7.refs_0_ = bf16[128,6144]{1,0:T(8,128)(2,1)} custom-call(bf16[1,512,6144]{2,1,0:T(8,128)(2,1)} %head_ref.19, bf16[1024,128]{1,0:T(8,128)(2,1)} %get-tuple-element.185.refs_0_.refs_1_.refs_2_.refs_3_.refs_4_.refs_5_, bf16[1024,128]{1,0:T(8,128)(2,1)} %get-tuple-element.185.refs_0_.refs_1_.refs_2_.refs_3_.refs_4_.refs_5_, ...), custom_call_target="tpu_custom_call" | custom-call | flops 1 | bytes 1 | tf_op jit(solution)/shard_map/partials/pallas_call | solution.py:364
  252.3 6.0 %states_gradient.1 = bf16[128,6144]{1,0:T(8,128)(2,1)} custom-call(bf16[128,6144]{1,0:T(8,128)(2,1)} %hidden_ref.5, f32[128,128]{1,0:T(8,128)} %pad_maximum_fusion.scale_ref, f32[1,6144]{1,0:T(1,128)} %gain_ref.7, bf16[128,6144]{1,0:T(8,128)(2,1)} %partials.7.refs_0_, bf16[128,6144]{1,0:T(8,128)(2,1)} %collective-permute-done.29.refs_1_, ...), custom_call_target="tpu_custom_call" | custom-call | flops 1 | bytes 1 | tf_op jit(solution)/shard_map/states_gradient/pallas_call | solution.py:431
  (117 shorter events, 105.0 us)
Async XLA Ops:
  2.9 20.0 %collective-permute-start = (bf16[64,6144]{1,0:T(8,128)(2,1)}, bf16[64,6144]{1,0:T(8,128)(2,1)}, u32[]{:S(2)}, u32[]{:S(2)}) collective-permute-start(bf16[64,6144]{1,0:T(8,128)(2,1)} %get-tuple-element.103.refs_0_.refs_8_), channel_id=1, source_target_pairs={{0,1},{1,0},{2,3},{3,2},{4,5},{5,4},{6,7},{7,6},{8,9},{9,8},{10,11... | collective-permute-start | bytes 2359304 | tf_op jit(solution)/shard_map/ppermute | solution.py:473
  5.4 19.8 %collective-permute-start.1 = (bf16[64,6144]{1,0:T(8,128)(2,1)}, bf16[64,6144]{1,0:T(8,128)(2,1)}, u32[]{:S(2)}, u32[]{:S(2)}) collective-permute-start(bf16[64,6144]{1,0:T(8,128)(2,1)} %get-tuple-element.103.refs_0_.refs_8_), channel_id=1, source_target_pairs={{0,2},{1,3},{2,4},{3,5},{4,6},{5,7},{6,0},{7,1},{8,10},{9,11},{10,... | collective-permute-start | bytes 2359304 | tf_op jit(solution)/shard_map/ppermute | solution.py:473
  10.4 31.7 %collective-permute-start.3 = (bf16[64,6144]{1,0:T(8,128)(2,1)}, bf16[64,6144]{1,0:T(8,128)(2,1)}, u32[]{:S(2)}, u32[]{:S(2)}) collective-permute-start(bf16[64,6144]{1,0:T(8,128)(2,1)} %get-tuple-element.109.refs_1_.refs_9_), channel_id=1, source_target_pairs={{0,2},{1,3},{2,4},{3,5},{4,6},{5,7},{6,0},{7,1},{8,10},{9,11},{10,... | collective-permute-start | bytes 2359304 | tf_op jit(solution)/shard_map/ppermute | solution.py:473
  10.4 31.7 %collective-permute-start.5 = (bf16[64,6144]{1,0:T(8,128)(2,1)}, bf16[64,6144]{1,0:T(8,128)(2,1)}, u32[]{:S(2)}, u32[]{:S(2)}) collective-permute-start(bf16[64,6144]{1,0:T(8,128)(2,1)} %get-tuple-element.109.refs_1_.refs_9_), channel_id=1, source_target_pairs={{0,6},{1,7},{2,0},{3,1},{4,2},{5,3},{6,4},{7,5},{8,14},{9,15},{10,... | collective-permute-start | bytes 2359304 | tf_op jit(solution)/shard_map/ppermute | solution.py:473
  30.6 30.6 %collective-permute-start.4 = (bf16[64,6144]{1,0:T(8,128)(2,1)}, bf16[64,6144]{1,0:T(8,128)(2,1)}, u32[]{:S(2)}, u32[]{:S(2)}) collective-permute-start(bf16[64,6144]{1,0:T(8,128)(2,1)} %collective-permute-done.refs_4_.refs_0_.refs_8_), channel_id=1, source_target_pairs={{0,2},{1,3},{2,4},{3,5},{4,6},{5,7},{6,0},{7,1},{8,10},{9,11},{10,... | collective-permute-start | bytes 2359304 | tf_op jit(solution)/shard_map/ppermute | solution.py:473
  31.4 29.8 %collective-permute-start.8 = (bf16[64,6144]{1,0:T(8,128)(2,1)}, bf16[64,6144]{1,0:T(8,128)(2,1)}, u32[]{:S(2)}, u32[]{:S(2)}) collective-permute-start(bf16[64,6144]{1,0:T(8,128)(2,1)} %collective-permute-done.refs_4_.refs_0_.refs_8_), channel_id=1, source_target_pairs={{0,6},{1,7},{2,0},{3,1},{4,2},{5,3},{6,4},{7,5},{8,14},{9,15},{10,... | collective-permute-start | bytes 2359304 | tf_op jit(solution)/shard_map/ppermute | solution.py:473
  42.0 19.2 %collective-permute-start.7 = (bf16[64,6144]{1,0:T(8,128)(2,1)}, bf16[64,6144]{1,0:T(8,128)(2,1)}, u32[]{:S(2)}, u32[]{:S(2)}) collective-permute-start(bf16[64,6144]{1,0:T(8,128)(2,1)} %collective-permute-done.5.refs_3_.refs_11_), channel_id=1, source_target_pairs={{0,1},{1,0},{2,3},{3,2},{4,5},{5,4},{6,7},{7,6},{8,9},{9,8},{10,11... | collective-permute-start | bytes 2359304 | tf_op jit(solution)/shard_map/ppermute | solution.py:473
  50.6 25.1 %collective-permute-start.12 = (bf16[64,6144]{1,0:T(8,128)(2,1)}, bf16[64,6144]{1,0:T(8,128)(2,1)}, u32[]{:S(2)}, u32[]{:S(2)}) collective-permute-start(bf16[64,6144]{1,0:T(8,128)(2,1)} %collective-permute-done.5.refs_3_.refs_11_), channel_id=1, source_target_pairs={{0,6},{1,7},{2,0},{3,1},{4,2},{5,3},{6,4},{7,5},{8,14},{9,15},{10,... | collective-permute-start | bytes 2359304 | tf_op jit(solution)/shard_map/ppermute | solution.py:473
  53.0 22.6 %collective-permute-start.11 = (bf16[64,6144]{1,0:T(8,128)(2,1)}, bf16[64,6144]{1,0:T(8,128)(2,1)}, u32[]{:S(2)}, u32[]{:S(2)}) collective-permute-start(bf16[64,6144]{1,0:T(8,128)(2,1)} %collective-permute-done.1.refs_0_.refs_14_.refs_6_), channel_id=1, source_target_pairs={{0,2},{1,3},{2,4},{3,5},{4,6},{5,7},{6,0},{7,1},{8,10},{9,11},{10,... | collective-permute-start | bytes 2359304 | tf_op jit(solution)/shard_map/ppermute | solution.py:473
  62.3 30.2 %collective-permute-start.9 = (bf16[64,6144]{1,0:T(8,128)(2,1)}, bf16[64,6144]{1,0:T(8,128)(2,1)}, u32[]{:S(2)}, u32[]{:S(2)}) collective-permute-start(bf16[64,6144]{1,0:T(8,128)(2,1)} %collective-permute-done.4.refs_2_.refs_6_.refs_14_), channel_id=1, source_target_pairs={{0,2},{1,3},{2,4},{3,5},{4,6},{5,7},{6,0},{7,1},{8,10},{9,11},{10,... | collective-permute-start | bytes 2359304 | tf_op jit(solution)/shard_map/ppermute | solution.py:473
  62.3 30.1 %collective-permute-start.10 = (bf16[64,6144]{1,0:T(8,128)(2,1)}, bf16[64,6144]{1,0:T(8,128)(2,1)}, u32[]{:S(2)}, u32[]{:S(2)}) collective-permute-start(bf16[64,6144]{1,0:T(8,128)(2,1)} %collective-permute-done.7.refs_1_.refs_3_.refs_11_), channel_id=1, source_target_pairs={{0,6},{1,7},{2,0},{3,1},{4,2},{5,3},{6,4},{7,5},{8,14},{9,15},{10,... | collective-permute-start | bytes 2359304 | tf_op jit(solution)/shard_map/ppermute | solution.py:473
  123.3 37.6 %collective-permute-start.22 = (bf16[128,4608]{1,0:T(8,128)(2,1)}, bf16[128,4608]{1,0:T(8,128)(2,1)}, u32[]{:S(2)}, u32[]{:S(2)}) collective-permute-start(bf16[128,4608]{1,0:T(8,128)(2,1)} %table_part.5), channel_id=1, source_target_pairs={{0,121},{1,120},{2,123},{3,122},{4,125},{5,124},{6,127},{7,126},{8... | collective-permute-start | bytes 3538952 | tf_op jit(solution)/shard_map/ppermute | solution.py:476
  139.9 20.4 %collective-permute-start.20 = (bf16[64,6144]{1,0:T(8,128)(2,1)}, bf16[64,6144]{1,0:T(8,128)(2,1)}, u32[]{:S(2)}, u32[]{:S(2)}) collective-permute-start(bf16[64,6144]{1,0:T(8,128)(2,1)} %get-tuple-element.139), channel_id=1, source_target_pairs={{0,6},{1,7},{2,0},{3,1},{4,2},{5,3},{6,4},{7,5},{8,14},{9,15},{10,... | collective-permute-start | bytes 2359304 | tf_op jit(solution)/shard_map/ppermute | solution.py:473
  139.9 20.4 %collective-permute-start.21 = (bf16[64,6144]{1,0:T(8,128)(2,1)}, bf16[64,6144]{1,0:T(8,128)(2,1)}, u32[]{:S(2)}, u32[]{:S(2)}) collective-permute-start(bf16[64,6144]{1,0:T(8,128)(2,1)} %get-tuple-element.146), channel_id=1, source_target_pairs={{0,2},{1,3},{2,4},{3,5},{4,6},{5,7},{6,0},{7,1},{8,10},{9,11},{10,... | collective-permute-start | bytes 2359304 | tf_op jit(solution)/shard_map/ppermute | solution.py:473
  155.8 48.3 %collective-permute-start.23 = (bf16[384,2304]{1,0:T(8,128)(2,1)}, bf16[384,2304]{1,0:T(8,128)(2,1)}, u32[]{:S(2)}, u32[]{:S(2)}) collective-permute-start(bf16[384,2304]{1,0:T(8,128)(2,1)} %table_part.6), channel_id=1, source_target_pairs={{0,121},{1,120},{2,123},{3,122},{4,125},{5,124},{6,127},{7,126},{8... | collective-permute-start | bytes 5308424 | tf_op jit(solution)/shard_map/ppermute | solution.py:476
  164.6 39.6 %collective-permute-start.24 = (bf16[128,6144]{1,0:T(8,128)(2,1)}, bf16[128,6144]{1,0:T(8,128)(2,1)}, u32[]{:S(2)}, u32[]{:S(2)}) collective-permute-start(bf16[128,6144]{1,0:T(8,128)(2,1)} %get-tuple-element.155), channel_id=1, source_target_pairs={{0,6},{1,7},{2,0},{3,1},{4,2},{5,3},{6,4},{7,5},{8,14},{9,15},{10,... | collective-permute-start | bytes 4718600 | tf_op jit(solution)/shard_map/ppermute | solution.py:473
  164.6 39.6 %collective-permute-start.25 = (bf16[128,6144]{1,0:T(8,128)(2,1)}, bf16[128,6144]{1,0:T(8,128)(2,1)}, u32[]{:S(2)}, u32[]{:S(2)}) collective-permute-start(bf16[128,6144]{1,0:T(8,128)(2,1)} %get-tuple-element.170), channel_id=1, source_target_pairs={{0,2},{1,3},{2,4},{3,5},{4,6},{5,7},{6,0},{7,1},{8,10},{9,11},{10,... | collective-permute-start | bytes 4718600 | tf_op jit(solution)/shard_map/ppermute | solution.py:473
  166.0 38.1 %collective-permute-start.26 = (bf16[128,6144]{1,0:T(8,128)(2,1)}, bf16[128,6144]{1,0:T(8,128)(2,1)}, u32[]{:S(2)}, u32[]{:S(2)}) collective-permute-start(bf16[128,6144]{1,0:T(8,128)(2,1)} %get-tuple-element.171), channel_id=1, source_target_pairs={{0,1},{1,0},{2,3},{3,2},{4,5},{5,4},{6,7},{7,6},{8,9},{9,8},{10,11... | collective-permute-start | bytes 4718600 | tf_op jit(solution)/shard_map/ppermute | solution.py:473
  171.9 66.8 %collective-permute-start.28 = (bf16[384,2304]{1,0:T(8,128)(2,1)}, bf16[384,2304]{1,0:T(8,128)(2,1)}, u32[]{:S(2)}, u32[]{:S(2)}) collective-permute-start(bf16[384,2304]{1,0:T(8,128)(2,1)} %table_part.8), channel_id=1, source_target_pairs={{0,121},{1,120},{2,123},{3,122},{4,125},{5,124},{6,127},{7,126},{8... | collective-permute-start | bytes 5308424 | tf_op jit(solution)/shard_map/ppermute | solution.py:476
  210.8 41.4 %collective-permute-start.29 = (bf16[128,6144]{1,0:T(8,128)(2,1)}, bf16[128,6144]{1,0:T(8,128)(2,1)}, u32[]{:S(2)}, u32[]{:S(2)}) collective-permute-start(bf16[128,6144]{1,0:T(8,128)(2,1)} %get-tuple-element.184), channel_id=1, source_target_pairs={{0,6},{1,7},{2,0},{3,1},{4,2},{5,3},{6,4},{7,5},{8,14},{9,15},{10,... | collective-permute-start | bytes 4718600 | tf_op jit(solution)/shard_map/ppermute | solution.py:473
  212.3 39.9 %collective-permute-start.30 = (bf16[128,6144]{1,0:T(8,128)(2,1)}, bf16[128,6144]{1,0:T(8,128)(2,1)}, u32[]{:S(2)}, u32[]{:S(2)}) collective-permute-start(bf16[128,6144]{1,0:T(8,128)(2,1)} %get-tuple-element.189), channel_id=1, source_target_pairs={{0,2},{1,3},{2,4},{3,5},{4,6},{5,7},{6,0},{7,1},{8,10},{9,11},{10,... | collective-permute-start | bytes 4718600 | tf_op jit(solution)/shard_map/ppermute | solution.py:473
  212.3 39.9 %collective-permute-start.31 = (bf16[128,6144]{1,0:T(8,128)(2,1)}, bf16[128,6144]{1,0:T(8,128)(2,1)}, u32[]{:S(2)}, u32[]{:S(2)}) collective-permute-start(bf16[128,6144]{1,0:T(8,128)(2,1)} %get-tuple-element.190), channel_id=1, source_target_pairs={{0,1},{1,0},{2,3},{3,2},{4,5},{5,4},{6,7},{7,6},{8,9},{9,8},{10,11... | collective-permute-start | bytes 4718600 | tf_op jit(solution)/shard_map/ppermute | solution.py:473
  213.7 53.4 %collective-permute-start.33 = (bf16[384,1536]{1,0:T(8,128)(2,1)}, bf16[384,1536]{1,0:T(8,128)(2,1)}, u32[]{:S(2)}, u32[]{:S(2)}) collective-permute-start(bf16[384,1536]{1,0:T(8,128)(2,1)} %table_part.7), channel_id=1, source_target_pairs={{0,121},{1,120},{2,123},{3,122},{4,125},{5,124},{6,127},{7,126},{8... | collective-permute-start | bytes 3538952 | tf_op jit(solution)/shard_map/ppermute | solution.py:476
  238.7 32.7 %collective-permute-start.32 = (bf16[128,1536]{1,0:T(8,128)(2,1)}, bf16[128,1536]{1,0:T(8,128)(2,1)}, u32[]{:S(2)}, u32[]{:S(2)}) collective-permute-start(bf16[128,1536]{1,0:T(8,128)(2,1)} %table_part.9), channel_id=1, source_target_pairs={{0,121},{1,120},{2,123},{3,122},{4,125},{5,124},{6,127},{7,126},{8... | collective-permute-start | bytes 1179656 | tf_op jit(solution)/shard_map/ppermute | solution.py:476
  (22 other events, 273.9 us)

commit v6 on v5

--- a/solution.py
+++ b/solution.py
@@ -602,7 +602,7 @@
     merged = None
     for n in range(2):
         merged = add_part(own, theirs[n], merged, PARTS[n])
-    parts[4] = gate((parts[4],), theirs[2], merged)
+    parts[4] = gate((parts[4],), theirs[2], merged, mine)
     theirs.append(exchange(parts[4]))
     merged = add_part(own, theirs[2], merged, PARTS[2])
 
@@ -622,7 +622,7 @@
     )
     merged_gain = (ours.astype(F32) + mirrored.astype(BF16).astype(F32)).astype(BF16)
     merged_gain = merged_gain.reshape(1, depth)
-    theirs[4], merged = gate((theirs[4], merged), grad_states)
+    theirs[4], merged, merged_gain = gate((theirs[4], merged, merged_gain), grad_states)
     merged = add_part(own, theirs[4], merged, PARTS[4])
     return (own_loss, grad_states, merged, merged_gain)
 

time: 277 us -> 277 us (level)
    ppermute x5, waiting for transfers between devices: 12 us -> 5.79 us  [exchange(): return lax.ppermute(x, ('pipe', 'fsdp'), facing)]
    ppermute x1, waiting for transfers between devices: 0.01 us -> 3.22 us  [body(): lax.ppermute(along, 'pipe', mirror)]
    ppermute x1, starting transfers between devices: 2.47 us -> 5.5 us  [body(): lax.ppermute(along, 'pipe', mirror)]
  transfers between devices with their start and end apart: 38 -> 38, of which waited for: 14 -> 16; matrix products, arithmetic and copies ran while one was open for 3% -> 3% of each run, Pallas kernels for 50% -> 49%
where the time goes in v6:
time: 277 us; the launch traced here: 275 us
  Pallas kernels  154 us (56%)
  starting transfers between devices  61.6 us (22%)
  waiting for transfers between devices  48.7 us (18%)
  other arithmetic  5.54 us (2%)
  local copies, waits for them, and re-layouts  4.58 us (2%)
    ppermute x31, waiting for transfers between devices, send(): return lax.ppermute(x, 'fsdp', perm)  39.1 us
    pallas_call x5, Pallas kernels, block_logits(): pl.pallas_call(functools.partial(logits_kernel, slots, earlier), grid=(de...  29.6 us
    ppermute x31, starting transfers between devices, send(): return lax.ppermute(x, 'fsdp', perm)  28 us
    pallas_call x5, Pallas kernels, table_part(): pl.pallas_call(part_kernel, grid=(size // step,), in_specs=[pl.BlockSpec(...  26.3 us
    ppermute x5, starting transfers between devices, exchange(): return lax.ppermute(x, ('pipe', 'fsdp'), facing)  25.4 us
    pallas_call x4, Pallas kernels, partials(): pl.pallas_call(functools.partial(partial_kernel, counts), grid=(depth //...  25.1 us
    pallas_call x5, Pallas kernels, add_part(): pl.pallas_call(add_kernel, grid=(num_rows, num_columns // wide), in_specs...  17.1 us
    pallas_call x2, Pallas kernels, teacher_weights(): pl.pallas_call(functools.partial(teacher_kernel, rest), grid_spec=pltpu.P...  15.3 us
  transfers between devices with their start and end apart: 38, of which 16 were waited for; matrix products, arithmetic and copies ran while one was open for 3% of the time, Pallas kernels for 49%

profile of v6, /device:TPU:1, one launch (start us, length us, event | category | flops | bytes accessed | tf_op | source)
XLA Modules:
  0.0 275.1 jit_solution(4317072756052281792)
XLA Ops:
  13.6 7.6 %teacher_weights.2.refs_2_.refs_6_.refs_7_.refs_4_.refs_0_ = f32[4,512,128]{2,1,0:T(8,128)} custom-call(s32[4]{0:T(128)} %bitcast.31, s32[1]{0:T(128)} %bitcast.2.base_ref, s32[64,1024]{1,0:T(8,128)} %bitcast.20, f32[64,1024]{1,0:T(8,128)} %bitcast.22), custom_call_target="tpu_custom_call" | custom-call | flops 1 | bytes 1 | tf_op jit(solution)/shard_map/teacher_weights/pallas_call | solution.py:91
  25.5 5.1 %block_logits.5 = (f32[1,512,128]{2,1,0:T(8,128)}, f32[24,128]{1,0:T(8,128)}) custom-call(bf16[1,512,6144]{2,1,0:T(8,128)(2,1)} %head_ref.19, bf16[64,6144]{1,0:T(8,128)(2,1)} %get-tuple-element.104.refs_0_.refs_8_, bf16[64,6144]{1,0:T(8,128)(2,1)} %get-tuple-element.110.refs_1_.refs_9_, f32[4,512,128]{2,1,0:T(8,128)} %teacher_weights.2.refs_2_.refs_6_.refs_7_.refs_4_.refs_0_), custom_call_target="tpu_custom_call" | custom-call | flops 1 | bytes 1 | tf_op jit(solution)/shard_map/block_logits/pallas_call | solution.py:151
  33.3 8.7 %collective-permute-done.3.refs_1_.refs_15_.refs_7_ = bf16[64,6144]{1,0:T(8,128)(2,1)} collective-permute-done((bf16[64,6144]{1,0:T(8,128)(2,1)}, bf16[64,6144]{1,0:T(8,128)(2,1)}, u32[]{:S(2)}, u32[]{:S(2)}) %collective-permute-start.3) | collective-permute-done | bytes 786464 | tf_op jit(solution)/shard_map/ppermute | solution.py:473
  42.9 7.6 %teacher_weights.3.refs_8_.refs_2_.refs_5_.refs_1_ = f32[4,512,128]{2,1,0:T(8,128)} custom-call(s32[4]{0:T(128)} %slice.58.order_ref, s32[1]{0:T(128)} %bitcast.2.base_ref, s32[64,1024]{1,0:T(8,128)} %bitcast.21, f32[64,1024]{1,0:T(8,128)} %bitcast.23), custom_call_target="tpu_custom_call" | custom-call | flops 1 | bytes 1 | tf_op jit(solution)/shard_map/teacher_weights/pallas_call | solution.py:91
  53.0 8.2 %block_logits.6 = (f32[3,512,128]{2,1,0:T(8,128)}, f32[24,128]{1,0:T(8,128)}) custom-call(bf16[1,512,6144]{2,1,0:T(8,128)(2,1)} %head_ref.19, bf16[64,6144]{1,0:T(8,128)(2,1)} %collective-permute-done.1.refs_0_.refs_14_.refs_6_, bf16[64,6144]{1,0:T(8,128)(2,1)} %collective-permute-done.3.refs_1_.refs_15_.refs_7_, ...), custom_call_target="tpu_custom_call" | custom-call | flops 1 | bytes 1 | tf_op jit(solution)/shard_map/block_logits/pallas_call | solution.py:151
  65.0 5.2 %block_logits.7 = (f32[1,512,128]{2,1,0:T(8,128)}, f32[24,128]{1,0:T(8,128)}) custom-call(bf16[1,512,6144]{2,1,0:T(8,128)(2,1)} %head_ref.19, bf16[64,6144]{1,0:T(8,128)(2,1)} %collective-permute-done.8.refs_0_.refs_2_.refs_10_, bf16[64,6144]{1,0:T(8,128)(2,1)} %collective-permute-done.7.refs_1_.refs_3_.refs_11_, ...), custom_call_target="tpu_custom_call" | custom-call | flops 1 | bytes 1 | tf_op jit(solution)/shard_map/block_logits/pallas_call | solution.py:151
  70.1 5.5 %collective-permute-done.11.refs_0_.refs_12_.refs_4_ = bf16[64,6144]{1,0:T(8,128)(2,1)} collective-permute-done((bf16[64,6144]{1,0:T(8,128)(2,1)}, bf16[64,6144]{1,0:T(8,128)(2,1)}, u32[]{:S(2)}, u32[]{:S(2)}) %collective-permute-start.11) | collective-permute-done | bytes 786464 | tf_op jit(solution)/shard_map/ppermute | solution.py:473
  76.7 5.9 %block_logits.8 = (f32[2,512,128]{2,1,0:T(8,128)}, f32[24,128]{1,0:T(8,128)}) custom-call(bf16[1,512,6144]{2,1,0:T(8,128)(2,1)} %head_ref.19, bf16[64,6144]{1,0:T(8,128)(2,1)} %collective-permute-done.11.refs_0_.refs_12_.refs_4_, bf16[64,6144]{1,0:T(8,128)(2,1)} %collective-permute-done.12.refs_1_.refs_13_.refs_5_, ...), custom_call_target="tpu_custom_call" | custom-call | flops 1 | bytes 1 | tf_op jit(solution)/shard_map/block_logits/pallas_call | solution.py:151
  82.6 9.9 %collective-permute-done.9.refs_0_.refs_4_.refs_12_ = bf16[64,6144]{1,0:T(8,128)(2,1)} collective-permute-done((bf16[64,6144]{1,0:T(8,128)(2,1)}, bf16[64,6144]{1,0:T(8,128)(2,1)}, u32[]{:S(2)}, u32[]{:S(2)}) %collective-permute-start.9) | collective-permute-done | bytes 786464 | tf_op jit(solution)/shard_map/ppermute | solution.py:473
  92.5 5.2 %block_logits.9 = (f32[1,512,128]{2,1,0:T(8,128)}, f32[24,128]{1,0:T(8,128)}) custom-call(bf16[1,512,6144]{2,1,0:T(8,128)(2,1)} %head_ref.19, bf16[64,6144]{1,0:T(8,128)(2,1)} %collective-permute-done.9.refs_0_.refs_4_.refs_12_, bf16[64,6144]{1,0:T(8,128)(2,1)} %collective-permute-done.10.refs_1_.refs_5_.refs_13_, ...), custom_call_target="tpu_custom_call" | custom-call | flops 1 | bytes 1 | tf_op jit(solution)/shard_map/block_logits/pallas_call | solution.py:151
  116.2 7.2 %table_part.5 = bf16[128,4608]{1,0:T(8,128)(2,1)} custom-call(bf16[128,1024]{1,0:T(8,128)(2,1)} %collective-permute-done.18.low_ref, bf16[64,6144]{1,0:T(8,128)(2,1)} %collective-permute-done.refs_4_.refs_0_.refs_8_, bf16[64,6144]{1,0:T(8,128)(2,1)} %collective-permute-done.6.refs_5_.refs_1_.refs_9_, ...), custom_call_target="tpu_custom_call" | custom-call | flops 1 | bytes 1 | tf_op jit(solution)/shard_map/table_part/pallas_call | solution.py:259
  123.4 10.5 %collective-permute-start.22 = (bf16[128,4608]{1,0:T(8,128)(2,1)}, bf16[128,4608]{1,0:T(8,128)(2,1)}, u32[]{:S(2)}, u32[]{:S(2)}) collective-permute-start(bf16[128,4608]{1,0:T(8,128)(2,1)} %table_part.5), channel_id=1, source_target_pairs={{0,121},{1,120},{2,123},{3,122},{4,125},{5,124},{6,127},{7,126},{8... | collective-permute-start | bytes 3538952 | tf_op jit(solution)/shard_map/ppermute | solution.py:476
  134.6 5.3 %partials.4 = (bf16[64,6144]{1,0:T(8,128)(2,1)}, bf16[64,6144]{1,0:T(8,128)(2,1)}) custom-call(bf16[1,512,6144]{2,1,0:T(8,128)(2,1)} %head_ref.19, bf16[1024,128]{1,0:T(8,128)(2,1)} %get-tuple-element.186.refs_0_.refs_1_.refs_2_.refs_3_.refs_4_.refs_5_, bf16[1024,128]{1,0:T(8,128)(2,1)} %get-tuple-element.186.refs_0_.refs_1_.refs_2_.refs_3_.refs_4_.refs_5_, ...), custom_call_target="tpu_custom_call" | custom-call | flops 1 | bytes 1 | tf_op jit(solution)/shard_map/partials/pallas_call | solution.py:364
  141.4 7.2 %partials.5 = (bf16[128,6144]{1,0:T(8,128)(2,1)}, bf16[128,6144]{1,0:T(8,128)(2,1)}, bf16[128,6144]{1,0:T(8,128)(2,1)}) custom-call(bf16[1,512,6144]{2,1,0:T(8,128)(2,1)} %head_ref.19, bf16[1024,128]{1,0:T(8,128)(2,1)} %get-tuple-element.186.refs_0_.refs_1_.refs_2_.refs_3_.refs_4_.refs_5_, ...), custom_call_target="tpu_custom_call" | custom-call | flops 1 | bytes 1 | tf_op jit(solution)/shard_map/partials/pallas_call | solution.py:364
  150.0 5.8 %table_part.6 = bf16[384,2304]{1,0:T(8,128)(2,1)} custom-call(bf16[384,1024]{1,0:T(8,128)(2,1)} %collective-permute-done.19.low_ref, bf16[64,6144]{1,0:T(8,128)(2,1)} %collective-permute-done.refs_4_.refs_0_.refs_8_, bf16[64,6144]{1,0:T(8,128)(2,1)} %collective-permute-done.6.refs_5_.refs_1_.refs_9_, ...), custom_call_target="tpu_custom_call" | custom-call | flops 1 | bytes 1 | tf_op jit(solution)/shard_map/table_part/pallas_call | solution.py:259
  155.9 4.5 %collective-permute-start.23 = (bf16[384,2304]{1,0:T(8,128)(2,1)}, bf16[384,2304]{1,0:T(8,128)(2,1)}, u32[]{:S(2)}, u32[]{:S(2)}) collective-permute-start(bf16[384,2304]{1,0:T(8,128)(2,1)} %table_part.6), channel_id=1, source_target_pairs={{0,121},{1,120},{2,123},{3,122},{4,125},{5,124},{6,127},{7,126},{8... | collective-permute-start | bytes 5308424 | tf_op jit(solution)/shard_map/ppermute | solution.py:476
  167.5 5.9 %table_part.8 = bf16[384,2304]{1,0:T(8,128)(2,1)} custom-call(bf16[384,1024]{1,0:T(8,128)(2,1)} %collective-permute-done.19.low_ref, bf16[64,6144]{1,0:T(8,128)(2,1)} %collective-permute-done.refs_4_.refs_0_.refs_8_, bf16[64,6144]{1,0:T(8,128)(2,1)} %collective-permute-done.6.refs_5_.refs_1_.refs_9_, ...), custom_call_target="tpu_custom_call" | custom-call | flops 1 | bytes 1 | tf_op jit(solution)/shard_map/table_part/pallas_call | solution.py:259
  177.2 7.2 %partials.6 = (bf16[128,6144]{1,0:T(8,128)(2,1)}, bf16[128,6144]{1,0:T(8,128)(2,1)}, bf16[128,6144]{1,0:T(8,128)(2,1)}) custom-call(bf16[1,512,6144]{2,1,0:T(8,128)(2,1)} %head_ref.19, bf16[1024,128]{1,0:T(8,128)(2,1)} %get-tuple-element.186.refs_0_.refs_1_.refs_2_.refs_3_.refs_4_.refs_5_, ...), custom_call_target="tpu_custom_call" | custom-call | flops 1 | bytes 1 | tf_op jit(solution)/shard_map/partials/pallas_call | solution.py:364
  188.6 14.6 %own_table.1 = (bf16[512,6144]{1,0:T(8,128)(2,1)}, f32[8,6144]{1,0:T(8,128)}) custom-call(bf16[128,1024]{1,0:T(8,128)(2,1)} %get-tuple-element.157.first_ref, bf16[384,1024]{1,0:T(8,128)(2,1)} %get-tuple-element.158.other_ref, bf16[1,512,6144]{2,1,0:T(8,128)(2,1)} %head_ref.19, f32[1,6144]{1,0:T(1,128)} %gain_ref.7, ...), custom_call_target="tpu_custom_call" | custom-call | flops 1 | bytes 1 | tf_op jit(solution)/shard_map/own_table/pallas_call | solution.py:287
  204.4 5.7 %join.3 = (bf16[128,6144]{1,0:T(8,128)(2,1)}, bf16[128,6144]{1,0:T(8,128)(2,1)}, bf16[128,6144]{1,0:T(8,128)(2,1)}) custom-call(bf16[128,6144]{1,0:T(8,128)(2,1)} %get-tuple-element.178.refs_0_, bf16[128,6144]{1,0:T(8,128)(2,1)} %get-tuple-element.179.refs_1_, bf16[128,6144]{1,0:T(8,128)(2,1)} %get-tuple-element.180.refs_2_, ...), custom_call_target="tpu_custom_call" | custom-call | flops 1 | bytes 1 | tf_op jit(solution)/shard_map/join/pallas_call | solution.py:402
  225.1 5.4 %partials.7.refs_0_ = bf16[128,6144]{1,0:T(8,128)(2,1)} custom-call(bf16[1,512,6144]{2,1,0:T(8,128)(2,1)} %head_ref.19, bf16[1024,128]{1,0:T(8,128)(2,1)} %get-tuple-element.186.refs_0_.refs_1_.refs_2_.refs_3_.refs_4_.refs_5_, bf16[1024,128]{1,0:T(8,128)(2,1)} %get-tuple-element.186.refs_0_.refs_1_.refs_2_.refs_3_.refs_4_.refs_5_, ...), custom_call_target="tpu_custom_call" | custom-call | flops 1 | bytes 1 | tf_op jit(solution)/shard_map/partials/pallas_call | solution.py:364
  233.6 5.1 %collective-permute-done.28.other_ref = bf16[384,2304]{1,0:T(8,128)(2,1)} collective-permute-done((bf16[384,2304]{1,0:T(8,128)(2,1)}, bf16[384,2304]{1,0:T(8,128)(2,1)}, u32[]{:S(2)}, u32[]{:S(2)}) %collective-permute-start.28) | collective-permute-done | bytes 1769504 | tf_op jit(solution)/shard_map/ppermute | solution.py:476
  249.3 6.0 %states_gradient.1 = bf16[128,6144]{1,0:T(8,128)(2,1)} custom-call(bf16[128,6144]{1,0:T(8,128)(2,1)} %hidden_ref.5, f32[128,128]{1,0:T(8,128)} %pad_maximum_fusion.scale_ref, f32[1,6144]{1,0:T(1,128)} %gain_ref.7, bf16[128,6144]{1,0:T(8,128)(2,1)} %partials.7.refs_0_, bf16[128,6144]{1,0:T(8,128)(2,1)} %collective-permute-done.29.refs_1_, ...), custom_call_target="tpu_custom_call" | custom-call | flops 1 | bytes 1 | tf_op jit(solution)/shard_map/states_gradient/pallas_call | solution.py:431
  256.0 5.5 %collective-permute-start.36 = (f32[8,768]{1,0:T(8,128)S(1)}, f32[8,768]{1,0:T(8,128)S(1)}, u32[]{:S(2)}, u32[]{:S(2)}) collective-permute-start(f32[8,768]{1,0:T(8,128)S(1)} %add.147), channel_id=1, source_target_pairs={{0,120},{8,112},{16,104},{24,96},{32,88},{40,80},{48,72},{56,64},{... | collective-permute-start | bytes 73736 | tf_op jit(solution)/shard_map/ppermute | solution.py:620
  (117 shorter events, 109.5 us)
Async XLA Ops:
  2.9 20.0 %collective-permute-start = (bf16[64,6144]{1,0:T(8,128)(2,1)}, bf16[64,6144]{1,0:T(8,128)(2,1)}, u32[]{:S(2)}, u32[]{:S(2)}) collective-permute-start(bf16[64,6144]{1,0:T(8,128)(2,1)} %get-tuple-element.104.refs_0_.refs_8_), channel_id=1, source_target_pairs={{0,1},{1,0},{2,3},{3,2},{4,5},{5,4},{6,7},{7,6},{8,9},{9,8},{10,11... | collective-permute-start | bytes 2359304 | tf_op jit(solution)/shard_map/ppermute | solution.py:473
  5.4 19.8 %collective-permute-start.1 = (bf16[64,6144]{1,0:T(8,128)(2,1)}, bf16[64,6144]{1,0:T(8,128)(2,1)}, u32[]{:S(2)}, u32[]{:S(2)}) collective-permute-start(bf16[64,6144]{1,0:T(8,128)(2,1)} %get-tuple-element.104.refs_0_.refs_8_), channel_id=1, source_target_pairs={{0,2},{1,3},{2,4},{3,5},{4,6},{5,7},{6,0},{7,1},{8,10},{9,11},{10,... | collective-permute-start | bytes 2359304 | tf_op jit(solution)/shard_map/ppermute | solution.py:473
  10.4 31.7 %collective-permute-start.3 = (bf16[64,6144]{1,0:T(8,128)(2,1)}, bf16[64,6144]{1,0:T(8,128)(2,1)}, u32[]{:S(2)}, u32[]{:S(2)}) collective-permute-start(bf16[64,6144]{1,0:T(8,128)(2,1)} %get-tuple-element.110.refs_1_.refs_9_), channel_id=1, source_target_pairs={{0,2},{1,3},{2,4},{3,5},{4,6},{5,7},{6,0},{7,1},{8,10},{9,11},{10,... | collective-permute-start | bytes 2359304 | tf_op jit(solution)/shard_map/ppermute | solution.py:473
  10.4 31.7 %collective-permute-start.5 = (bf16[64,6144]{1,0:T(8,128)(2,1)}, bf16[64,6144]{1,0:T(8,128)(2,1)}, u32[]{:S(2)}, u32[]{:S(2)}) collective-permute-start(bf16[64,6144]{1,0:T(8,128)(2,1)} %get-tuple-element.110.refs_1_.refs_9_), channel_id=1, source_target_pairs={{0,6},{1,7},{2,0},{3,1},{4,2},{5,3},{6,4},{7,5},{8,14},{9,15},{10,... | collective-permute-start | bytes 2359304 | tf_op jit(solution)/shard_map/ppermute | solution.py:473
  30.6 30.6 %collective-permute-start.4 = (bf16[64,6144]{1,0:T(8,128)(2,1)}, bf16[64,6144]{1,0:T(8,128)(2,1)}, u32[]{:S(2)}, u32[]{:S(2)}) collective-permute-start(bf16[64,6144]{1,0:T(8,128)(2,1)} %collective-permute-done.refs_4_.refs_0_.refs_8_), channel_id=1, source_target_pairs={{0,2},{1,3},{2,4},{3,5},{4,6},{5,7},{6,0},{7,1},{8,10},{9,11},{10,... | collective-permute-start | bytes 2359304 | tf_op jit(solution)/shard_map/ppermute | solution.py:473
  31.4 29.8 %collective-permute-start.8 = (bf16[64,6144]{1,0:T(8,128)(2,1)}, bf16[64,6144]{1,0:T(8,128)(2,1)}, u32[]{:S(2)}, u32[]{:S(2)}) collective-permute-start(bf16[64,6144]{1,0:T(8,128)(2,1)} %collective-permute-done.refs_4_.refs_0_.refs_8_), channel_id=1, source_target_pairs={{0,6},{1,7},{2,0},{3,1},{4,2},{5,3},{6,4},{7,5},{8,14},{9,15},{10,... | collective-permute-start | bytes 2359304 | tf_op jit(solution)/shard_map/ppermute | solution.py:473
  42.0 19.2 %collective-permute-start.7 = (bf16[64,6144]{1,0:T(8,128)(2,1)}, bf16[64,6144]{1,0:T(8,128)(2,1)}, u32[]{:S(2)}, u32[]{:S(2)}) collective-permute-start(bf16[64,6144]{1,0:T(8,128)(2,1)} %collective-permute-done.5.refs_3_.refs_11_), channel_id=1, source_target_pairs={{0,1},{1,0},{2,3},{3,2},{4,5},{5,4},{6,7},{7,6},{8,9},{9,8},{10,11... | collective-permute-start | bytes 2359304 | tf_op jit(solution)/shard_map/ppermute | solution.py:473
  50.6 25.1 %collective-permute-start.12 = (bf16[64,6144]{1,0:T(8,128)(2,1)}, bf16[64,6144]{1,0:T(8,128)(2,1)}, u32[]{:S(2)}, u32[]{:S(2)}) collective-permute-start(bf16[64,6144]{1,0:T(8,128)(2,1)} %collective-permute-done.5.refs_3_.refs_11_), channel_id=1, source_target_pairs={{0,6},{1,7},{2,0},{3,1},{4,2},{5,3},{6,4},{7,5},{8,14},{9,15},{10,... | collective-permute-start | bytes 2359304 | tf_op jit(solution)/shard_map/ppermute | solution.py:473
  53.0 22.6 %collective-permute-start.11 = (bf16[64,6144]{1,0:T(8,128)(2,1)}, bf16[64,6144]{1,0:T(8,128)(2,1)}, u32[]{:S(2)}, u32[]{:S(2)}) collective-permute-start(bf16[64,6144]{1,0:T(8,128)(2,1)} %collective-permute-done.1.refs_0_.refs_14_.refs_6_), channel_id=1, source_target_pairs={{0,2},{1,3},{2,4},{3,5},{4,6},{5,7},{6,0},{7,1},{8,10},{9,11},{10,... | collective-permute-start | bytes 2359304 | tf_op jit(solution)/shard_map/ppermute | solution.py:473
  62.3 30.2 %collective-permute-start.9 = (bf16[64,6144]{1,0:T(8,128)(2,1)}, bf16[64,6144]{1,0:T(8,128)(2,1)}, u32[]{:S(2)}, u32[]{:S(2)}) collective-permute-start(bf16[64,6144]{1,0:T(8,128)(2,1)} %collective-permute-done.4.refs_2_.refs_6_.refs_14_), channel_id=1, source_target_pairs={{0,2},{1,3},{2,4},{3,5},{4,6},{5,7},{6,0},{7,1},{8,10},{9,11},{10,... | collective-permute-start | bytes 2359304 | tf_op jit(solution)/shard_map/ppermute | solution.py:473
  62.3 30.1 %collective-permute-start.10 = (bf16[64,6144]{1,0:T(8,128)(2,1)}, bf16[64,6144]{1,0:T(8,128)(2,1)}, u32[]{:S(2)}, u32[]{:S(2)}) collective-permute-start(bf16[64,6144]{1,0:T(8,128)(2,1)} %collective-permute-done.7.refs_1_.refs_3_.refs_11_), channel_id=1, source_target_pairs={{0,6},{1,7},{2,0},{3,1},{4,2},{5,3},{6,4},{7,5},{8,14},{9,15},{10,... | collective-permute-start | bytes 2359304 | tf_op jit(solution)/shard_map/ppermute | solution.py:473
  123.4 37.6 %collective-permute-start.22 = (bf16[128,4608]{1,0:T(8,128)(2,1)}, bf16[128,4608]{1,0:T(8,128)(2,1)}, u32[]{:S(2)}, u32[]{:S(2)}) collective-permute-start(bf16[128,4608]{1,0:T(8,128)(2,1)} %table_part.5), channel_id=1, source_target_pairs={{0,121},{1,120},{2,123},{3,122},{4,125},{5,124},{6,127},{7,126},{8... | collective-permute-start | bytes 3538952 | tf_op jit(solution)/shard_map/ppermute | solution.py:476
  140.0 20.4 %collective-permute-start.20 = (bf16[64,6144]{1,0:T(8,128)(2,1)}, bf16[64,6144]{1,0:T(8,128)(2,1)}, u32[]{:S(2)}, u32[]{:S(2)}) collective-permute-start(bf16[64,6144]{1,0:T(8,128)(2,1)} %get-tuple-element.140), channel_id=1, source_target_pairs={{0,6},{1,7},{2,0},{3,1},{4,2},{5,3},{6,4},{7,5},{8,14},{9,15},{10,... | collective-permute-start | bytes 2359304 | tf_op jit(solution)/shard_map/ppermute | solution.py:473
  140.0 20.4 %collective-permute-start.21 = (bf16[64,6144]{1,0:T(8,128)(2,1)}, bf16[64,6144]{1,0:T(8,128)(2,1)}, u32[]{:S(2)}, u32[]{:S(2)}) collective-permute-start(bf16[64,6144]{1,0:T(8,128)(2,1)} %get-tuple-element.147), channel_id=1, source_target_pairs={{0,2},{1,3},{2,4},{3,5},{4,6},{5,7},{6,0},{7,1},{8,10},{9,11},{10,... | collective-permute-start | bytes 2359304 | tf_op jit(solution)/shard_map/ppermute | solution.py:473
  155.9 48.3 %collective-permute-start.23 = (bf16[384,2304]{1,0:T(8,128)(2,1)}, bf16[384,2304]{1,0:T(8,128)(2,1)}, u32[]{:S(2)}, u32[]{:S(2)}) collective-permute-start(bf16[384,2304]{1,0:T(8,128)(2,1)} %table_part.6), channel_id=1, source_target_pairs={{0,121},{1,120},{2,123},{3,122},{4,125},{5,124},{6,127},{7,126},{8... | collective-permute-start | bytes 5308424 | tf_op jit(solution)/shard_map/ppermute | solution.py:476
  164.6 39.6 %collective-permute-start.24 = (bf16[128,6144]{1,0:T(8,128)(2,1)}, bf16[128,6144]{1,0:T(8,128)(2,1)}, u32[]{:S(2)}, u32[]{:S(2)}) collective-permute-start(bf16[128,6144]{1,0:T(8,128)(2,1)} %get-tuple-element.156), channel_id=1, source_target_pairs={{0,6},{1,7},{2,0},{3,1},{4,2},{5,3},{6,4},{7,5},{8,14},{9,15},{10,... | collective-permute-start | bytes 4718600 | tf_op jit(solution)/shard_map/ppermute | solution.py:473
  164.6 39.6 %collective-permute-start.25 = (bf16[128,6144]{1,0:T(8,128)(2,1)}, bf16[128,6144]{1,0:T(8,128)(2,1)}, u32[]{:S(2)}, u32[]{:S(2)}) collective-permute-start(bf16[128,6144]{1,0:T(8,128)(2,1)} %get-tuple-element.171), channel_id=1, source_target_pairs={{0,2},{1,3},{2,4},{3,5},{4,6},{5,7},{6,0},{7,1},{8,10},{9,11},{10,... | collective-permute-start | bytes 4718600 | tf_op jit(solution)/shard_map/ppermute | solution.py:473
  166.1 38.1 %collective-permute-start.26 = (bf16[128,6144]{1,0:T(8,128)(2,1)}, bf16[128,6144]{1,0:T(8,128)(2,1)}, u32[]{:S(2)}, u32[]{:S(2)}) collective-permute-start(bf16[128,6144]{1,0:T(8,128)(2,1)} %get-tuple-element.172), channel_id=1, source_target_pairs={{0,1},{1,0},{2,3},{3,2},{4,5},{5,4},{6,7},{7,6},{8,9},{9,8},{10,11... | collective-permute-start | bytes 4718600 | tf_op jit(solution)/shard_map/ppermute | solution.py:473
  173.4 65.4 %collective-permute-start.28 = (bf16[384,2304]{1,0:T(8,128)(2,1)}, bf16[384,2304]{1,0:T(8,128)(2,1)}, u32[]{:S(2)}, u32[]{:S(2)}) collective-permute-start(bf16[384,2304]{1,0:T(8,128)(2,1)} %table_part.8), channel_id=1, source_target_pairs={{0,121},{1,120},{2,123},{3,122},{4,125},{5,124},{6,127},{7,126},{8... | collective-permute-start | bytes 5308424 | tf_op jit(solution)/shard_map/ppermute | solution.py:476
  210.8 36.0 %collective-permute-start.29 = (bf16[128,6144]{1,0:T(8,128)(2,1)}, bf16[128,6144]{1,0:T(8,128)(2,1)}, u32[]{:S(2)}, u32[]{:S(2)}) collective-permute-start(bf16[128,6144]{1,0:T(8,128)(2,1)} %get-tuple-element.185), channel_id=1, source_target_pairs={{0,6},{1,7},{2,0},{3,1},{4,2},{5,3},{6,4},{7,5},{8,14},{9,15},{10,... | collective-permute-start | bytes 4718600 | tf_op jit(solution)/shard_map/ppermute | solution.py:473
  212.4 36.9 %collective-permute-start.30 = (bf16[128,6144]{1,0:T(8,128)(2,1)}, bf16[128,6144]{1,0:T(8,128)(2,1)}, u32[]{:S(2)}, u32[]{:S(2)}) collective-permute-start(bf16[128,6144]{1,0:T(8,128)(2,1)} %get-tuple-element.190), channel_id=1, source_target_pairs={{0,2},{1,3},{2,4},{3,5},{4,6},{5,7},{6,0},{7,1},{8,10},{9,11},{10,... | collective-permute-start | bytes 4718600 | tf_op jit(solution)/shard_map/ppermute | solution.py:473
  212.4 36.9 %collective-permute-start.31 = (bf16[128,6144]{1,0:T(8,128)(2,1)}, bf16[128,6144]{1,0:T(8,128)(2,1)}, u32[]{:S(2)}, u32[]{:S(2)}) collective-permute-start(bf16[128,6144]{1,0:T(8,128)(2,1)} %get-tuple-element.191), channel_id=1, source_target_pairs={{0,1},{1,0},{2,3},{3,2},{4,5},{5,4},{6,7},{7,6},{8,9},{9,8},{10,11... | collective-permute-start | bytes 4718600 | tf_op jit(solution)/shard_map/ppermute | solution.py:473
  213.8 50.6 %collective-permute-start.33 = (bf16[384,1536]{1,0:T(8,128)(2,1)}, bf16[384,1536]{1,0:T(8,128)(2,1)}, u32[]{:S(2)}, u32[]{:S(2)}) collective-permute-start(bf16[384,1536]{1,0:T(8,128)(2,1)} %table_part.7), channel_id=1, source_target_pairs={{0,121},{1,120},{2,123},{3,122},{4,125},{5,124},{6,127},{7,126},{8... | collective-permute-start | bytes 3538952 | tf_op jit(solution)/shard_map/ppermute | solution.py:476
  238.8 34.4 %collective-permute-start.32 = (bf16[128,1536]{1,0:T(8,128)(2,1)}, bf16[128,1536]{1,0:T(8,128)(2,1)}, u32[]{:S(2)}, u32[]{:S(2)}) collective-permute-start(bf16[128,1536]{1,0:T(8,128)(2,1)} %table_part.9), channel_id=1, source_target_pairs={{0,121},{1,120},{2,123},{3,122},{4,125},{5,124},{6,127},{7,126},{8... | collective-permute-start | bytes 1179656 | tf_op jit(solution)/shard_map/ppermute | solution.py:476
  (22 other events, 272.9 us)
